TPU v7x, 32 devices: a whole 2x2x4 slice. The times are simulated.
32 devices in a mesh: section: 2 (over core), fsdp: 8 (over z, x), tensor: 2 (over y).
Axes of the slice: x: 2, y: 2, z: 4, core: 2. Of those that a mesh axis runs over, the one named last changes fastest.
Arguments:
- block_input: bfloat16 [2, 1792, 1024], P(None, 'fsdp'), may hold values from -6 to 6
- image_ids: int32 [2, 1792], P(None, 'fsdp'), may hold values from -1 to 7, as said below
- qkv_weight: bfloat16 [4, 1024, 3, 1024], P('section', 'fsdp', None, 'tensor'), may hold values from -0.1875 to 0.1875
- out_weight: bfloat16 [4, 1024, 1024], P('section', 'fsdp', 'tensor'), may hold values from -0.5 to 0.5
- up_weight: bfloat16 [4, 1024, 4096], P('section', 'fsdp', 'tensor'), may hold values from -0.1875 to 0.1875
- down_weight: bfloat16 [4, 1024, 4096], P('section', 'fsdp', 'tensor'), may hold values from -0.09375 to 0.09375
- norm_gains: bfloat16 [4, 2, 1024], P('section', None, 'fsdp'), may hold values from 0.5 to 1.5
- biases: bfloat16 [4, 4, 1024], P('section', None, 'fsdp'), may hold values from -3 to 3
- inner_bias: bfloat16 [4, 2, 3072], P('section', 'tensor', 'fsdp'), may hold values from -3 to 3
- cotangent: bfloat16 [2, 1792, 1024], P(None, 'fsdp'), may hold values from -6 to 6
Outputs:
- section_ends: float32 [2, 2, 1792, 1024], P('section', None, 'fsdp')
- qkv_grad: float32 [4, 1024, 3, 1024], P('section', 'fsdp', None, 'tensor')
- out_grad: float32 [4, 1024, 1024], P('section', 'fsdp', 'tensor')
- up_grad: float32 [4, 1024, 4096], P('section', 'fsdp', 'tensor')
- down_grad: float32 [4, 1024, 4096], P('section', 'fsdp', 'tensor')
- gains_grad: float32 [4, 2, 1024], P('section', None, 'fsdp')
- biases_grad: float32 [4, 4, 1024], P('section', None, 'fsdp')
- inner_grad: float32 [4, 2, 3072], P('section', 'tensor', 'fsdp')
Inputs may be any that keep to these rules, and one draw needn't show every extreme that they name: `image_ids`: -1 marks padding; in each aligned block of 224 tokens of a micro-batch (block r) lie images r*1 to (r+1) - 1 in this order, each of exactly 197 consecutive tokens, with padding between, before or after them.
All inputs are finite; a program needn't handle non-finite values.
Results may differ from a plain program's by a relative error of at most 0.02.
Values may be sent and summed in bfloat16 or wider, within the bound.
A program may use at most 256 MiB of HBM per device.

v0:
```python
import math

import jax
import jax.numpy as jnp
from jax import lax
from jax.sharding import PartitionSpec as P

HEAD_DIM = 64


EPSILON = 1e-06


def shifted(value, axis, steps):
    count = lax.axis_size(axis)
    initial, last = (max(0, -steps), min(count, count - steps))
    return lax.ppermute(value, axis, [(source, source + steps) for source in range(initial, last)])


def layer_norm(hidden, weight_gain, weight_shift):
    average = jnp.mean(hidden, axis=-1, keepdims=True)
    centred = hidden - average
    spread = jnp.mean(centred * centred, axis=-1, keepdims=True)
    return centred * lax.rsqrt(spread + EPSILON) * weight_gain + weight_shift


def gelu_exact(upward):
    return jax.nn.gelu(upward, approximate=False)


def contract_last(left, right):
    return lax.dot_general(
        left, right, (((1,), (1,)), ((), ())), preferred_element_type=jnp.float32
    )


def contract_rows(left, right):
    return lax.dot_general(
        left, right, (((0,), (0,)), ((), ())), preferred_element_type=jnp.float32
    )


def mix_sum(partial_sum):
    return lax.psum(partial_sum.astype(jnp.bfloat16), "tensor").astype(jnp.float32)


def mix_back(partial_sum):
    return lax.psum(partial_sum.astype(jnp.bfloat16), "tensor").astype(jnp.float32)


def allowed_pairs(ids_batch):
    places = jnp.arange(ids_batch.shape[0], dtype=jnp.int32)
    same_image = (ids_batch[:, None] == ids_batch[None, :]) & (ids_batch[:, None] >= 0)
    return same_image | (places[:, None] == places[None, :])


def masked_scores(query_heads, key_rows, allowed):
    head_count = query_heads.shape[1]
    key_heads = key_rows.reshape(-1, head_count, HEAD_DIM)
    scores = jnp.einsum("qhe,khe->hqk", query_heads, key_heads, preferred_element_type=jnp.float32)
    scores = scores * (1.0 / math.sqrt(HEAD_DIM))
    return (jnp.where(allowed[None], scores, -1e30), key_heads)


def layer_slice(gathered, layer_index):
    return tuple((array[layer_index] for array in gathered))


def layer_forward(hidden, weights, ids_batch):
    qkv_w, out_w, up_w, down_w, gains, shifts, inner_part = weights
    row_count, model_width = hidden.shape
    head_width = out_w.shape[1]
    head_count = head_width // HEAD_DIM
    gains32 = gains.astype(jnp.float32)
    shifts32 = shifts.astype(jnp.float32)
    inner32 = inner_part[0].astype(jnp.float32)
    normed = layer_norm(hidden, gains32[0], shifts32[0]).astype(jnp.bfloat16)
    projected = jnp.dot(
        normed, qkv_w.reshape(model_width, 3 * head_width), preferred_element_type=jnp.float32
    ).reshape(row_count, 3, head_width)
    queries = (projected[:, 0] + inner32[:head_width]).astype(jnp.bfloat16)
    key_rows = projected[:, 1].astype(jnp.bfloat16)
    value_rows = (projected[:, 2] + inner32[head_width : 2 * head_width]).astype(jnp.bfloat16)
    allowed = allowed_pairs(ids_batch)
    scores, key_heads = masked_scores(
        queries.reshape(row_count, head_count, HEAD_DIM), key_rows, allowed
    )
    row_top = jnp.max(scores, axis=-1, keepdims=True)
    exponent = jnp.exp(scores - row_top)
    row_total = jnp.sum(exponent, axis=-1, keepdims=True)
    probs = (exponent / row_total).astype(jnp.bfloat16)
    log_total = row_top + jnp.log(row_total)
    value_heads = value_rows.reshape(-1, head_count, HEAD_DIM)
    mixed_heads = jnp.einsum("hqk,khe->qhe", probs, value_heads, preferred_element_type=jnp.float32)
    mixed_heads = mixed_heads.reshape(row_count, head_width).astype(jnp.bfloat16)
    attended = mix_sum(contract_last(mixed_heads, out_w)) + shifts32[1]
    middle = hidden + attended
    normed_mlp = layer_norm(middle, gains32[1], shifts32[2]).astype(jnp.bfloat16)
    upward = (
        jnp.dot(normed_mlp, up_w, preferred_element_type=jnp.float32) + inner32[2 * head_width :]
    )
    activated = gelu_exact(upward).astype(jnp.bfloat16)
    result = middle + (mix_sum(contract_last(activated, down_w)) + shifts32[3])
    kept = (hidden, queries, key_rows, value_rows, log_total, mixed_heads, middle, upward)
    return (result, kept)


def layer_backward(grad_out, kept, weights, ids_batch):
    qkv_w, out_w, up_w, down_w, gains, shifts, inner_part = weights
    hidden, queries, key_rows, value_rows, log_total, mixed_heads, middle, upward = kept
    row_count, model_width = hidden.shape
    head_width = out_w.shape[1]
    head_count = head_width // HEAD_DIM
    gains32 = gains.astype(jnp.float32)
    shifts32 = shifts.astype(jnp.float32)
    score_scale = 1.0 / math.sqrt(HEAD_DIM)
    grad_low = grad_out.astype(jnp.bfloat16)
    down_bias_grad = jnp.sum(grad_low.astype(jnp.float32), axis=0)
    activated, gelu_back = jax.vjp(gelu_exact, upward)
    activated = activated.astype(jnp.bfloat16)
    down_w_grad = contract_rows(grad_low, activated)
    grad_act = jnp.dot(grad_low, down_w, preferred_element_type=jnp.float32)
    grad_up = gelu_back(grad_act)[0].astype(jnp.bfloat16)
    up_bias_grad = jnp.sum(grad_up.astype(jnp.float32), axis=0)
    normed_mlp, second_back = jax.vjp(layer_norm, middle, gains32[1], shifts32[2])
    up_w_grad = contract_rows(normed_mlp.astype(jnp.bfloat16), grad_up)
    grad_norm = mix_back(contract_last(grad_up, up_w))
    middle_part, second_gain_grad, second_shift_grad = second_back(grad_norm)
    grad_middle = grad_out + middle_part
    grad_attn = grad_middle.astype(jnp.bfloat16)
    out_bias_grad = jnp.sum(grad_attn.astype(jnp.float32), axis=0)
    out_w_grad = contract_rows(grad_attn, mixed_heads)
    grad_mixed = jnp.dot(grad_attn, out_w, preferred_element_type=jnp.float32).astype(jnp.bfloat16)
    allowed = allowed_pairs(ids_batch)
    query_heads = queries.reshape(row_count, head_count, HEAD_DIM)
    scores, key_heads = masked_scores(query_heads, key_rows, allowed)
    probs = jnp.exp(scores - log_total)
    value_heads = value_rows.reshape(-1, head_count, HEAD_DIM)
    grad_mixed_heads = grad_mixed.reshape(row_count, head_count, HEAD_DIM)
    grad_probs = jnp.einsum(
        "qhe,khe->hqk", grad_mixed_heads, value_heads, preferred_element_type=jnp.float32
    )
    value_term = jnp.einsum(
        "hqk,qhe->khe",
        probs.astype(jnp.bfloat16),
        grad_mixed_heads,
        preferred_element_type=jnp.float32,
    )
    centre_term = jnp.sum(probs * grad_probs, axis=-1, keepdims=True)
    grad_scores = (probs * (grad_probs - centre_term)).astype(jnp.bfloat16)
    grad_queries = jnp.einsum(
        "hqk,khe->qhe", grad_scores, key_heads, preferred_element_type=jnp.float32
    )
    grad_queries = (grad_queries * score_scale).reshape(row_count, head_width).astype(jnp.bfloat16)
    key_term = jnp.einsum(
        "hqk,qhe->khe", grad_scores, query_heads, preferred_element_type=jnp.float32
    )
    grad_keys = (key_term * score_scale).reshape(row_count, head_width).astype(jnp.bfloat16)
    grad_values = value_term.reshape(row_count, head_width).astype(jnp.bfloat16)
    grad_qkv = jnp.stack([grad_queries, grad_keys, grad_values], axis=1).reshape(
        row_count, 3 * head_width
    )
    normed, first_back = jax.vjp(layer_norm, hidden, gains32[0], shifts32[0])
    qkv_w_grad = contract_rows(normed.astype(jnp.bfloat16), grad_qkv).reshape(
        model_width, 3, head_width
    )
    grad_normed = mix_back(contract_last(grad_qkv, qkv_w.reshape(model_width, 3 * head_width)))
    hidden_part, first_gain_grad, first_shift_grad = first_back(grad_normed)
    grad_in = grad_middle + hidden_part
    inner_grad = jnp.concatenate(
        [
            jnp.sum(grad_queries.astype(jnp.float32), axis=0),
            jnp.sum(grad_values.astype(jnp.float32), axis=0),
            up_bias_grad,
        ]
    )[None]
    layer_grads = (
        qkv_w_grad,
        out_w_grad,
        up_w_grad,
        down_w_grad,
        jnp.stack([first_gain_grad, second_gain_grad]),
        jnp.stack([first_shift_grad, out_bias_grad, second_shift_grad, down_bias_grad]),
        inner_grad,
    )
    return (grad_in, layer_grads)


def body(
    block_input,
    image_ids,
    qkv_weight,
    out_weight,
    up_weight,
    down_weight,
    norm_gains,
    biases,
    inner_bias,
    cotangent,
):
    section = lax.axis_index("section")
    micro_count = block_input.shape[0]
    layer_count = qkv_weight.shape[0]
    ticks = micro_count + 1
    gathered = (
        lax.all_gather(qkv_weight, "fsdp", axis=1, tiled=True),
        lax.all_gather(out_weight, "fsdp", axis=1, tiled=True),
        lax.all_gather(up_weight, "fsdp", axis=1, tiled=True),
        lax.all_gather(down_weight, "fsdp", axis=1, tiled=True),
        lax.all_gather(norm_gains, "fsdp", axis=2, tiled=True),
        lax.all_gather(biases, "fsdp", axis=2, tiled=True),
        lax.all_gather(inner_bias, "fsdp", axis=2, tiled=True),
    )
    stored = []
    outputs = []
    received = jnp.zeros(block_input.shape[1:], jnp.bfloat16)
    for tick_index in range(ticks):
        micro_index = jnp.clip(tick_index - section, 0, micro_count - 1)
        ids_batch = lax.dynamic_index_in_dim(image_ids, micro_index, 0, keepdims=False)
        fresh = block_input[min(tick_index, micro_count - 1)]
        hidden = jnp.where(section == 0, fresh, received).astype(jnp.float32)
        kept_layers = []
        for layer_index in range(layer_count):
            hidden, kept = layer_forward(hidden, layer_slice(gathered, layer_index), ids_batch)
            kept_layers.append(kept)
        stored.append((ids_batch, kept_layers))
        outputs.append(hidden)
        if tick_index + 1 < ticks:
            received = shifted(hidden.astype(jnp.bfloat16), "section", 1)
    gathered = (
        lax.all_gather(qkv_weight, "fsdp", axis=1, tiled=True),
        lax.all_gather(out_weight, "fsdp", axis=1, tiled=True),
        lax.all_gather(up_weight, "fsdp", axis=1, tiled=True),
        lax.all_gather(down_weight, "fsdp", axis=1, tiled=True),
        lax.all_gather(norm_gains, "fsdp", axis=2, tiled=True),
        lax.all_gather(biases, "fsdp", axis=2, tiled=True),
        lax.all_gather(inner_bias, "fsdp", axis=2, tiled=True),
    )
    accumulated = None
    grad_inputs = []
    received = jnp.zeros(block_input.shape[1:], jnp.bfloat16)
    for tick_index in range(ticks):
        micro_index = micro_count - tick_index - section
        is_valid = (micro_index >= 0) & (micro_index < micro_count)
        fresh = cotangent[max(micro_count - 1 - tick_index, 0)]
        grad_out = jnp.where(section == 1, fresh, received).astype(jnp.float32)
        grad_out = jnp.where(is_valid, grad_out, jnp.zeros_like(grad_out))
        ids_batch, kept_layers = stored[micro_count - tick_index]
        per_layer = [None] * layer_count
        for layer_index in reversed(range(layer_count)):
            grad_out, per_layer[layer_index] = layer_backward(
                grad_out, kept_layers[layer_index], layer_slice(gathered, layer_index), ids_batch
            )
        tick_grads = tuple(
            (
                jnp.stack([per_layer[which_layer][member] for which_layer in range(layer_count)])
                for member in range(7)
            )
        )
        grad_inputs.append(grad_out)
        if tick_index + 1 < ticks:
            received = shifted(grad_out.astype(jnp.bfloat16), "section", -1)
        if accumulated is None:
            accumulated = tuple(tick_grads)
        else:
            accumulated = jax.tree.map(jnp.add, tuple(accumulated), tuple(tick_grads))
    accumulated = (
        lax.psum_scatter(
            accumulated[0].astype(jnp.bfloat16), "fsdp", scatter_dimension=1, tiled=True
        ).astype(jnp.float32),
        lax.psum_scatter(
            accumulated[1].astype(jnp.bfloat16), "fsdp", scatter_dimension=1, tiled=True
        ).astype(jnp.float32),
        lax.psum_scatter(
            accumulated[2].astype(jnp.bfloat16), "fsdp", scatter_dimension=1, tiled=True
        ).astype(jnp.float32),
        lax.psum_scatter(
            accumulated[3].astype(jnp.bfloat16), "fsdp", scatter_dimension=1, tiled=True
        ).astype(jnp.float32),
        lax.psum_scatter(
            accumulated[4].astype(jnp.bfloat16), "fsdp", scatter_dimension=2, tiled=True
        ).astype(jnp.float32),
        lax.psum_scatter(
            accumulated[5].astype(jnp.bfloat16), "fsdp", scatter_dimension=2, tiled=True
        ).astype(jnp.float32),
        lax.psum_scatter(
            accumulated[6].astype(jnp.bfloat16), "fsdp", scatter_dimension=2, tiled=True
        ).astype(jnp.float32),
    )
    block_outputs = jnp.stack([outputs[micro + 1] for micro in range(micro_count)])
    input_grads = jnp.stack([grad_inputs[micro_count - micro] for micro in range(micro_count)])
    section_ends = jnp.where(section == 0, input_grads, block_outputs)[None]
    return (
        section_ends,
        accumulated[0],
        accumulated[1],
        accumulated[2],
        accumulated[3],
        accumulated[4],
        accumulated[5],
        accumulated[6],
    )


def solution(mesh):
    placed = (
        P(None, "fsdp", None),
        P(None, "fsdp"),
        P("section", "fsdp", None, "tensor"),
        P("section", "fsdp", "tensor"),
        P("section", "fsdp", "tensor"),
        P("section", "fsdp", "tensor"),
        P("section", None, "fsdp"),
        P("section", None, "fsdp"),
        P("section", "tensor", "fsdp"),
        P(None, "fsdp", None),
    )
    return jax.shard_map(
        body,
        mesh=mesh,
        in_specs=placed,
        out_specs=(
            P("section", None, "fsdp", None),
            P("section", "fsdp", None, "tensor"),
            P("section", "fsdp", "tensor"),
            P("section", "fsdp", "tensor"),
            P("section", "fsdp", "tensor"),
            P("section", None, "fsdp"),
            P("section", None, "fsdp"),
            P("section", "tensor", "fsdp"),
        ),
        check_vma=False,
    )
```

profile of v0, /device:TPU:0, one launch (start us, length us, event | category | flops | bytes accessed | tf_op | source)
XLA Modules:
  0.0 2102.5 jit_solution(6772012499365642555)
XLA Ops:
  10.5 22.3 %all_gather.27 = bf16[2,2,1024]{2,1,0:T(2,128)(2,1)S(1)} all-gather(bf16[2,2,128]{2,1,0:T(2,128)(2,1)S(1)} %copy-done.363), channel_id=1, replica_groups=mesh['section'=2,'fsdp'=8,'tensor'=2] {'fsdp'}, dimensions={2}, use_global_device_ids=true | all-gather | bytes 9216 | tf_op jit(solution)/shard_map/all_gather | solution.py:210
  49.4 26.2 %all_gather.30 = bf16[2,1,3072]{2,0,1:T(2,128)(2,1)S(1)} all-gather(bf16[2,1,384]{2,0,1:T(2,128)(2,1)S(1)} %copy-done.362), channel_id=1, replica_groups=mesh['section'=2,'fsdp'=8,'tensor'=2] {'fsdp'}, dimensions={2}, use_global_device_ids=true | all-gather | bytes 13824 | tf_op jit(solution)/shard_map/all_gather | solution.py:212
  77.1 36.6 %all-gather.5.cloned.1.call-done = bf16[2,1024,3,512]{1,3,2,0:T(8,128)(2,1)} async-done(((bf16[2,128,3,512]{1,3,2,0:T(8,128)(2,1)}), bf16[2,1024,3,512]{1,3,2,0:T(8,128)(2,1)}) %all-gather.5.cloned.1.call-update) | async-done | bytes 6291472 | tf_op jit(solution)/shard_map/all_gather | solution.py:206
  119.7 43.6 %all-gather.7.cloned.1.call-done = bf16[2,1024,512]{2,1,0:T(8,128)(2,1)} async-done(((bf16[2,128,512]{2,1,0:T(8,128)(2,1)}), bf16[2,1024,512]{2,1,0:T(8,128)(2,1)}) %all-gather.7.cloned.1.call-update) | async-done | bytes 2097168 | tf_op jit(solution)/shard_map/all_gather | solution.py:207
  167.7 24.2 %all-reduce.25.cloned.1.call-done = bf16[224,1024]{1,0:T(8,128)(2,1)} async-done(((bf16[224,1024]{1,0:T(8,128)(2,1)}), bf16[224,1024]{1,0:T(8,128)(2,1)}) %all-reduce.25.cloned.1.call-update) | async-done | bytes 458768 | tf_op jit(solution)/shard_map/psum | solution.py:44
  194.7 124.5 %all-gather.9.cloned.1.call-done = bf16[2,1024,2048]{2,1,0:T(8,128)(2,1)} async-done(((bf16[2,128,2048]{2,1,0:T(8,128)(2,1)}), bf16[2,1024,2048]{2,1,0:T(8,128)(2,1)}) %all-gather.9.cloned.1.call-update) | async-done | bytes 8388624 | tf_op jit(solution)/shard_map/all_gather | solution.py:208
  327.3 117.3 %all-gather.11.cloned.1.call-done = bf16[2,1024,2048]{2,1,0:T(8,128)(2,1)} async-done(((bf16[2,128,2048]{2,1,0:T(8,128)(2,1)}), bf16[2,1024,2048]{2,1,0:T(8,128)(2,1)}) %all-gather.11.cloned.1.call-update) | async-done | bytes 8388624 | tf_op jit(solution)/shard_map/all_gather | solution.py:209
  449.4 25.1 %all-reduce.27.cloned.1.call-done = bf16[224,1024]{1,0:T(8,128)(2,1)} async-done(((bf16[224,1024]{1,0:T(8,128)(2,1)}), bf16[224,1024]{1,0:T(8,128)(2,1)}) %all-reduce.27.cloned.1.call-update) | async-done | bytes 458768 | tf_op jit(solution)/shard_map/psum | solution.py:44
  486.1 27.3 %all-reduce.29.cloned.1.call-done = bf16[224,1024]{1,0:T(8,128)(2,1)} async-done(((bf16[224,1024]{1,0:T(8,128)(2,1)}), bf16[224,1024]{1,0:T(8,128)(2,1)}) %all-reduce.29.cloned.1.call-update) | async-done | bytes 458768 | tf_op jit(solution)/shard_map/psum | solution.py:44
  525.9 27.3 %all-reduce.31.cloned.1.call-done = bf16[224,1024]{1,0:T(8,128)(2,1)} async-done(((bf16[224,1024]{1,0:T(8,128)(2,1)}), bf16[224,1024]{1,0:T(8,128)(2,1)}) %all-reduce.31.cloned.1.call-update) | async-done | bytes 458768 | tf_op jit(solution)/shard_map/psum | solution.py:44
  568.3 26.9 %all-reduce.33.cloned.1.call-done = bf16[224,1024]{1,0:T(8,128)(2,1)} async-done(((bf16[224,1024]{1,0:T(8,128)(2,1)}), bf16[224,1024]{1,0:T(8,128)(2,1)}) %all-reduce.33.cloned.1.call-update) | async-done | bytes 458768 | tf_op jit(solution)/shard_map/psum | solution.py:44
  608.6 27.3 %all-reduce.35.cloned.1.call-done = bf16[224,1024]{1,0:T(8,128)(2,1)} async-done(((bf16[224,1024]{1,0:T(8,128)(2,1)}), bf16[224,1024]{1,0:T(8,128)(2,1)}) %all-reduce.35.cloned.1.call-update) | async-done | bytes 458768 | tf_op jit(solution)/shard_map/psum | solution.py:44
  650.3 27.1 %all-reduce.37.cloned.1.call-done = bf16[224,1024]{1,0:T(8,128)(2,1)} async-done(((bf16[224,1024]{1,0:T(8,128)(2,1)}), bf16[224,1024]{1,0:T(8,128)(2,1)}) %all-reduce.37.cloned.1.call-update) | async-done | bytes 458768 | tf_op jit(solution)/shard_map/psum | solution.py:44
  690.7 27.3 %all-reduce.39.cloned.1.call-done = bf16[224,1024]{1,0:T(8,128)(2,1)} async-done(((bf16[224,1024]{1,0:T(8,128)(2,1)}), bf16[224,1024]{1,0:T(8,128)(2,1)}) %all-reduce.39.cloned.1.call-update) | async-done | bytes 458768 | tf_op jit(solution)/shard_map/psum | solution.py:44
  734.3 27.1 %all-reduce.41.cloned.1.call-done = bf16[224,1024]{1,0:T(8,128)(2,1)} async-done(((bf16[224,1024]{1,0:T(8,128)(2,1)}), bf16[224,1024]{1,0:T(8,128)(2,1)}) %all-reduce.41.cloned.1.call-update) | async-done | bytes 458768 | tf_op jit(solution)/shard_map/psum | solution.py:44
  778.3 27.3 %all-reduce.43.cloned.1.call-done = bf16[224,1024]{1,0:T(8,128)(2,1)} async-done(((bf16[224,1024]{1,0:T(8,128)(2,1)}), bf16[224,1024]{1,0:T(8,128)(2,1)}) %all-reduce.43.cloned.1.call-update) | async-done | bytes 458768 | tf_op jit(solution)/shard_map/psum | solution.py:44
  823.1 26.9 %all-reduce.45.cloned.1.call-done = bf16[224,1024]{1,0:T(8,128)(2,1)} async-done(((bf16[224,1024]{1,0:T(8,128)(2,1)}), bf16[224,1024]{1,0:T(8,128)(2,1)}) %all-reduce.45.cloned.1.call-update) | async-done | bytes 458768 | tf_op jit(solution)/shard_map/psum | solution.py:44
  876.6 20.2 all-reduce.47.cloned.1.call-done
  913.6 27.1 %all-reduce.49.cloned.1.call-done = bf16[224,1024]{1,0:T(8,128)(2,1)} async-done(((bf16[224,1024]{1,0:T(8,128)(2,1)}), bf16[224,1024]{1,0:T(8,128)(2,1)}) %all-reduce.49.cloned.1.call-update) | async-done | bytes 458768 | tf_op jit(solution)/shard_map/psum | solution.py:48
  956.6 27.3 %all-reduce.51.cloned.1.call-done = bf16[224,1024]{1,0:T(8,128)(2,1)} async-done(((bf16[224,1024]{1,0:T(8,128)(2,1)}), bf16[224,1024]{1,0:T(8,128)(2,1)}) %all-reduce.51.cloned.1.call-update) | async-done | bytes 458768 | tf_op jit(solution)/shard_map/psum | solution.py:48
  1000.7 27.3 %all-reduce.53.cloned.1.call-done = bf16[224,1024]{1,0:T(8,128)(2,1)} async-done(((bf16[224,1024]{1,0:T(8,128)(2,1)}), bf16[224,1024]{1,0:T(8,128)(2,1)}) %all-reduce.53.cloned.1.call-update) | async-done | bytes 458768 | tf_op jit(solution)/shard_map/psum | solution.py:48
  1050.1 27.2 %all-reduce.55.cloned.1.call-done = bf16[224,1024]{1,0:T(8,128)(2,1)} async-done(((bf16[224,1024]{1,0:T(8,128)(2,1)}), bf16[224,1024]{1,0:T(8,128)(2,1)}) %all-reduce.55.cloned.1.call-update) | async-done | bytes 458768 | tf_op jit(solution)/shard_map/psum | solution.py:48
  1093.5 27.3 %all-reduce.57.cloned.1.call-done = bf16[224,1024]{1,0:T(8,128)(2,1)} async-done(((bf16[224,1024]{1,0:T(8,128)(2,1)}), bf16[224,1024]{1,0:T(8,128)(2,1)}) %all-reduce.57.cloned.1.call-update) | async-done | bytes 458768 | tf_op jit(solution)/shard_map/psum | solution.py:48
  1136.2 26.8 %all-reduce.59.cloned.1.call-done = bf16[224,1024]{1,0:T(8,128)(2,1)} async-done(((bf16[224,1024]{1,0:T(8,128)(2,1)}), bf16[224,1024]{1,0:T(8,128)(2,1)}) %all-reduce.59.cloned.1.call-update) | async-done | bytes 458768 | tf_op jit(solution)/shard_map/psum | solution.py:48
  1238.6 23.1 %all-reduce.63.cloned.1.call-done = bf16[224,1024]{1,0:T(8,128)(2,1)} async-done(((bf16[224,1024]{1,0:T(8,128)(2,1)}), bf16[224,1024]{1,0:T(8,128)(2,1)}) %all-reduce.63.cloned.1.call-update) | async-done | bytes 458768 | tf_op jit(solution)/shard_map/psum | solution.py:48
  1284.8 20.9 all-reduce.65.cloned.1.call-done
  1380.2 23.3 %all-reduce.69.cloned.1.call-done = (bf16[224,1024]{1,0:T(8,128)(2,1)}, bf16[224,1024]{1,0:T(8,128)(2,1)}) async-done(((bf16[224,1024]{1,0:T(8,128)(2,1)}, bf16[224,1024]{1,0:T(8,128)(2,1)}), (bf16[224,1024]{1,0:T(8,128)(2,1)}, bf16[224,1024]{1,0:T(8,128)(2,1)})) %all-reduce.69.cloned.1.call-update) | async-done | bytes 917520 | tf_op jit(solution)/shard_map/psum | solution.py:48
  1538.0 59.4 %reduce-scatter.24.cloned.1.call-done = bf16[128,8]{1,0:T(8,128)(2,1)} async-done(((bf16[1024,8]{1,0:T(8,128)(2,1)}), bf16[128,8]{1,0:T(8,128)(2,1)}) %reduce-scatter.24.cloned.1.call-update) | async-done | bytes 2064
  1599.0 68.9 %reduce-scatter.16.cloned.1.call-done = bf16[2,128,512]{2,1,0:T(8,128)(2,1)} async-done(((bf16[2,1024,512]{2,1,0:T(8,128)(2,1)}), bf16[2,128,512]{2,1,0:T(8,128)(2,1)}) %reduce-scatter.16.cloned.1.call-update) | async-done | bytes 262160 | tf_op jit(solution)/shard_map/reduce_scatter | solution.py:271
  1669.7 119.2 %reduce-scatter.14.cloned.1.call-done = bf16[2,128,3,512]{3,1,2,0:T(8,128)(2,1)} async-done(((bf16[2,1024,3,512]{3,1,2,0:T(8,128)(2,1)}), bf16[2,128,3,512]{3,1,2,0:T(8,128)(2,1)}) %reduce-scatter.14.cloned.1.call-update) | async-done | bytes 786448 | tf_op jit(solution)/shard_map/reduce_scatter | solution.py:268
  1791.3 149.2 %reduce-scatter.20.cloned.1.call-done = bf16[2,128,2048]{2,1,0:T(8,128)(2,1)} async-done(((bf16[2,1024,2048]{2,1,0:T(8,128)(2,1)}), bf16[2,128,2048]{2,1,0:T(8,128)(2,1)}) %reduce-scatter.20.cloned.1.call-update) | async-done | bytes 1048592 | tf_op jit(solution)/shard_map/reduce_scatter | solution.py:277
  1943.3 149.3 %reduce-scatter.18.cloned.1.call-done = bf16[2,128,2048]{2,1,0:T(8,128)(2,1)} async-done(((bf16[2,1024,2048]{2,1,0:T(8,128)(2,1)}), bf16[2,128,2048]{2,1,0:T(8,128)(2,1)}) %reduce-scatter.18.cloned.1.call-update) | async-done | bytes 1048592 | tf_op jit(solution)/shard_map/reduce_scatter | solution.py:274
  (1224 shorter events, 623.2 us)
Async XLA Ops:
  7.2 106.5 %all-gather.5.cloned.1.call-start = ((), (), s32[]{:S(2)}) async-start(), calls=%async_computation.7 | async-start | bytes 7077888 | tf_op jit(solution)/shard_map/all_gather | solution.py:206
  9.7 153.7 %all-gather.7.cloned.1.call-start = ((), (), s32[]{:S(2)}) async-start(), calls=%async_computation.8 | async-start | bytes 2359296 | tf_op jit(solution)/shard_map/all_gather | solution.py:207
  10.4 181.5 %all-reduce.25.cloned.1.call-start = ((), (), s32[]{:S(2)}) async-start(), calls=%async_computation.9 | async-start | bytes 917504 | tf_op jit(solution)/shard_map/psum | solution.py:44
  165.9 153.3 %all-gather.9.cloned.1.call-start = ((), (), s32[]{:S(2)}) async-start(), calls=%async_computation.10 | async-start | bytes 9437184 | tf_op jit(solution)/shard_map/all_gather | solution.py:208
  166.5 278.1 %all-gather.11.cloned.1.call-start = ((), (), s32[]{:S(2)}) async-start(), calls=%async_computation.11 | async-start | bytes 9437184 | tf_op jit(solution)/shard_map/all_gather | solution.py:209
  167.1 307.4 %all-reduce.27.cloned.1.call-start = ((), (), s32[]{:S(2)}) async-start(), calls=%async_computation.12 | async-start | bytes 917504 | tf_op jit(solution)/shard_map/psum | solution.py:44
  525.8 69.4 %all-reduce.33.cloned.1.call-start = ((), (), s32[]{:S(2)}) async-start(), calls=%async_computation.15 | async-start | bytes 917504 | tf_op jit(solution)/shard_map/psum | solution.py:44
  567.8 68.1 %all-reduce.35.cloned.1.call-start = ((), (), s32[]{:S(2)}) async-start(), calls=%async_computation.16 | async-start | bytes 917504 | tf_op jit(solution)/shard_map/psum | solution.py:44
  608.6 68.8 %all-reduce.37.cloned.1.call-start = ((), (), s32[]{:S(2)}) async-start(), calls=%async_computation.17 | async-start | bytes 917504 | tf_op jit(solution)/shard_map/psum | solution.py:44
  650.1 67.8 %all-reduce.39.cloned.1.call-start = ((), (), s32[]{:S(2)}) async-start(), calls=%async_computation.18 | async-start | bytes 917504 | tf_op jit(solution)/shard_map/psum | solution.py:44
  690.6 70.8 %all-reduce.41.cloned.1.call-start = ((), (), s32[]{:S(2)}) async-start(), calls=%async_computation.19 | async-start | bytes 917504 | tf_op jit(solution)/shard_map/psum | solution.py:44
  734.1 71.4 %all-reduce.43.cloned.1.call-start = ((), (), s32[]{:S(2)}) async-start(), calls=%async_computation.20 | async-start | bytes 917504 | tf_op jit(solution)/shard_map/psum | solution.py:44
  778.2 71.7 %all-reduce.45.cloned.1.call-start = ((), (), s32[]{:S(2)}) async-start(), calls=%async_computation.21 | async-start | bytes 917504 | tf_op jit(solution)/shard_map/psum | solution.py:44
  822.6 74.2 %all-reduce.47.cloned.1.call-start = ((), (), s32[]{:S(2)}) async-start(), calls=%async_computation.22 | async-start | bytes 917504 | tf_op jit(solution)/shard_map/psum | solution.py:48
  869.5 71.1 %all-reduce.49.cloned.1.call-start = ((), (), s32[]{:S(2)}) async-start(), calls=%async_computation.23 | async-start | bytes 917504 | tf_op jit(solution)/shard_map/psum | solution.py:48
  913.4 70.5 %all-reduce.51.cloned.1.call-start = ((), (), s32[]{:S(2)}) async-start(), calls=%async_computation.24 | async-start | bytes 917504 | tf_op jit(solution)/shard_map/psum | solution.py:48
  956.5 71.5 %all-reduce.53.cloned.1.call-start = ((), (), s32[]{:S(2)}) async-start(), calls=%async_computation.25 | async-start | bytes 917504 | tf_op jit(solution)/shard_map/psum | solution.py:48
  1000.7 76.6 %all-reduce.55.cloned.1.call-start = ((), (), s32[]{:S(2)}) async-start(), calls=%async_computation.26 | async-start | bytes 917504 | tf_op jit(solution)/shard_map/psum | solution.py:48
  1050.0 70.7 %all-reduce.57.cloned.1.call-start = ((), (), s32[]{:S(2)}) async-start(), calls=%async_computation.27 | async-start | bytes 917504 | tf_op jit(solution)/shard_map/psum | solution.py:48
  1093.4 69.5 %all-reduce.59.cloned.1.call-start = ((), (), s32[]{:S(2)}) async-start(), calls=%async_computation.28 | async-start | bytes 917504 | tf_op jit(solution)/shard_map/psum | solution.py:48
  1135.6 72.8 %all-reduce.61.cloned.1.call-start = ((), (), s32[]{:S(2)}) async-start(), calls=%async_computation.29 | async-start | bytes 917504 | tf_op jit(solution)/shard_map/psum | solution.py:48
  1181.1 80.7 %all-reduce.63.cloned.1.call-start = ((), (), s32[]{:S(2)}) async-start(), calls=%async_computation.30 | async-start | bytes 917504 | tf_op jit(solution)/shard_map/psum | solution.py:48
  1233.6 72.1 %all-reduce.65.cloned.1.call-start = ((), (), s32[]{:S(2)}) async-start(), calls=%async_computation.31 | async-start | bytes 917504 | tf_op jit(solution)/shard_map/psum | solution.py:48
  1278.3 69.9 %all-reduce.67.cloned.1.call-start = ((), (), s32[]{:S(2)}) async-start(), calls=%async_computation.32 | async-start | bytes 917504 | tf_op jit(solution)/shard_map/psum | solution.py:48
  1320.9 82.6 %all-reduce.69.cloned.1.call-start = ((), (), s32[]{:S(2)}) async-start(), calls=%async_computation.40 | async-start | bytes 1835008 | tf_op jit(solution)/shard_map/psum | solution.py:48
  1366.0 164.1 %reduce-scatter.26.cloned.1.call-start = ((), (), s32[]{:S(2)}) async-start(), calls=%async_computation.39 | async-start | bytes 884736
  1380.2 156.3 %reduce-scatter.22.cloned.1.call-start = ((), (), s32[]{:S(2)}) async-start(), calls=%async_computation.37 | async-start | bytes 294912
  1411.7 185.7 %reduce-scatter.24.cloned.1.call-start = ((), (), s32[]{:S(2)}) async-start(), calls=%async_computation.38 | async-start | bytes 294912
  1416.5 251.3 %reduce-scatter.16.cloned.1.call-start = ((), (), s32[]{:S(2)}) async-start(), calls=%async_computation.34 | async-start | bytes 2359296 | tf_op jit(solution)/shard_map/reduce_scatter | solution.py:271
  1423.2 365.6 %reduce-scatter.14.cloned.1.call-start = ((), (), s32[]{:S(2)}) async-start(), calls=%async_computation.33 | async-start | bytes 7077888 | tf_op jit(solution)/shard_map/reduce_scatter | solution.py:268
  1452.2 488.3 %reduce-scatter.20.cloned.1.call-start = ((), (), s32[]{:S(2)}) async-start(), calls=%async_computation.36 | async-start | bytes 9437184 | tf_op jit(solution)/shard_map/reduce_scatter | solution.py:277
  1490.3 602.3 %reduce-scatter.18.cloned.1.call-start = ((), (), s32[]{:S(2)}) async-start(), calls=%async_computation.35 | async-start | bytes 9437184 | tf_op jit(solution)/shard_map/reduce_scatter | solution.py:274
  (396 other events, 7246.0 us)
Sparse Core Ops, SparseCore 0:
  10.7 102.9 all-gather.4
  115.9 47.4 all-gather.6
  194.2 124.8 all-gather.8
  321.4 123.0 all-gather.10
  486.2 27.1 all-reduce.28
  525.9 27.1 all-reduce.30
  567.9 27.1 all-reduce.32
  608.7 27.1 all-reduce.34
  650.2 27.1 all-reduce.36
  690.8 27.1 all-reduce.38
  734.2 27.1 all-reduce.40
  778.3 27.1 all-reduce.42
  822.7 27.1 all-reduce.44
  869.7 27.1 all-reduce.46
  913.5 27.1 all-reduce.48
  956.6 27.1 all-reduce.50
  1000.8 27.1 all-reduce.52
  1050.1 27.1 all-reduce.54
  1093.6 27.1 all-reduce.56
  1135.7 27.1 all-reduce.58
  1181.2 27.1 all-reduce.60
  1233.7 27.9 all-reduce.62
  1278.5 27.1 all-reduce.64
  1321.0 27.1 all-reduce.66
  1366.1 37.3 all-reduce.68
  1407.7 62.4 reduce-scatter.25
  1473.6 60.2 reduce-scatter.21
  1537.0 60.3 reduce-scatter.23
  1600.9 66.8 reduce-scatter.15
  1671.5 117.3 reduce-scatter.13
  1792.3 148.1 reduce-scatter.19
  1944.6 148.0 reduce-scatter.17
  (2 shorter events, 50.9 us)
where the time goes:
time: 2110 us; the launch traced here: 2100 us
  waiting for transfers between devices  1450 us (69%)
  matrix products  277 us (13%)
  other arithmetic  181 us (9%)
  local copies, waits for them, and re-layouts  96 us (5%)
  blocking collectives  65.1 us (3%)
    psum x11, waiting for transfers between devices, mix_sum(): lax.psum(partial_sum.astype(jnp.bfloat16), 'tensor').astype(jnp.float32)  294 us
    psum x12, waiting for transfers between devices, mix_back(): lax.psum(partial_sum.astype(jnp.bfloat16), 'tensor').astype(jnp.float32)  286 us
    reduce_scatter x1, waiting for transfers between devices, body(): lax.psum_scatter(accumulated[2].astype(jnp.bfloat16), 'fsdp', scatter_dim...  149 us
    reduce_scatter x1, waiting for transfers between devices, body(): lax.psum_scatter(accumulated[3].astype(jnp.bfloat16), 'fsdp', scatter_dim...  149 us
    all_gather x1, waiting for transfers between devices, body(): lax.all_gather(up_weight, 'fsdp', axis=1, tiled=True)  124 us
    reduce_scatter x1, waiting for transfers between devices, body(): lax.psum_scatter(accumulated[0].astype(jnp.bfloat16), 'fsdp', scatter_dim...  119 us
    all_gather x1, waiting for transfers between devices, body(): lax.all_gather(down_weight, 'fsdp', axis=1, tiled=True)  117 us
    dot_general x24, matrix products, contract_rows(): lax.dot_general(left, right, (((0,), (0,)), ((), ())), preferred_element_...  77.6 us
  transfers between devices with their start and end apart: 38, of which 35 were waited for; matrix products, arithmetic and copies ran while one was open for 10% of the time, Pallas kernels for 0%

commit v1 on v0

--- a/solution.py
+++ b/solution.py
@@ -1,11 +1,409 @@
+import functools
 import math
 
 import jax
 import jax.numpy as jnp
 from jax import lax
+from jax.experimental import pallas as pl
+from jax.experimental.pallas import tpu as pltpu
 from jax.sharding import PartitionSpec as P
 
 HEAD_DIM = 64
+MESH = pl.DeviceIdType.MESH
+X_FIRST_COLS = 1024
+
+
+def gather_kernel(line, w_ref, g_ref, local_sem, go_sem, sax, rax, sau, rau, sad, rad, sbx, rbx, sbu, rbu, sbd, rbd):
+    layers, shard_rows, cols = w_ref.shape
+    cols_a = cols - X_FIRST_COLS
+    section = lax.axis_index("section")
+    place = lax.axis_index("fsdp")
+    z = place // 2
+    x = lax.rem(place, 2)
+    has_up = z < line - 1
+    has_down = z > 0
+    to_x = {"fsdp": z * 2 + 1 - x}
+    to_up = {"fsdp": jnp.minimum(z + 1, line - 1) * 2 + x}
+    to_down = {"fsdp": jnp.maximum(z - 1, 0) * 2 + x}
+
+    barrier = pltpu.get_barrier_semaphore()
+    pl.semaphore_signal(barrier, inc=1, device_id=to_x, device_id_type=MESH)
+    pl.semaphore_signal(barrier, inc=1, device_id={"section": 1 - section}, device_id_type=MESH)
+
+    @pl.when(has_up)
+    def _():
+        pl.semaphore_signal(barrier, inc=1, device_id=to_up, device_id_type=MESH)
+
+    @pl.when(has_down)
+    def _():
+        pl.semaphore_signal(barrier, inc=1, device_id=to_down, device_id_type=MESH)
+
+    pl.semaphore_wait(barrier, 2 + jnp.where(has_up, 1, 0) + jnp.where(has_down, 1, 0))
+
+    span_a = pl.ds(0, cols_a)
+    span_b = pl.ds(cols_a, X_FIRST_COLS)
+
+    def spot(layer, row_z, row_x, span):
+        start = pl.multiple_of((row_z * 2 + row_x) * shard_rows, shard_rows)
+        return g_ref.at[layer, pl.ds(start, shard_rows), span]
+
+    def own(layer, span):
+        return w_ref.at[layer, :, span]
+
+    def send(source, layer, row_z, row_x, span, send_sem, recv_sem, target):
+        return pltpu.make_async_remote_copy(
+            src_ref=source,
+            dst_ref=spot(layer, row_z, row_x, span),
+            send_sem=send_sem,
+            recv_sem=recv_sem,
+            device_id=target,
+            device_id_type=MESH,
+        )
+
+    def relay(layer, row_z, row_x, span, send_sem, recv_sem, target):
+        return send(spot(layer, row_z, row_x, span), layer, row_z, row_x, span, send_sem, recv_sem, target)
+
+    @pl.when(section == 1)
+    def _():
+        pl.semaphore_wait(go_sem, 1)
+
+    finish = []
+
+    def launch(copy, condition=None):
+        if condition is None:
+            copy.start()
+            finish.append((copy, None))
+        else:
+            pl.when(condition)(copy.start)
+            finish.append((copy, condition))
+
+    locals_ = []
+    for layer in range(layers):
+        copy = pltpu.make_async_copy(
+            w_ref.at[layer], spot(layer, z, x, pl.ds(0, cols)), local_sem.at[layer]
+        )
+        copy.start()
+        locals_.append(copy)
+        a, b = own(layer, span_a), own(layer, span_b)
+        launch(send(b, layer, z, x, span_b, sbx.at[layer], rbx.at[layer], to_x))
+        launch(send(a, layer, z, x, span_a, sau.at[layer, 0], rau.at[layer, 0], to_up), has_up)
+        launch(send(a, layer, z, x, span_a, sad.at[layer, 0], rad.at[layer, 0], to_down), has_down)
+        launch(send(a, layer, z, x, span_a, sax.at[layer, 0], rax.at[layer, 0], to_x))
+        launch(send(b, layer, z, x, span_b, sbu.at[layer, 0, 0], rbu.at[layer, 0, 0], to_up), has_up)
+        launch(send(b, layer, z, x, span_b, sbd.at[layer, 0, 0], rbd.at[layer, 0, 0], to_down), has_down)
+
+    def arrive(layer, row_z, row_x, span, sem):
+        relay(layer, row_z, row_x, span, sem, sem, to_x).wait_recv()
+
+    for layer in range(layers):
+        arrive(layer, z, 1 - x, span_b, rbx.at[layer])
+        launch(relay(layer, z, 1 - x, span_b, sbu.at[layer, 0, 1], rbu.at[layer, 0, 1], to_up), has_up)
+        launch(relay(layer, z, 1 - x, span_b, sbd.at[layer, 0, 1], rbd.at[layer, 0, 1], to_down), has_down)
+    for hop in range(line - 1):
+        for layer in range(layers):
+            from_below = z - 1 - hop
+            from_above = z + 1 + hop
+            below = from_below >= 0
+            above = from_above < line
+            row_below = jnp.maximum(from_below, 0)
+            row_above = jnp.minimum(from_above, line - 1)
+
+            def pass_on(live, row, rau, sau, rbu, sbu, sem_place, onward, target, hop=hop, layer=layer):
+                pl.when(live)(lambda: arrive(layer, row, x, span_a, rau.at[layer, hop]))
+                launch(relay(layer, row, x, span_a, sax.at[layer, sem_place], rax.at[layer, sem_place], to_x), live)
+                if hop + 1 < line - 1:
+                    launch(
+                        relay(layer, row, x, span_a, sau.at[layer, hop + 1], rau.at[layer, hop + 1], target),
+                        live & onward,
+                    )
+                for side, row_x in ((0, x), (1, 1 - x)):
+                    pl.when(live)(
+                        functools.partial(arrive, layer, row, row_x, span_b, rbu.at[layer, hop, side])
+                    )
+                    if hop + 1 < line - 1:
+                        launch(
+                            relay(
+                                layer, row, row_x, span_b,
+                                sbu.at[layer, hop + 1, side], rbu.at[layer, hop + 1, side], target,
+                            ),
+                            live & onward,
+                        )
+
+            pass_on(below, row_below, rau, sau, rbu, sbu, 1 + hop, has_up, to_up)
+            pass_on(above, row_above, rad, sad, rbd, sbd, line + hop, has_down, to_down)
+    for layer in range(layers):
+        arrive(layer, z, 1 - x, span_a, rax.at[layer, 0])
+        for hop in range(line - 1):
+            from_below = z - 1 - hop
+            from_above = z + 1 + hop
+            pl.when(from_below >= 0)(
+                functools.partial(
+                    arrive, layer, jnp.maximum(from_below, 0), 1 - x, span_a, rax.at[layer, 1 + hop]
+                )
+            )
+            pl.when(from_above < line)(
+                functools.partial(
+                    arrive, layer, jnp.minimum(from_above, line - 1), 1 - x, span_a, rax.at[layer, line + hop]
+                )
+            )
+
+    @pl.when(section == 0)
+    def _():
+        pl.semaphore_signal(go_sem, inc=1, device_id={"section": 1}, device_id_type=MESH)
+
+    for copy in locals_:
+        copy.wait()
+    for copy, condition in finish:
+        if condition is None:
+            copy.wait_send()
+        else:
+            pl.when(condition)(copy.wait_send)
+
+
+def gather_weights(shard):
+    layers, shard_rows, cols = shard.shape
+    count = lax.axis_size("fsdp")
+    line = count // 2
+    dma = pltpu.SemaphoreType.DMA
+    return pl.pallas_call(
+        functools.partial(gather_kernel, line),
+        out_shape=jax.ShapeDtypeStruct((layers, shard_rows * count, cols), shard.dtype),
+        in_specs=[pl.BlockSpec(memory_space=pl.ANY)],
+        out_specs=pl.BlockSpec(memory_space=pl.ANY),
+        scratch_shapes=[
+            dma((layers,)),
+            pltpu.SemaphoreType.REGULAR,
+            dma((layers, 2 * line - 1)),
+            dma((layers, 2 * line - 1)),
+            dma((layers, line - 1)),
+            dma((layers, line - 1)),
+            dma((layers, line - 1)),
+            dma((layers, line - 1)),
+            dma((layers,)),
+            dma((layers,)),
+            dma((layers, line - 1, 2)),
+            dma((layers, line - 1, 2)),
+            dma((layers, line - 1, 2)),
+            dma((layers, line - 1, 2)),
+        ],
+        compiler_params=pltpu.CompilerParams(collective_id=0, has_side_effects=True),
+        name="gather_weights",
+    )(shard)
+
+
+def add_into(target, source):
+    rows = target.shape[0]
+
+    @pl.loop(0, rows, step=16)
+    def _(start):
+        span = pl.ds(pl.multiple_of(start, 16), 16)
+        target[span] = target[span] + source[span]
+
+
+def scatter_kernel(
+    line, d_ref, out_ref,
+    sa, xa, ua, da, sb, ub, db, xb,
+    load_a, load_b, sxa, rxa, sua, rua, sda, rda, sub, rub, sdb, rdb, sxb, rxb,
+):
+    layers, all_rows, cols = d_ref.shape
+    shard_rows = all_rows // (2 * line)
+    cols_a = cols - X_FIRST_COLS
+    place = lax.axis_index("fsdp")
+    z = place // 2
+    x = lax.rem(place, 2)
+    has_up = z < line - 1
+    has_down = z > 0
+    to_x = {"fsdp": z * 2 + 1 - x}
+    to_up = {"fsdp": jnp.minimum(z + 1, line - 1) * 2 + x}
+    to_down = {"fsdp": jnp.maximum(z - 1, 0) * 2 + x}
+
+    barrier = pltpu.get_barrier_semaphore()
+    pl.semaphore_signal(barrier, inc=1, device_id=to_x, device_id_type=MESH)
+
+    @pl.when(has_up)
+    def _():
+        pl.semaphore_signal(barrier, inc=1, device_id=to_up, device_id_type=MESH)
+
+    @pl.when(has_down)
+    def _():
+        pl.semaphore_signal(barrier, inc=1, device_id=to_down, device_id_type=MESH)
+
+    pl.semaphore_wait(barrier, 1 + jnp.where(has_up, 1, 0) + jnp.where(has_down, 1, 0))
+
+    span_a = pl.ds(0, cols_a)
+    span_b = pl.ds(cols_a, X_FIRST_COLS)
+
+    def part(layer, row_z, row_x, span):
+        start = pl.multiple_of((row_z * 2 + row_x) * shard_rows, shard_rows)
+        return d_ref.at[layer, pl.ds(start, shard_rows), span]
+
+    def remote(source, target_ref, send_sem, recv_sem, target):
+        return pltpu.make_async_remote_copy(
+            src_ref=source, dst_ref=target_ref, send_sem=send_sem, recv_sem=recv_sem,
+            device_id=target, device_id_type=MESH,
+        )
+
+    finish = []
+
+    def launch(copy, condition=None):
+        if condition is None:
+            copy.start()
+            finish.append((copy, None))
+        else:
+            pl.when(condition)(copy.start)
+            finish.append((copy, condition))
+
+    def arrived(buffer, sem):
+        remote(buffer, buffer, sem, sem, to_x).wait_recv()
+
+    loads = {}
+    order = []
+    for reach in range(line - 1, 0, -1):
+        order.append((reach, 1, z + reach < line, jnp.minimum(z + reach, line - 1)))
+        order.append((reach, 0, z - reach >= 0, jnp.maximum(z - reach, 0)))
+    order.append((0, 0, None, z))
+    for number, (reach, upward, live, row) in enumerate(order):
+        for layer in range(layers):
+            copy = pltpu.make_async_copy(part(layer, row, x, span_a), sa.at[layer, row], load_a.at[layer, number])
+            both = pltpu.make_async_copy(
+                d_ref.at[layer, pl.ds(pl.multiple_of(row * 2 * shard_rows, 2 * shard_rows), 2 * shard_rows), span_b],
+                sb.at[layer, row],
+                load_b.at[layer, number],
+            )
+            for local in (copy, both):
+                if live is None:
+                    local.start()
+                else:
+                    pl.when(live)(local.start)
+            loads[number, layer] = (copy, both)
+            launch(
+                remote(part(layer, row, 1 - x, span_a), xa.at[layer, row], sxa.at[layer, number], rxa.at[layer, number], to_x),
+                live,
+            )
+    for number, (reach, upward, live, row) in enumerate(order):
+        for layer in range(layers):
+            copy, both = loads[number, layer]
+            if reach:
+                wide, narrow = (ub, ua) if upward else (db, da)
+                s_a, r_a, s_b, r_b = (sua, rua, sub, rub) if upward else (sda, rda, sdb, rdb)
+                target = to_up if upward else to_down
+                fed = (z > 0) if upward else (z < line - 1)
+                slot = reach - 1
+
+                def step(copy=copy, both=both, layer=layer, row=row, number=number, wide=wide, narrow=narrow,
+                         r_a=r_a, r_b=r_b, fed=fed, slot=slot, reach=reach):
+                    both.wait()
+                    if reach < line - 1:
+
+                        @pl.when(fed)
+                        def _():
+                            arrived(wide.at[layer, slot + 1], r_b.at[layer, slot + 1])
+                            add_into(sb.at[layer, row], wide.at[layer, slot + 1])
+
+                def step_a(copy=copy, layer=layer, row=row, number=number, narrow=narrow, r_a=r_a, fed=fed, slot=slot, reach=reach):
+                    copy.wait()
+                    arrived(xa.at[layer, row], rxa.at[layer, number])
+                    add_into(sa.at[layer, row], xa.at[layer, row])
+                    if reach < line - 1:
+
+                        @pl.when(fed)
+                        def _():
+                            arrived(narrow.at[layer, slot + 1], r_a.at[layer, slot + 1])
+                            add_into(sa.at[layer, row], narrow.at[layer, slot + 1])
+
+                pl.when(live)(step)
+                launch(remote(sb.at[layer, row], wide.at[layer, slot], s_b.at[layer, slot], r_b.at[layer, slot], target), live)
+                pl.when(live)(step_a)
+                launch(remote(sa.at[layer, row], narrow.at[layer, slot], s_a.at[layer, slot], r_a.at[layer, slot], target), live)
+            else:
+                both.wait()
+
+                @pl.when(has_down)
+                def _(layer=layer):
+                    arrived(ub.at[layer, 0], rub.at[layer, 0])
+                    add_into(sb.at[layer, z], ub.at[layer, 0])
+
+                @pl.when(has_up)
+                def _(layer=layer):
+                    arrived(db.at[layer, 0], rdb.at[layer, 0])
+                    add_into(sb.at[layer, z], db.at[layer, 0])
+
+                theirs = pl.ds(pl.multiple_of((1 - x) * shard_rows, shard_rows), shard_rows)
+                launch(remote(sb.at[layer, z, theirs], xb.at[layer], sxb.at[layer], rxb.at[layer], to_x))
+                copy.wait()
+                arrived(xa.at[layer, z], rxa.at[layer, number])
+                add_into(sa.at[layer, z], xa.at[layer, z])
+
+                @pl.when(has_down)
+                def _(layer=layer):
+                    arrived(ua.at[layer, 0], rua.at[layer, 0])
+                    add_into(sa.at[layer, z], ua.at[layer, 0])
+
+                @pl.when(has_up)
+                def _(layer=layer):
+                    arrived(da.at[layer, 0], rda.at[layer, 0])
+                    add_into(sa.at[layer, z], da.at[layer, 0])
+
+    for layer in range(layers):
+        arrived(xb.at[layer], rxb.at[layer])
+
+        @pl.loop(0, shard_rows, step=16)
+        def _(start, layer=layer):
+            span = pl.ds(pl.multiple_of(start, 16), 16)
+            mine = pl.ds(pl.multiple_of(x * shard_rows + start, 16), 16)
+            out_ref[layer, span, span_a] = sa[layer, z, span].astype(jnp.float32)
+            out_ref[layer, span, span_b] = sb[layer, z, mine].astype(jnp.float32) + xb[layer, span].astype(jnp.float32)
+
+    for copy, condition in finish:
+        if condition is None:
+            copy.wait_send()
+        else:
+            pl.when(condition)(copy.wait_send)
+
+
+def scatter_grads(partial):
+    layers, all_rows, cols = partial.shape
+    count = lax.axis_size("fsdp")
+    line = count // 2
+    shard_rows = all_rows // count
+    cols_a = cols - X_FIRST_COLS
+    dma = pltpu.SemaphoreType.DMA
+    low = partial.dtype
+    slots = 2 * line - 1
+    return pl.pallas_call(
+        functools.partial(scatter_kernel, line),
+        out_shape=jax.ShapeDtypeStruct((layers, shard_rows, cols), jnp.float32),
+        in_specs=[pl.BlockSpec(memory_space=pl.ANY)],
+        out_specs=pl.BlockSpec(memory_space=pltpu.VMEM),
+        scratch_shapes=[
+            pltpu.VMEM((layers, line, shard_rows, cols_a), low),
+            pltpu.VMEM((layers, line, shard_rows, cols_a), low),
+            pltpu.VMEM((layers, line - 1, shard_rows, cols_a), low),
+            pltpu.VMEM((layers, line - 1, shard_rows, cols_a), low),
+            pltpu.VMEM((layers, line, 2 * shard_rows, X_FIRST_COLS), low),
+            pltpu.VMEM((layers, line - 1, 2 * shard_rows, X_FIRST_COLS), low),
+            pltpu.VMEM((layers, line - 1, 2 * shard_rows, X_FIRST_COLS), low),
+            pltpu.VMEM((layers, shard_rows, X_FIRST_COLS), low),
+            dma((layers, slots)),
+            dma((layers, slots)),
+            dma((layers, slots)),
+            dma((layers, slots)),
+            dma((layers, line - 1)),
+            dma((layers, line - 1)),
+            dma((layers, line - 1)),
+            dma((layers, line - 1)),
+            dma((layers, line - 1)),
+            dma((layers, line - 1)),
+            dma((layers, line - 1)),
+            dma((layers, line - 1)),
+            dma((layers,)),
+            dma((layers,)),
+        ],
+        compiler_params=pltpu.CompilerParams(
+            collective_id=1, has_side_effects=True, vmem_limit_bytes=60 << 20
+        ),
+        name="scatter_grads",
+    )(partial)
 
 
 EPSILON = 1e-06
@@ -186,6 +584,59 @@
     return (grad_in, layer_grads)
 
 
+SMALL_COLS = 128
+
+
+def pack_shard(qkv_w, out_w, up_w, down_w, gains, shifts, inner_part):
+    layers, rows = qkv_w.shape[:2]
+    columns = jnp.concatenate([gains, shifts, inner_part.reshape(layers, -1, rows)], axis=1)
+    columns = jnp.swapaxes(columns, 1, 2)
+    columns = jnp.pad(columns, ((0, 0), (0, 0), (0, SMALL_COLS - columns.shape[2])))
+    return jnp.concatenate([qkv_w.reshape(layers, rows, -1), out_w, up_w, down_w, columns], axis=2)
+
+
+def unpack(full, head_width, hidden_width, count):
+    layers, width, cols = full.shape
+    ends = [3 * head_width, 4 * head_width, 4 * head_width + hidden_width, 4 * head_width + 2 * hidden_width]
+    small = jnp.swapaxes(full[:, :, ends[3] : ends[3] + 9], 1, 2)
+    inner = small[:, 6:].reshape(layers, 3, count, width // count)
+    inner = jnp.swapaxes(inner, 1, 2).reshape(layers, 1, -1)
+    return (
+        full[:, :, : ends[0]].reshape(layers, width, 3, head_width),
+        full[:, :, ends[0] : ends[1]],
+        full[:, :, ends[1] : ends[2]],
+        full[:, :, ends[2] : ends[3]],
+        small[:, :2],
+        small[:, 2:6],
+        inner,
+    )
+
+
+def pack_grads(grads, count):
+    qkv_g, out_g, up_g, down_g, gain_g, shift_g, inner_g = grads
+    layers, width = qkv_g.shape[:2]
+    inner = jnp.swapaxes(inner_g.reshape(layers, count, 3, width // count), 1, 2).reshape(layers, 3, width)
+    small = jnp.swapaxes(jnp.concatenate([gain_g, shift_g, inner], axis=1), 1, 2)
+    small = jnp.pad(small, ((0, 0), (0, 0), (0, SMALL_COLS - small.shape[2])))
+    whole = jnp.concatenate([qkv_g.reshape(layers, width, -1), out_g, up_g, down_g, small], axis=2)
+    return whole.astype(jnp.bfloat16)
+
+
+def unpack_grads(full, head_width, hidden_width):
+    layers, rows, cols = full.shape
+    ends = [3 * head_width, 4 * head_width, 4 * head_width + hidden_width, 4 * head_width + 2 * hidden_width]
+    small = jnp.swapaxes(full[:, :, ends[3] : ends[3] + 9], 1, 2)
+    return (
+        full[:, :, : ends[0]].reshape(layers, rows, 3, head_width),
+        full[:, :, ends[0] : ends[1]],
+        full[:, :, ends[1] : ends[2]],
+        full[:, :, ends[2] : ends[3]],
+        small[:, :2],
+        small[:, 2:6],
+        small[:, 6:].reshape(layers, 1, -1),
+    )
+
+
 def body(
     block_input,
     image_ids,
@@ -202,15 +653,10 @@
     micro_count = block_input.shape[0]
     layer_count = qkv_weight.shape[0]
     ticks = micro_count + 1
-    gathered = (
-        lax.all_gather(qkv_weight, "fsdp", axis=1, tiled=True),
-        lax.all_gather(out_weight, "fsdp", axis=1, tiled=True),
-        lax.all_gather(up_weight, "fsdp", axis=1, tiled=True),
-        lax.all_gather(down_weight, "fsdp", axis=1, tiled=True),
-        lax.all_gather(norm_gains, "fsdp", axis=2, tiled=True),
-        lax.all_gather(biases, "fsdp", axis=2, tiled=True),
-        lax.all_gather(inner_bias, "fsdp", axis=2, tiled=True),
-    )
+    shard = pack_shard(
+        qkv_weight, out_weight, up_weight, down_weight, norm_gains, biases, inner_bias
+    )
+    gathered = unpack(gather_weights(shard), out_weight.shape[2], up_weight.shape[2], lax.axis_size("fsdp"))
     stored = []
     outputs = []
     received = jnp.zeros(block_input.shape[1:], jnp.bfloat16)
@@ -227,15 +673,6 @@
         outputs.append(hidden)
         if tick_index + 1 < ticks:
             received = shifted(hidden.astype(jnp.bfloat16), "section", 1)
-    gathered = (
-        lax.all_gather(qkv_weight, "fsdp", axis=1, tiled=True),
-        lax.all_gather(out_weight, "fsdp", axis=1, tiled=True),
-        lax.all_gather(up_weight, "fsdp", axis=1, tiled=True),
-        lax.all_gather(down_weight, "fsdp", axis=1, tiled=True),
-        lax.all_gather(norm_gains, "fsdp", axis=2, tiled=True),
-        lax.all_gather(biases, "fsdp", axis=2, tiled=True),
-        lax.all_gather(inner_bias, "fsdp", axis=2, tiled=True),
-    )
     accumulated = None
     grad_inputs = []
     received = jnp.zeros(block_input.shape[1:], jnp.bfloat16)
@@ -264,28 +701,8 @@
             accumulated = tuple(tick_grads)
         else:
             accumulated = jax.tree.map(jnp.add, tuple(accumulated), tuple(tick_grads))
-    accumulated = (
-        lax.psum_scatter(
-            accumulated[0].astype(jnp.bfloat16), "fsdp", scatter_dimension=1, tiled=True
-        ).astype(jnp.float32),
-        lax.psum_scatter(
-            accumulated[1].astype(jnp.bfloat16), "fsdp", scatter_dimension=1, tiled=True
-        ).astype(jnp.float32),
-        lax.psum_scatter(
-            accumulated[2].astype(jnp.bfloat16), "fsdp", scatter_dimension=1, tiled=True
-        ).astype(jnp.float32),
-        lax.psum_scatter(
-            accumulated[3].astype(jnp.bfloat16), "fsdp", scatter_dimension=1, tiled=True
-        ).astype(jnp.float32),
-        lax.psum_scatter(
-            accumulated[4].astype(jnp.bfloat16), "fsdp", scatter_dimension=2, tiled=True
-        ).astype(jnp.float32),
-        lax.psum_scatter(
-            accumulated[5].astype(jnp.bfloat16), "fsdp", scatter_dimension=2, tiled=True
-        ).astype(jnp.float32),
-        lax.psum_scatter(
-            accumulated[6].astype(jnp.bfloat16), "fsdp", scatter_dimension=2, tiled=True
-        ).astype(jnp.float32),
+    accumulated = unpack_grads(
+        scatter_grads(pack_grads(accumulated, lax.axis_size("fsdp"))), out_weight.shape[2], up_weight.shape[2]
     )
     block_outputs = jnp.stack([outputs[micro + 1] for micro in range(micro_count)])
     input_grads = jnp.stack([grad_inputs[micro_count - micro] for micro in range(micro_count)])

time: 2110 us -> 1650 us (0.78)
  waiting for transfers between devices: 1450 us -> 628 us
  Pallas kernels: 0 us -> 406 us
  blocking collectives: 65.1 us -> 0 us
  matrix products: 277 us -> 312 us
  other arithmetic: 181 us -> 154 us
    reduce_scatter x4 -> x0, waiting for transfers between devices: 487 us -> none  [the longest x1 149 us: body(): lax.psum_scatter(accumulated[2].astype(jnp.bfloat16), 'fsdp', scatter_dim...]
    pallas_call x0 -> x2, Pallas kernels: none -> 406 us  [the longest x1 267 us: scatter_grads(): pl.pallas_call(functools.partial(scatter_kernel, line), out_shape=jax.Sha...]
    all_gather x4 -> x0, waiting for transfers between devices: 322 us -> none  [the longest x1 124 us: body(): lax.all_gather(up_weight, 'fsdp', axis=1, tiled=True)]
    psum x11, waiting for transfers between devices: 294 us -> 422 us  [mix_sum(): lax.psum(partial_sum.astype(jnp.bfloat16), 'tensor').astype(jnp.float32)]
    psum x12, waiting for transfers between devices: 286 us -> 204 us  [mix_back(): lax.psum(partial_sum.astype(jnp.bfloat16), 'tensor').astype(jnp.float32)]
    all_gather x3 -> x0, blocking collectives: 65.1 us -> none  [the longest x1 26.2 us: body(): lax.all_gather(inner_bias, 'fsdp', axis=2, tiled=True)]
    convert_element_type x14 -> x0, other arithmetic: 62.4 us -> none  [the longest x1 15.2 us: body(): accumulated[3].astype(jnp.bfloat16)]
    unnamed x37 -> x23, waiting for transfers between devices: 61.6 us -> 0.38 us
  transfers between devices with their start and end apart: 38 -> 27, of which waited for: 35 -> 24; matrix products, arithmetic and copies ran while one was open for 10% -> 10% of each run, Pallas kernels for 0% -> 0%
where the time goes in v1:
time: 1650 us; the launch traced here: 1640 us
  waiting for transfers between devices  628 us (38%)
  Pallas kernels  406 us (25%)
  matrix products  312 us (19%)
  other arithmetic  154 us (9%)
  local copies, waits for them, and re-layouts  107 us (6%)
  between operations  18.1 us (1%)
    psum x11, waiting for transfers between devices, mix_sum(): lax.psum(partial_sum.astype(jnp.bfloat16), 'tensor').astype(jnp.float32)  422 us
    pallas_call x1, Pallas kernels, scatter_grads(): pl.pallas_call(functools.partial(scatter_kernel, line), out_shape=jax.Sha...  267 us
    psum x12, waiting for transfers between devices, mix_back(): lax.psum(partial_sum.astype(jnp.bfloat16), 'tensor').astype(jnp.float32)  204 us
    pallas_call x1, Pallas kernels, gather_weights(): pl.pallas_call(functools.partial(gather_kernel, line), out_shape=jax.Shap...  140 us
    dot_general x24, matrix products, contract_rows(): lax.dot_general(left, right, (((0,), (0,)), ((), ())), preferred_element_...  99.3 us
    dot_general x24, matrix products, contract_last(): lax.dot_general(left, right, (((1,), (1,)), ((), ())), preferred_element_...  93.6 us
    unnamed x6, other arithmetic  57 us
    dot_general x6, matrix products, layer_forward(): jnp.dot(normed_mlp, up_w, preferred_element_type=jnp.float32)  48.3 us
  transfers between devices with their start and end apart: 27, of which 24 were waited for; matrix products, arithmetic and copies ran while one was open for 10% of the time, Pallas kernels for 0%

profile of v1, /device:TPU:0, one launch (start us, length us, event | category | flops | bytes accessed | tf_op | source)
XLA Modules:
  0.0 1636.7 jit_solution(3983053094371798419)
XLA Ops:
  16.3 139.7 %gather_weights.1 = bf16[2,1024,6272]{2,1,0:T(8,128)(2,1)} custom-call(bf16[2,128,6272]{2,1,0:T(8,128)(2,1)} %copy-done.61), custom_call_target="tpu_custom_call" | custom-call | tf_op jit(solution)/shard_map/gather_weights/pallas_call | solution.py:168
  183.2 157.0 %all-reduce.27.cloned.1.call-done = bf16[224,1024]{1,0:T(8,128)(2,1)} async-done(((bf16[224,1024]{1,0:T(8,128)(2,1)}), bf16[224,1024]{1,0:T(8,128)(2,1)}) %all-reduce.27.cloned.1.call-update) | async-done | bytes 458768 | tf_op jit(solution)/shard_map/psum | solution.py:442
  343.5 8.1 multiply_convert_fusion.11
  361.2 22.5 %all-reduce.29.cloned.1.call-done = bf16[224,1024]{1,0:T(8,128)(2,1)} async-done(((bf16[224,1024]{1,0:T(8,128)(2,1)}), bf16[224,1024]{1,0:T(8,128)(2,1)}) %all-reduce.29.cloned.1.call-update) | async-done | bytes 458768 | tf_op jit(solution)/shard_map/psum | solution.py:442
  395.0 27.0 %all-reduce.31.cloned.1.call-done = bf16[224,1024]{1,0:T(8,128)(2,1)} async-done(((bf16[224,1024]{1,0:T(8,128)(2,1)}), bf16[224,1024]{1,0:T(8,128)(2,1)}) %all-reduce.31.cloned.1.call-update) | async-done | bytes 458768 | tf_op jit(solution)/shard_map/psum | solution.py:442
  423.5 8.0 multiply_convert_fusion.10
  437.0 27.3 %all-reduce.33.cloned.1.call-done = bf16[224,1024]{1,0:T(8,128)(2,1)} async-done(((bf16[224,1024]{1,0:T(8,128)(2,1)}), bf16[224,1024]{1,0:T(8,128)(2,1)}) %all-reduce.33.cloned.1.call-update) | async-done | bytes 458768 | tf_op jit(solution)/shard_map/psum | solution.py:442
  478.3 26.8 %all-reduce.35.cloned.1.call-done = bf16[224,1024]{1,0:T(8,128)(2,1)} async-done(((bf16[224,1024]{1,0:T(8,128)(2,1)}), bf16[224,1024]{1,0:T(8,128)(2,1)}) %all-reduce.35.cloned.1.call-update) | async-done | bytes 458768 | tf_op jit(solution)/shard_map/psum | solution.py:442
  507.8 8.2 multiply_convert_fusion.9
  520.8 27.3 %all-reduce.37.cloned.1.call-done = bf16[224,1024]{1,0:T(8,128)(2,1)} async-done(((bf16[224,1024]{1,0:T(8,128)(2,1)}), bf16[224,1024]{1,0:T(8,128)(2,1)}) %all-reduce.37.cloned.1.call-update) | async-done | bytes 458768 | tf_op jit(solution)/shard_map/psum | solution.py:442
  559.4 27.1 %all-reduce.39.cloned.1.call-done = bf16[224,1024]{1,0:T(8,128)(2,1)} async-done(((bf16[224,1024]{1,0:T(8,128)(2,1)}), bf16[224,1024]{1,0:T(8,128)(2,1)}) %all-reduce.39.cloned.1.call-update) | async-done | bytes 458768 | tf_op jit(solution)/shard_map/psum | solution.py:442
  588.0 8.1 multiply_convert_fusion.8
  601.6 27.3 %all-reduce.41.cloned.1.call-done = bf16[224,1024]{1,0:T(8,128)(2,1)} async-done(((bf16[224,1024]{1,0:T(8,128)(2,1)}), bf16[224,1024]{1,0:T(8,128)(2,1)}) %all-reduce.41.cloned.1.call-update) | async-done | bytes 458768 | tf_op jit(solution)/shard_map/psum | solution.py:442
  642.0 27.1 %all-reduce.43.cloned.1.call-done = bf16[224,1024]{1,0:T(8,128)(2,1)} async-done(((bf16[224,1024]{1,0:T(8,128)(2,1)}), bf16[224,1024]{1,0:T(8,128)(2,1)}) %all-reduce.43.cloned.1.call-update) | async-done | bytes 458768 | tf_op jit(solution)/shard_map/psum | solution.py:442
  671.8 8.2 multiply_convert_fusion.7
  685.4 26.6 %all-reduce.45.cloned.1.call-done = bf16[224,1024]{1,0:T(8,128)(2,1)} async-done(((bf16[224,1024]{1,0:T(8,128)(2,1)}), bf16[224,1024]{1,0:T(8,128)(2,1)}) %all-reduce.45.cloned.1.call-update) | async-done | bytes 458768 | tf_op jit(solution)/shard_map/psum | solution.py:442
  725.8 26.4 %all-reduce.47.cloned.1.call-done = bf16[224,1024]{1,0:T(8,128)(2,1)} async-done(((bf16[224,1024]{1,0:T(8,128)(2,1)}), bf16[224,1024]{1,0:T(8,128)(2,1)}) %all-reduce.47.cloned.1.call-update) | async-done | bytes 458768 | tf_op jit(solution)/shard_map/psum | solution.py:442
  782.8 16.6 %all-reduce.49.cloned.1.call-done = bf16[224,1024]{1,0:T(8,128)(2,1)} async-done(((bf16[224,1024]{1,0:T(8,128)(2,1)}), bf16[224,1024]{1,0:T(8,128)(2,1)}) %all-reduce.49.cloned.1.call-update) | async-done | bytes 458768 | tf_op jit(solution)/shard_map/psum | solution.py:446
  835.5 11.5 all-reduce.51.cloned.1.call-done
  870.0 19.9 %all-reduce.53.cloned.1.call-done = bf16[224,1024]{1,0:T(8,128)(2,1)} async-done(((bf16[224,1024]{1,0:T(8,128)(2,1)}), bf16[224,1024]{1,0:T(8,128)(2,1)}) %all-reduce.53.cloned.1.call-update) | async-done | bytes 458768 | tf_op jit(solution)/shard_map/psum | solution.py:446
  917.7 17.8 %all-reduce.55.cloned.1.call-done = bf16[224,1024]{1,0:T(8,128)(2,1)} async-done(((bf16[224,1024]{1,0:T(8,128)(2,1)}), bf16[224,1024]{1,0:T(8,128)(2,1)}) %all-reduce.55.cloned.1.call-update) | async-done | bytes 458768 | tf_op jit(solution)/shard_map/psum | solution.py:446
  966.5 18.7 %all-reduce.57.cloned.1.call-done = bf16[224,1024]{1,0:T(8,128)(2,1)} async-done(((bf16[224,1024]{1,0:T(8,128)(2,1)}), bf16[224,1024]{1,0:T(8,128)(2,1)}) %all-reduce.57.cloned.1.call-update) | async-done | bytes 458768 | tf_op jit(solution)/shard_map/psum | solution.py:446
  1009.7 20.4 %all-reduce.59.cloned.1.call-done = bf16[224,1024]{1,0:T(8,128)(2,1)} async-done(((bf16[224,1024]{1,0:T(8,128)(2,1)}), bf16[224,1024]{1,0:T(8,128)(2,1)}) %all-reduce.59.cloned.1.call-update) | async-done | bytes 458768 | tf_op jit(solution)/shard_map/psum | solution.py:446
  1050.2 21.2 %all-reduce.61.cloned.1.call-done = bf16[224,1024]{1,0:T(8,128)(2,1)} async-done(((bf16[224,1024]{1,0:T(8,128)(2,1)}), bf16[224,1024]{1,0:T(8,128)(2,1)}) %all-reduce.61.cloned.1.call-update) | async-done | bytes 458768 | tf_op jit(solution)/shard_map/psum | solution.py:446
  1097.6 18.6 %all-reduce.63.cloned.1.call-done = bf16[224,1024]{1,0:T(8,128)(2,1)} async-done(((bf16[224,1024]{1,0:T(8,128)(2,1)}), bf16[224,1024]{1,0:T(8,128)(2,1)}) %all-reduce.63.cloned.1.call-update) | async-done | bytes 458768 | tf_op jit(solution)/shard_map/psum | solution.py:446
  1147.8 17.8 %all-reduce.65.cloned.1.call-done = bf16[224,1024]{1,0:T(8,128)(2,1)} async-done(((bf16[224,1024]{1,0:T(8,128)(2,1)}), bf16[224,1024]{1,0:T(8,128)(2,1)}) %all-reduce.65.cloned.1.call-update) | async-done | bytes 458768 | tf_op jit(solution)/shard_map/psum | solution.py:446
  1189.3 20.1 %all-reduce.67.cloned.1.call-done = bf16[224,1024]{1,0:T(8,128)(2,1)} async-done(((bf16[224,1024]{1,0:T(8,128)(2,1)}), bf16[224,1024]{1,0:T(8,128)(2,1)}) %all-reduce.67.cloned.1.call-update) | async-done | bytes 458768 | tf_op jit(solution)/shard_map/psum | solution.py:446
  1233.1 21.4 %all-reduce.69.cloned.1.call-done = bf16[224,1024]{1,0:T(8,128)(2,1)} async-done(((bf16[224,1024]{1,0:T(8,128)(2,1)}), bf16[224,1024]{1,0:T(8,128)(2,1)}) %all-reduce.69.cloned.1.call-update) | async-done | bytes 458768 | tf_op jit(solution)/shard_map/psum | solution.py:446
  1278.8 17.1 %fusion.8 = bf16[2,1024,6272]{2,1,0:T(8,128)(2,1)} fusion(f32[1,1024,1536]{2,1,0:T(8,128)} %convolution_bitcast_fusion.12, f32[1,1024,1536]{2,1,0:T(8,128)} %convolution_bitcast_fusion.13, f32[1,1024,1536]{2,1,0:T(8,128)} %convolution_bitcast_fusion.14, f32[1,1024,1536]{2,1,0:T(8,128)} %convolution_bitcast_fusion.15, ...), kind=kLoop, calls=%fused_computation.11 | loop fusion | flops 18874368 | bytes 44040192
  1300.0 21.1 %fusion.7 = bf16[2,1024,6272]{2,1,0:T(8,128)(2,1)} fusion(bf16[2,1024,6272]{2,1,0:T(8,128)(2,1)} %fusion.89, f32[1,1024,2048]{2,1,0:T(8,128)} %convolution_bitcast_fusion.6, f32[1,1024,2048]{2,1,0:T(8,128)} %convolution_bitcast_fusion.7, f32[1,1024,2048]{2,1,0:T(8,128)} %convolution_bitcast_fusion.8, f32[1,1024,2048]{2,1,0:T(8,128)} %convolution_bitcast_fusion.9, ...), kind=kLoop, calls=%fused_computation.10 | loop fusion | flops 25165824 | bytes 58720256
  1321.2 15.0 fusion.6
  1343.5 266.6 %scatter_grads.1 = f32[2,128,6272]{2,1,0:T(8,128)} custom-call(bf16[2,1024,6272]{2,1,0:T(8,128)(2,1)} %pad_dynamic-update-slice_fusion.d_ref), custom_call_target="tpu_custom_call" | custom-call | tf_op jit(solution)/shard_map/scatter_grads/pallas_call | solution.py:373
  (1115 shorter events, 492.4 us)
Async XLA Ops:
  7.2 333.1 %all-reduce.27.cloned.1.call-start = ((), (), s32[]{:S(2)}) async-start(), calls=%async_computation | async-start | bytes 917504 | tf_op jit(solution)/shard_map/psum | solution.py:442
  172.9 249.1 %copy-start.180 = (f32[1024]{0:T(1024)}, f32[1024]{0:T(1024)S(1)}, u32[]{:S(2)}) copy-start(f32[1024]{0:T(1024)S(1)} %get-tuple-element.82) | copy-start | bytes 12292
  172.9 291.4 %copy-start.177 = (f32[1024]{0:T(1024)}, f32[1024]{0:T(1024)S(1)}, u32[]{:S(2)}) copy-start(f32[1024]{0:T(1024)S(1)} %get-tuple-element.80) | copy-start | bytes 12292
  177.4 460.8 %copy-start.161 = (f32[8,64]{1,0:T(8,128)}, f32[8,64]{1,0:T(8,128)S(1)}, u32[]{:S(2)}) copy-start(f32[8,64]{1,0:T(8,128)S(1)} %get-tuple-element.189) | copy-start | bytes 6148
  180.3 162.6 %copy-start.145 = (bf16[8,64,224]{2,1,0:T(8,128)(2,1)}, bf16[8,64,224]{2,1,0:T(8,128)(2,1)S(1)}, u32[]{:S(2)}) copy-start(bf16[8,64,224]{2,1,0:T(8,128)(2,1)S(1)} %convolution_convert_fusion.17) | copy-start | bytes 688132
  182.9 200.7 %all-reduce.29.cloned.1.call-start = ((), (), s32[]{:S(2)}) async-start(), calls=%async_computation.1 | async-start | bytes 917504 | tf_op jit(solution)/shard_map/psum | solution.py:442
  183.2 168.4 %copy-start.321 = (f32[2048]{0:T(1024)}, f32[2048]{0:T(1024)S(1)}, u32[]{:S(2)}) copy-start(f32[2048]{0:T(1024)S(1)} %slice_convert_fusion.11) | copy-start | bytes 24580
  356.4 65.6 %all-reduce.31.cloned.1.call-start = ((), (), s32[]{:S(2)}) async-start(), calls=%async_computation.2 | async-start | bytes 917504 | tf_op jit(solution)/shard_map/psum | solution.py:442
  394.7 69.6 %all-reduce.33.cloned.1.call-start = ((), (), s32[]{:S(2)}) async-start(), calls=%async_computation.3 | async-start | bytes 917504 | tf_op jit(solution)/shard_map/psum | solution.py:442
  437.0 68.1 %all-reduce.35.cloned.1.call-start = ((), (), s32[]{:S(2)}) async-start(), calls=%async_computation.4 | async-start | bytes 917504 | tf_op jit(solution)/shard_map/psum | solution.py:442
  465.6 3.2 collective-permute-start
  477.8 70.3 %all-reduce.37.cloned.1.call-start = ((), (), s32[]{:S(2)}) async-start(), calls=%async_computation.5 | async-start | bytes 917504 | tf_op jit(solution)/shard_map/psum | solution.py:442
  520.8 65.7 %all-reduce.39.cloned.1.call-start = ((), (), s32[]{:S(2)}) async-start(), calls=%async_computation.6 | async-start | bytes 917504 | tf_op jit(solution)/shard_map/psum | solution.py:442
  559.2 69.7 %all-reduce.41.cloned.1.call-start = ((), (), s32[]{:S(2)}) async-start(), calls=%async_computation.7 | async-start | bytes 917504 | tf_op jit(solution)/shard_map/psum | solution.py:442
  601.5 67.5 %all-reduce.43.cloned.1.call-start = ((), (), s32[]{:S(2)}) async-start(), calls=%async_computation.8 | async-start | bytes 917504 | tf_op jit(solution)/shard_map/psum | solution.py:442
  631.1 3.2 collective-permute-start.1
  641.7 70.3 %all-reduce.45.cloned.1.call-start = ((), (), s32[]{:S(2)}) async-start(), calls=%async_computation.9 | async-start | bytes 917504 | tf_op jit(solution)/shard_map/psum | solution.py:442
  684.7 67.4 %all-reduce.47.cloned.1.call-start = ((), (), s32[]{:S(2)}) async-start(), calls=%async_computation.10 | async-start | bytes 917504 | tf_op jit(solution)/shard_map/psum | solution.py:442
  724.9 74.4 %all-reduce.49.cloned.1.call-start = ((), (), s32[]{:S(2)}) async-start(), calls=%async_computation.11 | async-start | bytes 917504 | tf_op jit(solution)/shard_map/psum | solution.py:446
  772.0 75.0 %all-reduce.51.cloned.1.call-start = ((), (), s32[]{:S(2)}) async-start(), calls=%async_computation.12 | async-start | bytes 917504 | tf_op jit(solution)/shard_map/psum | solution.py:446
  819.7 70.2 %all-reduce.53.cloned.1.call-start = ((), (), s32[]{:S(2)}) async-start(), calls=%async_computation.13 | async-start | bytes 917504 | tf_op jit(solution)/shard_map/psum | solution.py:446
  862.5 72.9 %all-reduce.55.cloned.1.call-start = ((), (), s32[]{:S(2)}) async-start(), calls=%async_computation.14 | async-start | bytes 917504 | tf_op jit(solution)/shard_map/psum | solution.py:446
  908.1 77.0 %all-reduce.57.cloned.1.call-start = ((), (), s32[]{:S(2)}) async-start(), calls=%async_computation.15 | async-start | bytes 917504 | tf_op jit(solution)/shard_map/psum | solution.py:446
  940.1 6.9 collective-permute-start.2
  957.1 73.0 %all-reduce.59.cloned.1.call-start = ((), (), s32[]{:S(2)}) async-start(), calls=%async_computation.16 | async-start | bytes 917504 | tf_op jit(solution)/shard_map/psum | solution.py:446
  1002.8 68.6 %all-reduce.61.cloned.1.call-start = ((), (), s32[]{:S(2)}) async-start(), calls=%async_computation.17 | async-start | bytes 917504 | tf_op jit(solution)/shard_map/psum | solution.py:446
  1044.1 72.1 %all-reduce.63.cloned.1.call-start = ((), (), s32[]{:S(2)}) async-start(), calls=%async_computation.18 | async-start | bytes 917504 | tf_op jit(solution)/shard_map/psum | solution.py:446
  1088.9 76.6 %all-reduce.65.cloned.1.call-start = ((), (), s32[]{:S(2)}) async-start(), calls=%async_computation.19 | async-start | bytes 917504 | tf_op jit(solution)/shard_map/psum | solution.py:446
  1120.9 6.6 collective-permute-start.3
  1137.5 72.0 %all-reduce.67.cloned.1.call-start = ((), (), s32[]{:S(2)}) async-start(), calls=%async_computation.20 | async-start | bytes 917504 | tf_op jit(solution)/shard_map/psum | solution.py:446
  1182.2 72.3 %all-reduce.69.cloned.1.call-start = ((), (), s32[]{:S(2)}) async-start(), calls=%async_computation.21 | async-start | bytes 917504 | tf_op jit(solution)/shard_map/psum | solution.py:446
  1227.2 109.2 %all-reduce.71.cloned.1.call-start = ((), (), s32[]{:S(2)}) async-start(), calls=%async_computation.22 | async-start | bytes 1835008 | tf_op jit(solution)/shard_map/psum | solution.py:446
  (339 other events, 2683.1 us)
Sparse Core Ops, SparseCore 0:
  183.1 157.1 all-reduce.26
  356.5 27.1 all-reduce.28
  394.8 27.1 all-reduce.30
  437.1 27.1 all-reduce.32
  477.9 27.1 all-reduce.34
  520.9 27.1 all-reduce.36
  559.3 27.1 all-reduce.38
  601.7 27.1 all-reduce.40
  641.8 27.1 all-reduce.42
  684.9 27.1 all-reduce.44
  725.0 27.1 all-reduce.46
  772.1 27.1 all-reduce.48
  819.8 27.1 all-reduce.50
  862.7 27.1 all-reduce.52
  908.2 27.1 all-reduce.54
  957.1 27.9 all-reduce.56
  1002.9 27.1 all-reduce.58
  1044.2 27.1 all-reduce.60
  1089.0 27.1 all-reduce.62
  1137.5 27.9 all-reduce.64
  1182.3 27.1 all-reduce.66
  1227.3 27.1 all-reduce.68
  1278.9 37.3 all-reduce.70

commit v2 on v1

--- a/solution.py
+++ b/solution.py
@@ -9,6 +9,9 @@
 from jax.sharding import PartitionSpec as P
 
 HEAD_DIM = 64
+EPSILON = 1e-06
+
+
 MESH = pl.DeviceIdType.MESH
 X_FIRST_COLS = 1024
 
@@ -406,185 +409,25 @@
     )(partial)
 
 
-EPSILON = 1e-06
+SMALL_COLS = 128
+
+
+def contract_last(left, right):
+    return lax.dot_general(
+        left, right, (((1,), (1,)), ((), ())), preferred_element_type=jnp.float32
+    )
+
+
+def contract_rows(left, right):
+    return lax.dot_general(
+        left, right, (((0,), (0,)), ((), ())), preferred_element_type=jnp.float32
+    )
 
 
 def shifted(value, axis, steps):
     count = lax.axis_size(axis)
     initial, last = (max(0, -steps), min(count, count - steps))
     return lax.ppermute(value, axis, [(source, source + steps) for source in range(initial, last)])
-
-
-def layer_norm(hidden, weight_gain, weight_shift):
-    average = jnp.mean(hidden, axis=-1, keepdims=True)
-    centred = hidden - average
-    spread = jnp.mean(centred * centred, axis=-1, keepdims=True)
-    return centred * lax.rsqrt(spread + EPSILON) * weight_gain + weight_shift
-
-
-def gelu_exact(upward):
-    return jax.nn.gelu(upward, approximate=False)
-
-
-def contract_last(left, right):
-    return lax.dot_general(
-        left, right, (((1,), (1,)), ((), ())), preferred_element_type=jnp.float32
-    )
-
-
-def contract_rows(left, right):
-    return lax.dot_general(
-        left, right, (((0,), (0,)), ((), ())), preferred_element_type=jnp.float32
-    )
-
-
-def mix_sum(partial_sum):
-    return lax.psum(partial_sum.astype(jnp.bfloat16), "tensor").astype(jnp.float32)
-
-
-def mix_back(partial_sum):
-    return lax.psum(partial_sum.astype(jnp.bfloat16), "tensor").astype(jnp.float32)
-
-
-def allowed_pairs(ids_batch):
-    places = jnp.arange(ids_batch.shape[0], dtype=jnp.int32)
-    same_image = (ids_batch[:, None] == ids_batch[None, :]) & (ids_batch[:, None] >= 0)
-    return same_image | (places[:, None] == places[None, :])
-
-
-def masked_scores(query_heads, key_rows, allowed):
-    head_count = query_heads.shape[1]
-    key_heads = key_rows.reshape(-1, head_count, HEAD_DIM)
-    scores = jnp.einsum("qhe,khe->hqk", query_heads, key_heads, preferred_element_type=jnp.float32)
-    scores = scores * (1.0 / math.sqrt(HEAD_DIM))
-    return (jnp.where(allowed[None], scores, -1e30), key_heads)
-
-
-def layer_slice(gathered, layer_index):
-    return tuple((array[layer_index] for array in gathered))
-
-
-def layer_forward(hidden, weights, ids_batch):
-    qkv_w, out_w, up_w, down_w, gains, shifts, inner_part = weights
-    row_count, model_width = hidden.shape
-    head_width = out_w.shape[1]
-    head_count = head_width // HEAD_DIM
-    gains32 = gains.astype(jnp.float32)
-    shifts32 = shifts.astype(jnp.float32)
-    inner32 = inner_part[0].astype(jnp.float32)
-    normed = layer_norm(hidden, gains32[0], shifts32[0]).astype(jnp.bfloat16)
-    projected = jnp.dot(
-        normed, qkv_w.reshape(model_width, 3 * head_width), preferred_element_type=jnp.float32
-    ).reshape(row_count, 3, head_width)
-    queries = (projected[:, 0] + inner32[:head_width]).astype(jnp.bfloat16)
-    key_rows = projected[:, 1].astype(jnp.bfloat16)
-    value_rows = (projected[:, 2] + inner32[head_width : 2 * head_width]).astype(jnp.bfloat16)
-    allowed = allowed_pairs(ids_batch)
-    scores, key_heads = masked_scores(
-        queries.reshape(row_count, head_count, HEAD_DIM), key_rows, allowed
-    )
-    row_top = jnp.max(scores, axis=-1, keepdims=True)
-    exponent = jnp.exp(scores - row_top)
-    row_total = jnp.sum(exponent, axis=-1, keepdims=True)
-    probs = (exponent / row_total).astype(jnp.bfloat16)
-    log_total = row_top + jnp.log(row_total)
-    value_heads = value_rows.reshape(-1, head_count, HEAD_DIM)
-    mixed_heads = jnp.einsum("hqk,khe->qhe", probs, value_heads, preferred_element_type=jnp.float32)
-    mixed_heads = mixed_heads.reshape(row_count, head_width).astype(jnp.bfloat16)
-    attended = mix_sum(contract_last(mixed_heads, out_w)) + shifts32[1]
-    middle = hidden + attended
-    normed_mlp = layer_norm(middle, gains32[1], shifts32[2]).astype(jnp.bfloat16)
-    upward = (
-        jnp.dot(normed_mlp, up_w, preferred_element_type=jnp.float32) + inner32[2 * head_width :]
-    )
-    activated = gelu_exact(upward).astype(jnp.bfloat16)
-    result = middle + (mix_sum(contract_last(activated, down_w)) + shifts32[3])
-    kept = (hidden, queries, key_rows, value_rows, log_total, mixed_heads, middle, upward)
-    return (result, kept)
-
-
-def layer_backward(grad_out, kept, weights, ids_batch):
-    qkv_w, out_w, up_w, down_w, gains, shifts, inner_part = weights
-    hidden, queries, key_rows, value_rows, log_total, mixed_heads, middle, upward = kept
-    row_count, model_width = hidden.shape
-    head_width = out_w.shape[1]
-    head_count = head_width // HEAD_DIM
-    gains32 = gains.astype(jnp.float32)
-    shifts32 = shifts.astype(jnp.float32)
-    score_scale = 1.0 / math.sqrt(HEAD_DIM)
-    grad_low = grad_out.astype(jnp.bfloat16)
-    down_bias_grad = jnp.sum(grad_low.astype(jnp.float32), axis=0)
-    activated, gelu_back = jax.vjp(gelu_exact, upward)
-    activated = activated.astype(jnp.bfloat16)
-    down_w_grad = contract_rows(grad_low, activated)
-    grad_act = jnp.dot(grad_low, down_w, preferred_element_type=jnp.float32)
-    grad_up = gelu_back(grad_act)[0].astype(jnp.bfloat16)
-    up_bias_grad = jnp.sum(grad_up.astype(jnp.float32), axis=0)
-    normed_mlp, second_back = jax.vjp(layer_norm, middle, gains32[1], shifts32[2])
-    up_w_grad = contract_rows(normed_mlp.astype(jnp.bfloat16), grad_up)
-    grad_norm = mix_back(contract_last(grad_up, up_w))
-    middle_part, second_gain_grad, second_shift_grad = second_back(grad_norm)
-    grad_middle = grad_out + middle_part
-    grad_attn = grad_middle.astype(jnp.bfloat16)
-    out_bias_grad = jnp.sum(grad_attn.astype(jnp.float32), axis=0)
-    out_w_grad = contract_rows(grad_attn, mixed_heads)
-    grad_mixed = jnp.dot(grad_attn, out_w, preferred_element_type=jnp.float32).astype(jnp.bfloat16)
-    allowed = allowed_pairs(ids_batch)
-    query_heads = queries.reshape(row_count, head_count, HEAD_DIM)
-    scores, key_heads = masked_scores(query_heads, key_rows, allowed)
-    probs = jnp.exp(scores - log_total)
-    value_heads = value_rows.reshape(-1, head_count, HEAD_DIM)
-    grad_mixed_heads = grad_mixed.reshape(row_count, head_count, HEAD_DIM)
-    grad_probs = jnp.einsum(
-        "qhe,khe->hqk", grad_mixed_heads, value_heads, preferred_element_type=jnp.float32
-    )
-    value_term = jnp.einsum(
-        "hqk,qhe->khe",
-        probs.astype(jnp.bfloat16),
-        grad_mixed_heads,
-        preferred_element_type=jnp.float32,
-    )
-    centre_term = jnp.sum(probs * grad_probs, axis=-1, keepdims=True)
-    grad_scores = (probs * (grad_probs - centre_term)).astype(jnp.bfloat16)
-    grad_queries = jnp.einsum(
-        "hqk,khe->qhe", grad_scores, key_heads, preferred_element_type=jnp.float32
-    )
-    grad_queries = (grad_queries * score_scale).reshape(row_count, head_width).astype(jnp.bfloat16)
-    key_term = jnp.einsum(
-        "hqk,qhe->khe", grad_scores, query_heads, preferred_element_type=jnp.float32
-    )
-    grad_keys = (key_term * score_scale).reshape(row_count, head_width).astype(jnp.bfloat16)
-    grad_values = value_term.reshape(row_count, head_width).astype(jnp.bfloat16)
-    grad_qkv = jnp.stack([grad_queries, grad_keys, grad_values], axis=1).reshape(
-        row_count, 3 * head_width
-    )
-    normed, first_back = jax.vjp(layer_norm, hidden, gains32[0], shifts32[0])
-    qkv_w_grad = contract_rows(normed.astype(jnp.bfloat16), grad_qkv).reshape(
-        model_width, 3, head_width
-    )
-    grad_normed = mix_back(contract_last(grad_qkv, qkv_w.reshape(model_width, 3 * head_width)))
-    hidden_part, first_gain_grad, first_shift_grad = first_back(grad_normed)
-    grad_in = grad_middle + hidden_part
-    inner_grad = jnp.concatenate(
-        [
-            jnp.sum(grad_queries.astype(jnp.float32), axis=0),
-            jnp.sum(grad_values.astype(jnp.float32), axis=0),
-            up_bias_grad,
-        ]
-    )[None]
-    layer_grads = (
-        qkv_w_grad,
-        out_w_grad,
-        up_w_grad,
-        down_w_grad,
-        jnp.stack([first_gain_grad, second_gain_grad]),
-        jnp.stack([first_shift_grad, out_bias_grad, second_shift_grad, down_bias_grad]),
-        inner_grad,
-    )
-    return (grad_in, layer_grads)
-
-
-SMALL_COLS = 128
 
 
 def pack_shard(qkv_w, out_w, up_w, down_w, gains, shifts, inner_part):
@@ -595,31 +438,655 @@
     return jnp.concatenate([qkv_w.reshape(layers, rows, -1), out_w, up_w, down_w, columns], axis=2)
 
 
-def unpack(full, head_width, hidden_width, count):
+def unpack_params(full, head_width, count):
     layers, width, cols = full.shape
-    ends = [3 * head_width, 4 * head_width, 4 * head_width + hidden_width, 4 * head_width + 2 * hidden_width]
-    small = jnp.swapaxes(full[:, :, ends[3] : ends[3] + 9], 1, 2)
+    small = jnp.swapaxes(full[:, :, cols - SMALL_COLS : cols - SMALL_COLS + 9], 1, 2).astype(jnp.float32)
     inner = small[:, 6:].reshape(layers, 3, count, width // count)
     inner = jnp.swapaxes(inner, 1, 2).reshape(layers, 1, -1)
+    query_bias, value_bias, up_bias = jnp.split(inner, [head_width, 2 * head_width], axis=2)
+    qkv_bias = jnp.concatenate([query_bias, jnp.zeros_like(query_bias), value_bias], axis=2)
+    return small[:, :6], qkv_bias, up_bias
+
+
+LANES = 128
+
+
+def forward_kernel(
+    tick, has_alias, head_width, hidden_width, h0_ref, ids_col_ref, ids_row_ref, rows_ref, qkv_bias_ref, up_bias_ref, full_ref, *refs
+):
+    saved_count = 9
+    if has_alias:
+        refs = refs[saved_count:]
+    outs = refs[:saved_count]
+    (
+        w_qkv, w_out, w_up, w_down, hid, qkv, lse, mixed, mid, act, slope, final, final_low,
+        normed, mask, send, recv, w_sem, save_sem, send_sem, recv_sem,
+    ) = refs[saved_count:]
+    layers, micro, tokens, width = hid.shape
+    section = lax.axis_index("section")
+    partner = {"tensor": 1 - lax.axis_index("tensor")}
+
+    @pl.when(section == tick)
+    def _():
+        ends = (0, 3 * head_width, 4 * head_width, 4 * head_width + hidden_width, 4 * head_width + 2 * hidden_width)
+
+        def fetch(layer, index):
+            buffer = (w_qkv, w_out, w_up, w_down)[index]
+            return pltpu.make_async_copy(
+                full_ref.at[layer, :, pl.ds(ends[index], ends[index + 1] - ends[index])],
+                buffer.at[layer],
+                w_sem.at[layer, index],
+            )
+
+        for layer in range(layers):
+            for index in range(4):
+                fetch(layer, index).start()
+        barrier = pltpu.get_barrier_semaphore()
+        pl.semaphore_signal(barrier, inc=1, device_id=partner, device_id_type=MESH)
+        pl.semaphore_wait(barrier, 1)
+
+        def save(index, source, layer, part):
+            return pltpu.make_async_copy(source.at[layer, part], outs[index].at[layer, part], save_sem.at[index, layer, part])
+
+        saves = ((0, hid), (1, qkv), (2, lse), (3, mixed), (4, mid), (5, act), (6, slope))
+
+        def exchange(layer, stage, part):
+            return pltpu.make_async_remote_copy(
+                src_ref=send.at[layer, stage, part],
+                dst_ref=recv.at[layer, stage, part],
+                send_sem=send_sem.at[layer, stage, part],
+                recv_sem=recv_sem.at[layer, stage, part],
+                device_id=partner,
+                device_id_type=MESH,
+            )
+
+        for part in range(micro):
+            col = ids_col_ref[part]
+            row = ids_row_ref[part]
+            one = lax.broadcasted_iota(jnp.int32, (tokens, tokens), 0)
+            two = lax.broadcasted_iota(jnp.int32, (tokens, tokens), 1)
+            allowed = ((col == row) & (col >= 0)) | (one == two)
+            mask[part] = jnp.where(allowed, 0.0, -1e30)
+
+        def norm_rows(value, gain, shift):
+            average = jnp.mean(value, axis=-1, keepdims=True)
+            centred = value - average
+            spread = jnp.mean(centred * centred, axis=-1, keepdims=True)
+            return centred * lax.rsqrt(spread + EPSILON) * gain + shift
+
+        def joined(layer, stage, part, span):
+            return send[layer, stage, part, span].astype(jnp.float32) + recv[layer, stage, part, span].astype(jnp.float32)
+
+        def attention_stage(layer, part):
+            @pl.when(layer > 0)
+            def _():
+                exchange(layer - 1, 1, part).wait_recv()
+
+                @pl.loop(0, tokens, step=32)
+                def _(start):
+                    span = pl.ds(pl.multiple_of(start, 32), 32)
+                    hid[layer, part, span] = mid[layer - 1, part, span] + (
+                        joined(layer - 1, 1, part, span) + rows_ref[layer - 1, 5:6]
+                    )
+
+            @pl.when(layer == 0)
+            def _():
+                @pl.loop(0, tokens, step=32)
+                def _(start):
+                    span = pl.ds(pl.multiple_of(start, 32), 32)
+                    hid[layer, part, span] = h0_ref[part, span].astype(jnp.float32)
+
+            @pl.loop(0, tokens, step=32)
+            def _(start):
+                span = pl.ds(pl.multiple_of(start, 32), 32)
+                normed[span] = norm_rows(hid[layer, part, span], rows_ref[layer, 0:1], rows_ref[layer, 2:3]).astype(jnp.bfloat16)
+
+            @pl.when(part == 0)
+            def _():
+                fetch(layer, 0).wait()
+
+            for piece in range(3):
+                @pl.loop(0, head_width, step=256)
+                def _(start, piece=piece):
+                    span = pl.ds(pl.multiple_of(piece * head_width + start, 256), 256)
+                    value = jnp.dot(normed[...], w_qkv[layer, :, span], preferred_element_type=jnp.float32)
+                    value = (value + qkv_bias_ref[layer, :, span]).astype(jnp.bfloat16)
+                    if piece == 0:
+                        value = value * jnp.asarray(1.0 / math.sqrt(HEAD_DIM), jnp.bfloat16)
+                    qkv[layer, part, :, span] = value
+
+            lane = lax.broadcasted_iota(jnp.int32, (tokens, LANES), 1)
+            tops = []
+            for pair in range(head_width // LANES):
+                q2 = qkv[layer, part, :, pair * LANES : (pair + 1) * LANES]
+                k2 = qkv[layer, part, :, head_width + pair * LANES : head_width + (pair + 1) * LANES]
+                v2 = qkv[layer, part, :, 2 * head_width + pair * LANES : 2 * head_width + (pair + 1) * LANES]
+                halves = []
+                for side in range(2):
+                    live = (lane < HEAD_DIM) if side == 0 else (lane >= HEAD_DIM)
+                    scores = contract_last(jnp.where(live, q2, jnp.zeros_like(q2)), k2) + mask[part]
+                    top = jnp.max(scores, axis=-1, keepdims=True)
+                    exponent = jnp.exp(scores - top)
+                    total = jnp.sum(exponent, axis=-1, keepdims=True)
+                    probs = (exponent / total).astype(jnp.bfloat16)
+                    halves.append(jnp.dot(probs, v2, preferred_element_type=jnp.float32))
+                    head = 2 * pair + side
+                    lse[layer, part, :, head : head + 1] = top + jnp.log(total)
+                mixed[layer, part, :, pair * LANES : (pair + 1) * LANES] = jnp.where(
+                    lane < HEAD_DIM, halves[0], halves[1]
+                ).astype(jnp.bfloat16)
+
+            @pl.when(part == 0)
+            def _():
+                fetch(layer, 1).wait()
+
+            @pl.loop(0, width, step=256)
+            def _(start):
+                span = pl.ds(pl.multiple_of(start, 256), 256)
+                value = contract_last(mixed[layer, part], w_out[layer, span])
+                send[layer, 0, part, :, span] = value.astype(jnp.bfloat16)
+
+            exchange(layer, 0, part).start()
+            for index in range(4):
+                save(index, saves[index][1], layer, part).start()
+
+        def mlp_stage(layer, part):
+            exchange(layer, 0, part).wait_recv()
+
+            @pl.loop(0, tokens, step=32)
+            def _(start):
+                span = pl.ds(pl.multiple_of(start, 32), 32)
+                middle = hid[layer, part, span] + (joined(layer, 0, part, span) + rows_ref[layer, 3:4])
+                mid[layer, part, span] = middle
+                normed[span] = norm_rows(middle, rows_ref[layer, 1:2], rows_ref[layer, 4:5]).astype(jnp.bfloat16)
+
+            @pl.when(part == 0)
+            def _():
+                fetch(layer, 2).wait()
+
+            @pl.loop(0, hidden_width, step=256)
+            def _(start):
+                span = pl.ds(pl.multiple_of(start, 256), 256)
+                upward = jnp.dot(normed[...], w_up[layer, :, span], preferred_element_type=jnp.float32)
+                upward = upward + up_bias_ref[layer, :, span]
+                phi = 0.5 + 0.5 * lax.erf(upward * math.sqrt(0.5))
+                density = jnp.exp(-0.5 * upward * upward) * (1.0 / math.sqrt(2.0 * math.pi))
+                act[layer, part, :, span] = (upward * phi).astype(jnp.bfloat16)
+                slope[layer, part, :, span] = (phi + upward * density).astype(jnp.bfloat16)
+
+            @pl.when(part == 0)
+            def _():
+                fetch(layer, 3).wait()
+
+            @pl.loop(0, width, step=256)
+            def _(start):
+                span = pl.ds(pl.multiple_of(start, 256), 256)
+                value = contract_last(act[layer, part], w_down[layer, span])
+                send[layer, 1, part, :, span] = value.astype(jnp.bfloat16)
+
+            exchange(layer, 1, part).start()
+            for index in range(4, 7):
+                save(index, saves[index][1], layer, part).start()
+
+        @pl.loop(0, layers)
+        def _(layer):
+            @pl.loop(0, micro)
+            def _(part):
+                attention_stage(layer, part)
+
+            @pl.loop(0, micro)
+            def _(part):
+                mlp_stage(layer, part)
+
+        last = layers - 1
+
+        @pl.loop(0, micro)
+        def _(part):
+            exchange(last, 1, part).wait_recv()
+
+            @pl.loop(0, tokens, step=32)
+            def _(start):
+                span = pl.ds(pl.multiple_of(start, 32), 32)
+                value = mid[last, part, span] + (joined(last, 1, part, span) + rows_ref[last, 5:6])
+                final[part, span] = value
+                final_low[part, span] = value.astype(jnp.bfloat16)
+
+        ending = [
+            pltpu.make_async_copy(final, outs[7], save_sem.at[7, 0, 0]),
+            pltpu.make_async_copy(final_low, outs[8], save_sem.at[8, 0, 0]),
+        ]
+        for copy in ending:
+            copy.start()
+
+        @pl.loop(0, layers)
+        def _(layer):
+            @pl.loop(0, micro)
+            def _(part):
+                for stage in range(2):
+                    exchange(layer, stage, part).wait_send()
+                for index, source in saves:
+                    save(index, source, layer, part).wait()
+
+        for copy in ending:
+            copy.wait()
+
+
+def saved_shapes(layers, micro, tokens, width, head_width, hidden_width):
+    low, full = jnp.bfloat16, jnp.float32
+    heads = head_width // HEAD_DIM
     return (
-        full[:, :, : ends[0]].reshape(layers, width, 3, head_width),
-        full[:, :, ends[0] : ends[1]],
-        full[:, :, ends[1] : ends[2]],
-        full[:, :, ends[2] : ends[3]],
-        small[:, :2],
-        small[:, 2:6],
-        inner,
+        ((layers, micro, tokens, width), full),
+        ((layers, micro, tokens, 3 * head_width), low),
+        ((layers, micro, tokens, heads), full),
+        ((layers, micro, tokens, head_width), low),
+        ((layers, micro, tokens, width), full),
+        ((layers, micro, tokens, hidden_width), low),
+        ((layers, micro, tokens, hidden_width), low),
+        ((micro, tokens, width), full),
+        ((micro, tokens, width), low),
     )
 
 
-def pack_grads(grads, count):
-    qkv_g, out_g, up_g, down_g, gain_g, shift_g, inner_g = grads
-    layers, width = qkv_g.shape[:2]
-    inner = jnp.swapaxes(inner_g.reshape(layers, count, 3, width // count), 1, 2).reshape(layers, 3, width)
-    small = jnp.swapaxes(jnp.concatenate([gain_g, shift_g, inner], axis=1), 1, 2)
-    small = jnp.pad(small, ((0, 0), (0, 0), (0, SMALL_COLS - small.shape[2])))
-    whole = jnp.concatenate([qkv_g.reshape(layers, width, -1), out_g, up_g, down_g, small], axis=2)
-    return whole.astype(jnp.bfloat16)
+def forward(tick, h0, ids, params, full, previous, head_width, hidden_width):
+    rows, qkv_bias, up_bias = params
+    layers, width = full.shape[:2]
+    micro, tokens = ids.shape
+    shapes = saved_shapes(layers, micro, tokens, width, head_width, hidden_width)
+    vmem = pl.BlockSpec(memory_space=pltpu.VMEM)
+    hbm = pl.BlockSpec(memory_space=pl.ANY)
+    dma = pltpu.SemaphoreType.DMA
+    low = jnp.bfloat16
+    aliased = () if previous is None else tuple(previous)
+    return pl.pallas_call(
+        functools.partial(forward_kernel, tick, previous is not None, head_width, hidden_width),
+        out_shape=[jax.ShapeDtypeStruct(shape, kind) for shape, kind in shapes],
+        in_specs=[vmem] * 6 + [hbm] * (1 + len(aliased)),
+        out_specs=[hbm] * len(shapes),
+        input_output_aliases={7 + number: number for number in range(len(aliased))},
+        scratch_shapes=[
+            pltpu.VMEM((layers, width, 3 * head_width), low),
+            pltpu.VMEM((layers, width, head_width), low),
+            pltpu.VMEM((layers, width, hidden_width), low),
+            pltpu.VMEM((layers, width, hidden_width), low),
+            *(pltpu.VMEM(shape, kind) for shape, kind in shapes),
+            pltpu.VMEM((tokens, width), low),
+            pltpu.VMEM((micro, tokens, tokens), jnp.float32),
+            pltpu.VMEM((layers, 2, micro, tokens, width), low),
+            pltpu.VMEM((layers, 2, micro, tokens, width), low),
+            dma((layers, 4)),
+            dma((len(shapes), layers, micro)),
+            dma((layers, 2, micro)),
+            dma((layers, 2, micro)),
+        ],
+        compiler_params=pltpu.CompilerParams(
+            collective_id=2 + tick, has_side_effects=True, vmem_limit_bytes=62 << 20
+        ),
+        name="forward",
+    )(h0, ids[:, :, None], ids[:, None, :], rows, qkv_bias, up_bias, full, *aliased)
+
+
+def backward_kernel(
+    tick, has_alias, head_width, hidden_width, g0_ref, ids_col_ref, ids_row_ref, rows_ref, full_ref, *refs
+):
+    saves = refs[:7]
+    refs = refs[7:]
+    out_count = 6
+    if has_alias:
+        refs = refs[out_count:]
+    d_out, small_out, qkv_bias_out, up_bias_out, g_out, low_out = refs[:out_count]
+    (
+        w_qkv, w_out, w_up, w_down, hid, qkv, lse, mixed, mid, act, slope, grad, low, hidden_grad, qkv_grad, normed,
+        mixed_grad, mask, send, recv, stage, small, qkv_bias, up_bias,
+        w_sem, load_sem, send_sem, recv_sem, stage_sem, end_sem,
+    ) = refs[out_count:]
+    held = (hid, qkv, lse, mixed, mid, act, slope)
+    layers, micro, tokens, width = hid.shape
+    section = lax.axis_index("section")
+    partner = {"tensor": 1 - lax.axis_index("tensor")}
+    tile = 256
+    scale = 1.0 / math.sqrt(HEAD_DIM)
+
+    @pl.when(section == 1 - tick)
+    def _():
+        ends = (0, 3 * head_width, 4 * head_width, 4 * head_width + hidden_width, 4 * head_width + 2 * hidden_width)
+
+        def fetch(layer, index):
+            buffer = (w_qkv, w_out, w_up, w_down)[index]
+            return pltpu.make_async_copy(
+                full_ref.at[layer, :, pl.ds(ends[index], ends[index + 1] - ends[index])], buffer, w_sem.at[index]
+            )
+
+        def load(index, layer):
+            return pltpu.make_async_copy(saves[index].at[layer], held[index].at[layer], load_sem.at[index, layer])
+
+        last = layers - 1
+        fetch(last, 3).start()
+        load(6, last).start()
+        fetch(last, 2).start()
+        for index in (5, 4):
+            load(index, last).start()
+        fetch(last, 1).start()
+        for index in (1, 2, 3, 0):
+            load(index, last).start()
+        fetch(last, 0).start()
+        for layer in range(last - 1, -1, -1):
+            for index in range(7):
+                load(index, layer).start()
+        barrier = pltpu.get_barrier_semaphore()
+        pl.semaphore_signal(barrier, inc=1, device_id=partner, device_id_type=MESH)
+        pl.semaphore_wait(barrier, 1)
+
+        small[...] = jnp.zeros_like(small)
+        qkv_bias[...] = jnp.zeros_like(qkv_bias)
+        up_bias[...] = jnp.zeros_like(up_bias)
+        for part in range(micro):
+            col = ids_col_ref[part]
+            row = ids_row_ref[part]
+            one = lax.broadcasted_iota(jnp.int32, (tokens, tokens), 0)
+            two = lax.broadcasted_iota(jnp.int32, (tokens, tokens), 1)
+            allowed = ((col == row) & (col >= 0)) | (one == two)
+            mask[part] = jnp.where(allowed, 0.0, -1e30)
+            grad[part] = g0_ref[part].astype(jnp.float32)
+
+        def exchange(layer, step, part):
+            return pltpu.make_async_remote_copy(
+                src_ref=send.at[layer, step, part],
+                dst_ref=recv.at[layer, step, part],
+                send_sem=send_sem.at[layer, step, part],
+                recv_sem=recv_sem.at[layer, step, part],
+                device_id=partner,
+                device_id_type=MESH,
+            )
+
+        def rows_of(part):
+            return pl.ds(pl.multiple_of(part * tokens, tokens), tokens)
+
+        def column_sum(value):
+            return jnp.sum(value.astype(jnp.float32), axis=0, keepdims=True)
+
+        def norm_parts(value):
+            average = jnp.mean(value, axis=-1, keepdims=True)
+            centred = value - average
+            spread = jnp.mean(centred * centred, axis=-1, keepdims=True)
+            inverse = lax.rsqrt(spread + EPSILON)
+            return centred * inverse, inverse
+
+        def norm_back(layer, step, part, source, gain_row, shift_row):
+            gain = rows_ref[layer, gain_row : gain_row + 1]
+
+            @pl.loop(0, tokens, step=32)
+            def _(start):
+                span = pl.ds(pl.multiple_of(start, 32), 32)
+                outer = send[layer, step, part, span].astype(jnp.float32) + recv[layer, step, part, span].astype(jnp.float32)
+                unit, inverse = norm_parts(source[layer, part, span])
+                inner = outer * gain
+                first = jnp.mean(inner, axis=-1, keepdims=True)
+                second = jnp.mean(inner * unit, axis=-1, keepdims=True)
+                small[layer, gain_row : gain_row + 1] += column_sum(outer * unit)
+                small[layer, shift_row : shift_row + 1] += column_sum(outer)
+                grad[part, span] = grad[part, span] + inverse * (inner - first - unit * second)
+
+        def renorm(layer, part, source, gain_row, shift_row):
+            @pl.loop(0, tokens, step=32)
+            def _(start):
+                span = pl.ds(pl.multiple_of(start, 32), 32)
+                unit, _ = norm_parts(source[layer, part, span])
+                value = unit * rows_ref[layer, gain_row : gain_row + 1] + rows_ref[layer, shift_row : shift_row + 1]
+                normed[pl.ds(pl.multiple_of(part * tokens + start, 32), 32)] = value.astype(jnp.bfloat16)
+
+        def round_grad(layer, part, bias_row):
+            @pl.loop(0, tokens, step=32)
+            def _(start):
+                span = pl.ds(pl.multiple_of(start, 32), 32)
+                value = grad[part, span].astype(jnp.bfloat16)
+                low[pl.ds(pl.multiple_of(part * tokens + start, 32), 32)] = value
+                small[layer, bias_row : bias_row + 1] += column_sum(value)
+
+        def put(layer, number, group):
+            start = (2 * head_width + 2 * head_width, 4 * head_width + hidden_width, 0)[group]
+            return pltpu.make_async_copy(
+                stage.at[number],
+                d_out.at[layer, pl.ds(pl.multiple_of(number * tile, tile), tile), pl.ds(start, stage.shape[2])],
+                stage_sem.at[number],
+            )
+
+        def mlp_stage(layer, part):
+            round_grad(layer, part, 5)
+
+            @pl.when(part == 0)
+            def _():
+                fetch(layer, 3).wait()
+                load(6, layer).wait()
+
+            @pl.loop(0, hidden_width, step=tile)
+            def _(start):
+                span = pl.ds(pl.multiple_of(start, tile), tile)
+                value = jnp.dot(low[rows_of(part)], w_down[:, span], preferred_element_type=jnp.float32)
+                value = (value * slope[layer, part, :, span].astype(jnp.float32)).astype(jnp.bfloat16)
+                hidden_grad[rows_of(part), span] = value
+                up_bias[layer, :, span] += column_sum(value)
+
+            @pl.when(part == 0)
+            def _():
+                fetch(layer, 2).wait()
+
+            @pl.loop(0, width, step=tile)
+            def _(start):
+                span = pl.ds(pl.multiple_of(start, tile), tile)
+                value = contract_last(hidden_grad[rows_of(part)], w_up[span])
+                send[layer, 0, part, :, span] = value.astype(jnp.bfloat16)
+
+            exchange(layer, 0, part).start()
+
+        def weight_tiles(layer, group, free, fill):
+            @pl.loop(0, width // tile)
+            def _(number):
+                pl.when(free)(lambda: put(layer, number, group).wait())
+                fill(number, pl.ds(pl.multiple_of(number * tile, tile), tile))
+                put(layer, number, group).start()
+
+        def attention_stage(layer, part):
+            exchange(layer, 0, part).wait_recv()
+            norm_back(layer, 0, part, mid, 1, 4)
+            round_grad(layer, part, 3)
+
+            @pl.when(part == 0)
+            def _():
+                fetch(layer, 1).wait()
+                load(1, layer).wait()
+                load(2, layer).wait()
+
+            @pl.loop(0, head_width, step=tile)
+            def _(start):
+                span = pl.ds(pl.multiple_of(start, tile), tile)
+                value = jnp.dot(low[rows_of(part)], w_out[:, span], preferred_element_type=jnp.float32)
+                mixed_grad[:, span] = value.astype(jnp.bfloat16)
+
+            lane = lax.broadcasted_iota(jnp.int32, (tokens, LANES), 1)
+            for pair in range(head_width // LANES):
+                spans = [pl.ds(piece * head_width + pair * LANES, LANES) for piece in range(3)]
+                q2, k2, v2 = (qkv[layer, part, :, span] for span in spans)
+                go2 = mixed_grad[:, pair * LANES : (pair + 1) * LANES]
+                halves = []
+                for side in range(2):
+                    live = (lane < HEAD_DIM) if side == 0 else (lane >= HEAD_DIM)
+                    head = 2 * pair + side
+                    scores = contract_last(jnp.where(live, q2, jnp.zeros_like(q2)), k2) + mask[part]
+                    probs = jnp.exp(scores - lse[layer, part, :, head : head + 1])
+                    outer = contract_last(jnp.where(live, go2, jnp.zeros_like(go2)), v2)
+                    centre = jnp.sum(probs * outer, axis=-1, keepdims=True)
+                    inner = (probs * (outer - centre)).astype(jnp.bfloat16)
+                    halves.append((
+                        jnp.dot(inner, k2, preferred_element_type=jnp.float32) * scale,
+                        contract_rows(inner, q2),
+                        contract_rows(probs.astype(jnp.bfloat16), go2),
+                    ))
+                for piece in range(3):
+                    value = jnp.where(lane < HEAD_DIM, halves[0][piece], halves[1][piece]).astype(jnp.bfloat16)
+                    qkv_grad[rows_of(part), spans[piece]] = value
+                    qkv_bias[layer, :, spans[piece]] += column_sum(value)
+
+            @pl.when(part == 0)
+            def _():
+                fetch(layer, 0).wait()
+
+            @pl.loop(0, width, step=tile)
+            def _(start):
+                span = pl.ds(pl.multiple_of(start, tile), tile)
+                value = contract_last(qkv_grad[rows_of(part)], w_qkv[span])
+                send[layer, 1, part, :, span] = value.astype(jnp.bfloat16)
+
+            exchange(layer, 1, part).start()
+
+        @pl.loop(0, layers)
+        def _(turn):
+            layer = layers - 1 - turn
+
+            @pl.loop(0, micro)
+            def _(part):
+                mlp_stage(layer, part)
+
+            @pl.when(layer > 0)
+            def _():
+                fetch(layer - 1, 3).start()
+                fetch(layer - 1, 2).start()
+
+            load(5, layer).wait()
+
+            def fill_down(number, span):
+                both = act[layer].reshape(micro * tokens, hidden_width)
+                stage[number] = contract_rows(low[:, span], both).astype(jnp.bfloat16)
+
+            weight_tiles(layer, 1, turn > 0, fill_down)
+            load(4, layer).wait()
+
+            @pl.loop(0, micro)
+            def _(part):
+                renorm(layer, part, mid, 1, 4)
+
+            def fill_up(number, span):
+                stage[number] = contract_rows(normed[:, span], hidden_grad[...]).astype(jnp.bfloat16)
+
+            weight_tiles(layer, 0, turn >= 0, fill_up)
+
+            @pl.loop(0, micro)
+            def _(part):
+                attention_stage(layer, part)
+
+            @pl.when(layer > 0)
+            def _():
+                fetch(layer - 1, 1).start()
+                fetch(layer - 1, 0).start()
+
+            load(3, layer).wait()
+            load(0, layer).wait()
+
+            @pl.loop(0, micro)
+            def _(part):
+                renorm(layer, part, hid, 0, 2)
+
+            def fill_attention(number, span):
+                both = mixed[layer].reshape(micro * tokens, head_width)
+                stage[number, :, : 3 * head_width] = contract_rows(normed[:, span], qkv_grad[...]).astype(jnp.bfloat16)
+                stage[number, :, 3 * head_width :] = contract_rows(low[:, span], both).astype(jnp.bfloat16)
+
+            weight_tiles(layer, 2, turn >= 0, fill_attention)
+
+            @pl.loop(0, micro)
+            def _(part):
+                exchange(layer, 1, part).wait_recv()
+                norm_back(layer, 1, part, hid, 0, 2)
+
+        for part in range(micro):
+            low[pl.ds(part * tokens, tokens)] = grad[part].astype(jnp.bfloat16)
+        ending = [
+            pltpu.make_async_copy(small, small_out, end_sem.at[0]),
+            pltpu.make_async_copy(qkv_bias, qkv_bias_out, end_sem.at[1]),
+            pltpu.make_async_copy(up_bias, up_bias_out, end_sem.at[2]),
+            pltpu.make_async_copy(grad, g_out, end_sem.at[3]),
+            pltpu.make_async_copy(low, low_out, end_sem.at[4]),
+        ]
+        for copy in ending:
+            copy.start()
+        for number in range(width // tile):
+            put(0, number, 2).wait()
+
+        @pl.loop(0, layers)
+        def _(layer):
+            @pl.loop(0, micro)
+            def _(part):
+                for step in range(2):
+                    exchange(layer, step, part).wait_send()
+
+        for copy in ending:
+            copy.wait()
+
+
+def backward(tick, g0, ids, params, full, saves, previous, head_width, hidden_width):
+    rows, qkv_bias, up_bias = params
+    layers, width, cols = full.shape
+    micro, tokens = ids.shape
+    shapes = saved_shapes(layers, micro, tokens, width, head_width, hidden_width)
+    vmem = pl.BlockSpec(memory_space=pltpu.VMEM)
+    hbm = pl.BlockSpec(memory_space=pl.ANY)
+    dma = pltpu.SemaphoreType.DMA
+    low, wide = jnp.bfloat16, jnp.float32
+    outs = (
+        ((layers, width, cols), low),
+        ((layers, 8, width), wide),
+        ((layers, 1, 3 * head_width), wide),
+        ((layers, 1, hidden_width), wide),
+        ((micro, tokens, width), wide),
+        ((micro * tokens, width), low),
+    )
+    aliased = () if previous is None else tuple(previous)
+    return pl.pallas_call(
+        functools.partial(backward_kernel, tick, previous is not None, head_width, hidden_width),
+        out_shape=[jax.ShapeDtypeStruct(shape, kind) for shape, kind in outs],
+        in_specs=[vmem] * 4 + [hbm] * (8 + len(aliased)),
+        out_specs=[hbm] * len(outs),
+        input_output_aliases={12 + number: number for number in range(len(aliased))},
+        scratch_shapes=[
+            pltpu.VMEM((width, 3 * head_width), low),
+            pltpu.VMEM((width, head_width), low),
+            pltpu.VMEM((width, hidden_width), low),
+            pltpu.VMEM((width, hidden_width), low),
+            *(pltpu.VMEM(shape, kind) for shape, kind in shapes[:7]),
+            pltpu.VMEM((micro, tokens, width), wide),
+            pltpu.VMEM((micro * tokens, width), low),
+            pltpu.VMEM((micro * tokens, hidden_width), low),
+            pltpu.VMEM((micro * tokens, 3 * head_width), low),
+            pltpu.VMEM((micro * tokens, width), low),
+            pltpu.VMEM((tokens, head_width), low),
+            pltpu.VMEM((micro, tokens, tokens), wide),
+            pltpu.VMEM((layers, 2, micro, tokens, width), low),
+            pltpu.VMEM((layers, 2, micro, tokens, width), low),
+            pltpu.VMEM((width // 256, 256, 4 * head_width), low),
+            pltpu.VMEM((layers, 8, width), wide),
+            pltpu.VMEM((layers, 1, 3 * head_width), wide),
+            pltpu.VMEM((layers, 1, hidden_width), wide),
+            dma((4,)),
+            dma((7, layers)),
+            dma((layers, 2, micro)),
+            dma((layers, 2, micro)),
+            dma((width // 256,)),
+            dma((5,)),
+        ],
+        compiler_params=pltpu.CompilerParams(
+            collective_id=4 + tick, has_side_effects=True, vmem_limit_bytes=62 << 20
+        ),
+        name="backward",
+    )(g0, ids[:, :, None], ids[:, None, :], rows, full, *saves, *aliased)
+
+
+def pack_small(small, qkv_bias, up_bias, head_width, count):
+    layers, _, width = small.shape
+    inner = jnp.concatenate(
+        [qkv_bias[:, 0, :head_width], qkv_bias[:, 0, 2 * head_width :], up_bias[:, 0]], axis=1
+    )
+    inner = jnp.swapaxes(inner.reshape(layers, count, 3, width // count), 1, 2).reshape(layers, 3, width)
+    columns = jnp.swapaxes(jnp.concatenate([small[:, :6], inner], axis=1), 1, 2)
+    return jnp.pad(columns, ((0, 0), (0, 0), (0, SMALL_COLS - columns.shape[2]))).astype(jnp.bfloat16)
 
 
 def unpack_grads(full, head_width, hidden_width):
@@ -650,73 +1117,23 @@
     cotangent,
 ):
     section = lax.axis_index("section")
-    micro_count = block_input.shape[0]
-    layer_count = qkv_weight.shape[0]
-    ticks = micro_count + 1
-    shard = pack_shard(
-        qkv_weight, out_weight, up_weight, down_weight, norm_gains, biases, inner_bias
-    )
-    gathered = unpack(gather_weights(shard), out_weight.shape[2], up_weight.shape[2], lax.axis_size("fsdp"))
-    stored = []
-    outputs = []
-    received = jnp.zeros(block_input.shape[1:], jnp.bfloat16)
-    for tick_index in range(ticks):
-        micro_index = jnp.clip(tick_index - section, 0, micro_count - 1)
-        ids_batch = lax.dynamic_index_in_dim(image_ids, micro_index, 0, keepdims=False)
-        fresh = block_input[min(tick_index, micro_count - 1)]
-        hidden = jnp.where(section == 0, fresh, received).astype(jnp.float32)
-        kept_layers = []
-        for layer_index in range(layer_count):
-            hidden, kept = layer_forward(hidden, layer_slice(gathered, layer_index), ids_batch)
-            kept_layers.append(kept)
-        stored.append((ids_batch, kept_layers))
-        outputs.append(hidden)
-        if tick_index + 1 < ticks:
-            received = shifted(hidden.astype(jnp.bfloat16), "section", 1)
-    accumulated = None
-    grad_inputs = []
-    received = jnp.zeros(block_input.shape[1:], jnp.bfloat16)
-    for tick_index in range(ticks):
-        micro_index = micro_count - tick_index - section
-        is_valid = (micro_index >= 0) & (micro_index < micro_count)
-        fresh = cotangent[max(micro_count - 1 - tick_index, 0)]
-        grad_out = jnp.where(section == 1, fresh, received).astype(jnp.float32)
-        grad_out = jnp.where(is_valid, grad_out, jnp.zeros_like(grad_out))
-        ids_batch, kept_layers = stored[micro_count - tick_index]
-        per_layer = [None] * layer_count
-        for layer_index in reversed(range(layer_count)):
-            grad_out, per_layer[layer_index] = layer_backward(
-                grad_out, kept_layers[layer_index], layer_slice(gathered, layer_index), ids_batch
-            )
-        tick_grads = tuple(
-            (
-                jnp.stack([per_layer[which_layer][member] for which_layer in range(layer_count)])
-                for member in range(7)
-            )
-        )
-        grad_inputs.append(grad_out)
-        if tick_index + 1 < ticks:
-            received = shifted(grad_out.astype(jnp.bfloat16), "section", -1)
-        if accumulated is None:
-            accumulated = tuple(tick_grads)
-        else:
-            accumulated = jax.tree.map(jnp.add, tuple(accumulated), tuple(tick_grads))
-    accumulated = unpack_grads(
-        scatter_grads(pack_grads(accumulated, lax.axis_size("fsdp"))), out_weight.shape[2], up_weight.shape[2]
-    )
-    block_outputs = jnp.stack([outputs[micro + 1] for micro in range(micro_count)])
-    input_grads = jnp.stack([grad_inputs[micro_count - micro] for micro in range(micro_count)])
-    section_ends = jnp.where(section == 0, input_grads, block_outputs)[None]
-    return (
-        section_ends,
-        accumulated[0],
-        accumulated[1],
-        accumulated[2],
-        accumulated[3],
-        accumulated[4],
-        accumulated[5],
-        accumulated[6],
-    )
+    count = lax.axis_size("fsdp")
+    head_width, hidden_width = out_weight.shape[2], up_weight.shape[2]
+    shard = pack_shard(qkv_weight, out_weight, up_weight, down_weight, norm_gains, biases, inner_bias)
+    full = gather_weights(shard)
+    params = unpack_params(full, head_width, count)
+    saved = forward(0, block_input, image_ids, params, full, None, head_width, hidden_width)
+    received = shifted(saved[8], "section", 1)
+    saved = forward(1, received, image_ids, params, full, saved, head_width, hidden_width)
+    grads = backward(0, cotangent, image_ids, params, full, saved[:7], None, head_width, hidden_width)
+    received = shifted(grads[5], "section", -1).reshape(cotangent.shape)
+    grads = backward(1, received, image_ids, params, full, saved[:7], grads, head_width, hidden_width)
+    partial, small, qkv_bias, up_bias, input_grad, _ = grads
+    columns = pack_small(small, qkv_bias, up_bias, head_width, count)
+    partial = lax.dynamic_update_slice(partial, columns, (0, 0, partial.shape[2] - SMALL_COLS))
+    summed = unpack_grads(scatter_grads(partial), head_width, hidden_width)
+    section_ends = jnp.where(section == 0, input_grad, saved[7])[None]
+    return (section_ends, *summed)
 
 
 def solution(mesh):

time: 1650 us -> 740 us (0.45)
  waiting for transfers between devices: 628 us -> 160 us
  matrix products: 312 us -> 0 us
  other arithmetic: 154 us -> 4.05 us
  local copies, waits for them, and re-layouts: 107 us -> 31.3 us
  Pallas kernels: 406 us -> 472 us
  starting transfers between devices: 11.7 us -> 71.6 us
  between operations: 18.1 us -> 0.95 us
    psum x23 -> x0, waiting for transfers between devices: 626 us -> none  [the longest x11 422 us: mix_sum(): lax.psum(partial_sum.astype(jnp.bfloat16), 'tensor').astype(jnp.float32)]
    dot_general x108 -> x0, matrix products: 312 us -> none  [the longest x24 99.3 us: contract_rows(): lax.dot_general(left, right, (((0,), (0,)), ((), ())), preferred_element_...]
    pallas_call x0 -> x4, Pallas kernels: none -> 166 us  [the longest x2 98 us: backward(): pl.pallas_call(functools.partial(backward_kernel, tick, previous is not N...]
    ppermute x4 -> x2, waiting for transfers between devices: 2.01 us -> 160 us  [shifted(): lax.ppermute(value, axis, [(source, source + steps) for source in range(i...]
    pallas_call x1, Pallas kernels: 267 us -> 167 us  [scatter_grads(): pl.pallas_call(functools.partial(scatter_kernel, line), out_shape=jax.Sha...]
    reduce_sum x65 -> x0, other arithmetic: 70.5 us -> none  [the longest x21 35.1 us: layer_norm(): return centred * lax.rsqrt(spread + EPSILON) * weight_gain + weight_shift]
    ppermute x4 -> x2, starting transfers between devices: 6.71 us -> 71.6 us  [shifted(): lax.ppermute(value, axis, [(source, source + steps) for source in range(i...]
    unnamed x6 -> x0, other arithmetic: 57 us -> none
  transfers between devices with their start and end apart: 27 -> 2, of which waited for: 24 -> 2; matrix products, arithmetic and copies ran while one was open for 10% -> 0% of each run, Pallas kernels for 0% -> 0%
where the time goes in v2:
time: 740 us
  Pallas kernels  472 us (64%)
  waiting for transfers between devices  160 us (22%)
  starting transfers between devices  71.6 us (10%)
  local copies, waits for them, and re-layouts  31.3 us (4%)
    pallas_call x1, Pallas kernels, scatter_grads(): pl.pallas_call(functools.partial(scatter_kernel, line), out_shape=jax.Sha...  167 us
    ppermute x2, waiting for transfers between devices, shifted(): lax.ppermute(value, axis, [(source, source + steps) for source in range(i...  160 us
    pallas_call x1, Pallas kernels, gather_weights(): pl.pallas_call(functools.partial(gather_kernel, line), out_shape=jax.Shap...  140 us
    pallas_call x2, Pallas kernels, backward(): pl.pallas_call(functools.partial(backward_kernel, tick, previous is not N...  98 us
    ppermute x2, starting transfers between devices, shifted(): lax.ppermute(value, axis, [(source, source + steps) for source in range(i...  71.6 us
    pallas_call x2, Pallas kernels, forward(): pl.pallas_call(functools.partial(forward_kernel, tick, previous is not No...  67.7 us
  transfers between devices with their start and end apart: 2, of which 2 were waited for; matrix products, arithmetic and copies ran while one was open for 0% of the time, Pallas kernels for 0%

profile of v2, /device:TPU:0, one launch (start us, length us, event | category | flops | bytes accessed | tf_op | source)
XLA Modules:
  0.0 739.6 jit_solution(12203585081291296564)
XLA Ops:
  0.7 1.5 copy.139
  2.2 1.2 copy.143
  3.4 1.2 constant_dynamic-update-slice_fusion.3
  4.8 0.8 copy.140
  5.5 0.8 copy.141
  6.3 1.4 constant_dynamic-update-slice_fusion.1
  8.1 1.6 copy-done.2
  9.7 139.7 %gather_weights.1.full_ref = bf16[2,1024,6272]{2,1,0:T(8,128)(2,1)} custom-call(bf16[2,128,6272]{2,1,0:T(8,128)(2,1)} %copy-done.2), custom_call_target="tpu_custom_call" | custom-call | tf_op jit(solution)/shard_map/gather_weights/pallas_call | solution.py:171
  149.4 1.1 slice.45
  152.7 0.8 copy.152.ids_col_ref
  154.2 65.8 %forward.2 = (f32[2,2,224,1024]{3,2,1,0:T(8,128)}, bf16[2,2,224,1536]{3,2,1,0:T(8,128)(2,1)}, f32[2,2,224,8]{3,2,1,0:T(8,128)}, bf16[2,2,224,512]{3,2,1,0:T(8,12...) custom-call(bf16[2,224,1024]{2,1,0:T(8,128)(2,1)} %h0_ref.1, ...), custom_call_target="tpu_custom_call" | custom-call | tf_op jit(solution)/shard_map/forward/pallas_call | solution.py:700
  220.0 70.3 %collective-permute-start = (bf16[2,224,1024]{2,1,0:T(8,128)(2,1)}, bf16[2,224,1024]{2,1,0:T(8,128)(2,1)S(1)}, u32[]{:S(2)}, u32[]{:S(2)}) collective-permute-start(bf16[2,224,1024]{2,1,0:T(8,128)(2,1)} %get-tuple-element.36.refs_8_), channel_id=1, source_target_pairs={{0,16},{1,17},{2,18},{3,19},{4,20},{5,21},{6,22},{7,23},{8,24},{9,... | collective-permute-start | bytes 2752520 | tf_op jit(solution)/shard_map/ppermute | solution.py:430
  290.3 2.2 collective-permute-done.h0_ref
  292.5 0.9 copy-done.5
  293.5 1.9 forward.3
  295.4 1.7 backward.2
  297.1 1.3 collective-permute-start.1
  298.4 157.3 %collective-permute-done.1 = bf16[448,1024]{1,0:T(8,128)(2,1)S(1)} collective-permute-done((bf16[448,1024]{1,0:T(8,128)(2,1)}, bf16[448,1024]{1,0:T(8,128)(2,1)S(1)}, u32[]{:S(2)}, u32[]{:S(2)}) %collective-permute-start.1) | collective-permute-done | bytes 917536 | tf_op jit(solution)/shard_map/ppermute | solution.py:430
  455.8 0.9 copy-done.4
  456.7 96.3 %backward.3 = (bf16[2,1024,6272]{2,1,0:T(8,128)(2,1)}, f32[2,8,1024]{2,1,0:T(8,128)}, f32[2,1,1536]{2,1,0:T(1,128)}, f32[2,1,2048]{2,1,0:T(1,128)}, f32[2,224,1024]{2,1,0:T(8,128)}, /*index=5*/bf16[448,1024]{1,0:T(8,128)(2,1)}) custom-call(bf16[2,224,1024]{2,1,0:T(8,128)(2,1)} %bitcast.32, ...), custom_call_target="tpu_custom_call", output_to_operand_aliasing={{0}: (12, {}), {1}: (13, {}), {2}: (14, {}), {3}: (15, {}),... | custom-call | tf_op jit(solution)/shard_map/backward/pallas_call | solution.py:1043
  553.0 0.7 convert.25
  553.7 0.7 convert.26
  554.8 0.9 slice.69
  556.3 1.0 pad_dynamic-update-slice_fusion.d_ref
  557.3 166.7 %scatter_grads.1 = f32[2,128,6272]{2,1,0:T(8,128)} custom-call(bf16[2,1024,6272]{2,1,0:T(8,128)(2,1)} %pad_dynamic-update-slice_fusion.d_ref), custom_call_target="tpu_custom_call" | custom-call | tf_op jit(solution)/shard_map/scatter_grads/pallas_call | solution.py:376
  724.0 5.0 fusion
  729.0 0.9 slice.52
  729.8 0.7 slice.66
  730.6 0.8 slice.65
  731.4 1.6 copy.157
  733.0 3.1 copy.159
  738.1 1.6 select_bitcast_fusion
  (61 shorter events, 6.3 us)
Async XLA Ops:
  0.6 3.9 copy-start.13
  0.6 4.1 copy-start.14
  0.7 4.9 copy-start.12
  0.7 5.6 copy-start.8
  6.3 1.5 copy-start.3
  6.3 1.6 copy-start.9
  6.3 1.6 copy-start.10
  8.1 1.6 copy-start.2
  9.7 142.4 %copy-start.11 = (s32[2,224]{1,0:T(2,128)S(1)}, s32[2,224]{1,0:T(2,128)}, u32[]{:S(2)}) copy-start(s32[2,224]{1,0:T(2,128)} %param.11) | copy-start | bytes 5380
  220.0 72.5 %collective-permute-start = (bf16[2,224,1024]{2,1,0:T(8,128)(2,1)}, bf16[2,224,1024]{2,1,0:T(8,128)(2,1)S(1)}, u32[]{:S(2)}, u32[]{:S(2)}) collective-permute-start(bf16[2,224,1024]{2,1,0:T(8,128)(2,1)} %get-tuple-element.36.refs_8_), channel_id=1, source_target_pairs={{0,16},{1,17},{2,18},{3,19},{4,20},{5,21},{6,22},{7,23},{8,24},{9,... | collective-permute-start | bytes 2752520 | tf_op jit(solution)/shard_map/ppermute | solution.py:430
  292.5 0.9 copy-start.5
  297.1 158.6 %collective-permute-start.1 = (bf16[448,1024]{1,0:T(8,128)(2,1)}, bf16[448,1024]{1,0:T(8,128)(2,1)S(1)}, u32[]{:S(2)}, u32[]{:S(2)}) collective-permute-start(bf16[448,1024]{1,0:T(8,128)(2,1)} %get-tuple-element.52.refs_12_), channel_id=1, source_target_pairs={{16,0},{17,1},{18,2},{19,3},{20,4},{21,5},{22,6},{23,7},{24,8},{25... | collective-permute-start | bytes 2752520 | tf_op jit(solution)/shard_map/ppermute | solution.py:430
  455.7 0.9 copy-start.4
  723.9 5.0 copy-start
  724.0 7.4 %slice-start = ((f32[2,128,6272]{2,1,0:T(8,128)}), f32[2,128,1536]{2,1,0:T(8,128)S(1)}, s32[]{:S(2)}) async-start(f32[2,128,6272]{2,1,0:T(8,128)} %scatter_grads.1), calls=%async_computation | async-start | bytes 3145728 | tf_op jit(solution)/shard_map/slice | solution.py:1097
  731.4 6.7 copy-start.1
  733.0 3.1 copy-start.7
  733.0 3.8 copy-start.6

commit v3 on v2

--- a/solution.py
+++ b/solution.py
@@ -192,221 +192,6 @@
         compiler_params=pltpu.CompilerParams(collective_id=0, has_side_effects=True),
         name="gather_weights",
     )(shard)
-
-
-def add_into(target, source):
-    rows = target.shape[0]
-
-    @pl.loop(0, rows, step=16)
-    def _(start):
-        span = pl.ds(pl.multiple_of(start, 16), 16)
-        target[span] = target[span] + source[span]
-
-
-def scatter_kernel(
-    line, d_ref, out_ref,
-    sa, xa, ua, da, sb, ub, db, xb,
-    load_a, load_b, sxa, rxa, sua, rua, sda, rda, sub, rub, sdb, rdb, sxb, rxb,
-):
-    layers, all_rows, cols = d_ref.shape
-    shard_rows = all_rows // (2 * line)
-    cols_a = cols - X_FIRST_COLS
-    place = lax.axis_index("fsdp")
-    z = place // 2
-    x = lax.rem(place, 2)
-    has_up = z < line - 1
-    has_down = z > 0
-    to_x = {"fsdp": z * 2 + 1 - x}
-    to_up = {"fsdp": jnp.minimum(z + 1, line - 1) * 2 + x}
-    to_down = {"fsdp": jnp.maximum(z - 1, 0) * 2 + x}
-
-    barrier = pltpu.get_barrier_semaphore()
-    pl.semaphore_signal(barrier, inc=1, device_id=to_x, device_id_type=MESH)
-
-    @pl.when(has_up)
-    def _():
-        pl.semaphore_signal(barrier, inc=1, device_id=to_up, device_id_type=MESH)
-
-    @pl.when(has_down)
-    def _():
-        pl.semaphore_signal(barrier, inc=1, device_id=to_down, device_id_type=MESH)
-
-    pl.semaphore_wait(barrier, 1 + jnp.where(has_up, 1, 0) + jnp.where(has_down, 1, 0))
-
-    span_a = pl.ds(0, cols_a)
-    span_b = pl.ds(cols_a, X_FIRST_COLS)
-
-    def part(layer, row_z, row_x, span):
-        start = pl.multiple_of((row_z * 2 + row_x) * shard_rows, shard_rows)
-        return d_ref.at[layer, pl.ds(start, shard_rows), span]
-
-    def remote(source, target_ref, send_sem, recv_sem, target):
-        return pltpu.make_async_remote_copy(
-            src_ref=source, dst_ref=target_ref, send_sem=send_sem, recv_sem=recv_sem,
-            device_id=target, device_id_type=MESH,
-        )
-
-    finish = []
-
-    def launch(copy, condition=None):
-        if condition is None:
-            copy.start()
-            finish.append((copy, None))
-        else:
-            pl.when(condition)(copy.start)
-            finish.append((copy, condition))
-
-    def arrived(buffer, sem):
-        remote(buffer, buffer, sem, sem, to_x).wait_recv()
-
-    loads = {}
-    order = []
-    for reach in range(line - 1, 0, -1):
-        order.append((reach, 1, z + reach < line, jnp.minimum(z + reach, line - 1)))
-        order.append((reach, 0, z - reach >= 0, jnp.maximum(z - reach, 0)))
-    order.append((0, 0, None, z))
-    for number, (reach, upward, live, row) in enumerate(order):
-        for layer in range(layers):
-            copy = pltpu.make_async_copy(part(layer, row, x, span_a), sa.at[layer, row], load_a.at[layer, number])
-            both = pltpu.make_async_copy(
-                d_ref.at[layer, pl.ds(pl.multiple_of(row * 2 * shard_rows, 2 * shard_rows), 2 * shard_rows), span_b],
-                sb.at[layer, row],
-                load_b.at[layer, number],
-            )
-            for local in (copy, both):
-                if live is None:
-                    local.start()
-                else:
-                    pl.when(live)(local.start)
-            loads[number, layer] = (copy, both)
-            launch(
-                remote(part(layer, row, 1 - x, span_a), xa.at[layer, row], sxa.at[layer, number], rxa.at[layer, number], to_x),
-                live,
-            )
-    for number, (reach, upward, live, row) in enumerate(order):
-        for layer in range(layers):
-            copy, both = loads[number, layer]
-            if reach:
-                wide, narrow = (ub, ua) if upward else (db, da)
-                s_a, r_a, s_b, r_b = (sua, rua, sub, rub) if upward else (sda, rda, sdb, rdb)
-                target = to_up if upward else to_down
-                fed = (z > 0) if upward else (z < line - 1)
-                slot = reach - 1
-
-                def step(copy=copy, both=both, layer=layer, row=row, number=number, wide=wide, narrow=narrow,
-                         r_a=r_a, r_b=r_b, fed=fed, slot=slot, reach=reach):
-                    both.wait()
-                    if reach < line - 1:
-
-                        @pl.when(fed)
-                        def _():
-                            arrived(wide.at[layer, slot + 1], r_b.at[layer, slot + 1])
-                            add_into(sb.at[layer, row], wide.at[layer, slot + 1])
-
-                def step_a(copy=copy, layer=layer, row=row, number=number, narrow=narrow, r_a=r_a, fed=fed, slot=slot, reach=reach):
-                    copy.wait()
-                    arrived(xa.at[layer, row], rxa.at[layer, number])
-                    add_into(sa.at[layer, row], xa.at[layer, row])
-                    if reach < line - 1:
-
-                        @pl.when(fed)
-                        def _():
-                            arrived(narrow.at[layer, slot + 1], r_a.at[layer, slot + 1])
-                            add_into(sa.at[layer, row], narrow.at[layer, slot + 1])
-
-                pl.when(live)(step)
-                launch(remote(sb.at[layer, row], wide.at[layer, slot], s_b.at[layer, slot], r_b.at[layer, slot], target), live)
-                pl.when(live)(step_a)
-                launch(remote(sa.at[layer, row], narrow.at[layer, slot], s_a.at[layer, slot], r_a.at[layer, slot], target), live)
-            else:
-                both.wait()
-
-                @pl.when(has_down)
-                def _(layer=layer):
-                    arrived(ub.at[layer, 0], rub.at[layer, 0])
-                    add_into(sb.at[layer, z], ub.at[layer, 0])
-
-                @pl.when(has_up)
-                def _(layer=layer):
-                    arrived(db.at[layer, 0], rdb.at[layer, 0])
-                    add_into(sb.at[layer, z], db.at[layer, 0])
-
-                theirs = pl.ds(pl.multiple_of((1 - x) * shard_rows, shard_rows), shard_rows)
-                launch(remote(sb.at[layer, z, theirs], xb.at[layer], sxb.at[layer], rxb.at[layer], to_x))
-                copy.wait()
-                arrived(xa.at[layer, z], rxa.at[layer, number])
-                add_into(sa.at[layer, z], xa.at[layer, z])
-
-                @pl.when(has_down)
-                def _(layer=layer):
-                    arrived(ua.at[layer, 0], rua.at[layer, 0])
-                    add_into(sa.at[layer, z], ua.at[layer, 0])
-
-                @pl.when(has_up)
-                def _(layer=layer):
-                    arrived(da.at[layer, 0], rda.at[layer, 0])
-                    add_into(sa.at[layer, z], da.at[layer, 0])
-
-    for layer in range(layers):
-        arrived(xb.at[layer], rxb.at[layer])
-
-        @pl.loop(0, shard_rows, step=16)
-        def _(start, layer=layer):
-            span = pl.ds(pl.multiple_of(start, 16), 16)
-            mine = pl.ds(pl.multiple_of(x * shard_rows + start, 16), 16)
-            out_ref[layer, span, span_a] = sa[layer, z, span].astype(jnp.float32)
-            out_ref[layer, span, span_b] = sb[layer, z, mine].astype(jnp.float32) + xb[layer, span].astype(jnp.float32)
-
-    for copy, condition in finish:
-        if condition is None:
-            copy.wait_send()
-        else:
-            pl.when(condition)(copy.wait_send)
-
-
-def scatter_grads(partial):
-    layers, all_rows, cols = partial.shape
-    count = lax.axis_size("fsdp")
-    line = count // 2
-    shard_rows = all_rows // count
-    cols_a = cols - X_FIRST_COLS
-    dma = pltpu.SemaphoreType.DMA
-    low = partial.dtype
-    slots = 2 * line - 1
-    return pl.pallas_call(
-        functools.partial(scatter_kernel, line),
-        out_shape=jax.ShapeDtypeStruct((layers, shard_rows, cols), jnp.float32),
-        in_specs=[pl.BlockSpec(memory_space=pl.ANY)],
-        out_specs=pl.BlockSpec(memory_space=pltpu.VMEM),
-        scratch_shapes=[
-            pltpu.VMEM((layers, line, shard_rows, cols_a), low),
-            pltpu.VMEM((layers, line, shard_rows, cols_a), low),
-            pltpu.VMEM((layers, line - 1, shard_rows, cols_a), low),
-            pltpu.VMEM((layers, line - 1, shard_rows, cols_a), low),
-            pltpu.VMEM((layers, line, 2 * shard_rows, X_FIRST_COLS), low),
-            pltpu.VMEM((layers, line - 1, 2 * shard_rows, X_FIRST_COLS), low),
-            pltpu.VMEM((layers, line - 1, 2 * shard_rows, X_FIRST_COLS), low),
-            pltpu.VMEM((layers, shard_rows, X_FIRST_COLS), low),
-            dma((layers, slots)),
-            dma((layers, slots)),
-            dma((layers, slots)),
-            dma((layers, slots)),
-            dma((layers, line - 1)),
-            dma((layers, line - 1)),
-            dma((layers, line - 1)),
-            dma((layers, line - 1)),
-            dma((layers, line - 1)),
-            dma((layers, line - 1)),
-            dma((layers, line - 1)),
-            dma((layers, line - 1)),
-            dma((layers,)),
-            dma((layers,)),
-        ],
-        compiler_params=pltpu.CompilerParams(
-            collective_id=1, has_side_effects=True, vmem_limit_bytes=60 << 20
-        ),
-        name="scatter_grads",
-    )(partial)
 
 
 SMALL_COLS = 128
@@ -725,29 +510,41 @@
     )(h0, ids[:, :, None], ids[:, None, :], rows, qkv_bias, up_bias, full, *aliased)
 
 
+SLOTS = 2
+
+
 def backward_kernel(
-    tick, has_alias, head_width, hidden_width, g0_ref, ids_col_ref, ids_row_ref, rows_ref, full_ref, *refs
+    line, aligned, head_width, hidden_width, g0_ref, ids_col_ref, ids_row_ref, rows_ref, full_ref, *refs
 ):
     saves = refs[:7]
-    refs = refs[7:]
-    out_count = 6
-    if has_alias:
-        refs = refs[out_count:]
-    d_out, small_out, qkv_bias_out, up_bias_out, g_out, low_out = refs[:out_count]
     (
+        out, small_out, inner_out, g_out, d_out, own_in, x_in, z_in,
         w_qkv, w_out, w_up, w_down, hid, qkv, lse, mixed, mid, act, slope, grad, low, hidden_grad, qkv_grad, normed,
-        mixed_grad, mask, send, recv, stage, small, qkv_bias, up_bias,
-        w_sem, load_sem, send_sem, recv_sem, stage_sem, end_sem,
-    ) = refs[out_count:]
+        mixed_grad, mask, send, recv, stage, small, inner_sum, given, run_own, run_x, run_z, run_out, small_in, inner_in,
+        w_sem, load_sem, send_sem, recv_sem, stage_sem, end_sem, given_sem, own_send, own_recv, x_send, x_recv, z_send, z_recv, run_sem,
+        out_sem, small_send, small_recv, inner_send, inner_recv,
+    ) = refs[7:]
     held = (hid, qkv, lse, mixed, mid, act, slope)
     layers, micro, tokens, width = hid.shape
     section = lax.axis_index("section")
     partner = {"tensor": 1 - lax.axis_index("tensor")}
+    other = {"section": 1 - section}
+    place = lax.axis_index("fsdp")
+    count = 2 * line
+    z = place // 2
+    x = lax.rem(place, 2)
+    to_x = {"fsdp": z * 2 + 1 - x}
+    to_up = {"fsdp": jnp.minimum(z + 1, line - 1) * 2 + x}
+    to_down = {"fsdp": jnp.maximum(z - 1, 0) * 2 + x}
     tile = 256
+    tiles = width // tile
+    shard_rows = width // count
+    group_cols = stage.shape[2]
+    steps = 3 * line
+    groups = 3
     scale = 1.0 / math.sqrt(HEAD_DIM)
 
-    @pl.when(section == 1 - tick)
-    def _():
+    if True:
         ends = (0, 3 * head_width, 4 * head_width, 4 * head_width + hidden_width, 4 * head_width + 2 * hidden_width)
 
         def fetch(layer, index):
@@ -774,11 +571,22 @@
                 load(index, layer).start()
         barrier = pltpu.get_barrier_semaphore()
         pl.semaphore_signal(barrier, inc=1, device_id=partner, device_id_type=MESH)
-        pl.semaphore_wait(barrier, 1)
+        pl.semaphore_signal(barrier, inc=1, device_id=other, device_id_type=MESH)
+        for turn in range(1, count):
+            peer = {"fsdp": lax.rem(place + turn, count)}
+            pl.semaphore_signal(barrier, inc=1, device_id=peer, device_id_type=MESH)
+        pl.semaphore_signal(
+            barrier, inc=1, device_id={"section": 1 - section, "fsdp": z * 2 + 1 - x}, device_id_type=MESH
+        )
+        pl.semaphore_wait(barrier, count + 2)
+
+        hand_over = pltpu.make_async_remote_copy(
+            src_ref=low, dst_ref=given, send_sem=given_sem.at[0], recv_sem=given_sem.at[1],
+            device_id=other, device_id_type=MESH,
+        )
 
         small[...] = jnp.zeros_like(small)
-        qkv_bias[...] = jnp.zeros_like(qkv_bias)
-        up_bias[...] = jnp.zeros_like(up_bias)
+        inner_sum[...] = jnp.zeros_like(inner_sum)
         for part in range(micro):
             col = ids_col_ref[part]
             row = ids_row_ref[part]
@@ -786,14 +594,19 @@
             two = lax.broadcasted_iota(jnp.int32, (tokens, tokens), 1)
             allowed = ((col == row) & (col >= 0)) | (one == two)
             mask[part] = jnp.where(allowed, 0.0, -1e30)
-            grad[part] = g0_ref[part].astype(jnp.float32)
-
-        def exchange(layer, step, part):
+
+        @pl.when(section == 1)
+        def _():
+            for part in range(micro):
+                grad[part] = g0_ref[part].astype(jnp.float32)
+
+
+        def exchange(step, part):
             return pltpu.make_async_remote_copy(
-                src_ref=send.at[layer, step, part],
-                dst_ref=recv.at[layer, step, part],
-                send_sem=send_sem.at[layer, step, part],
-                recv_sem=recv_sem.at[layer, step, part],
+                src_ref=send.at[step, part],
+                dst_ref=recv.at[step, part],
+                send_sem=send_sem.at[step, part],
+                recv_sem=recv_sem.at[step, part],
                 device_id=partner,
                 device_id_type=MESH,
             )
@@ -817,7 +630,7 @@
             @pl.loop(0, tokens, step=32)
             def _(start):
                 span = pl.ds(pl.multiple_of(start, 32), 32)
-                outer = send[layer, step, part, span].astype(jnp.float32) + recv[layer, step, part, span].astype(jnp.float32)
+                outer = send[step, part, span].astype(jnp.float32) + recv[step, part, span].astype(jnp.float32)
                 unit, inverse = norm_parts(source[layer, part, span])
                 inner = outer * gain
                 first = jnp.mean(inner, axis=-1, keepdims=True)
@@ -842,13 +655,155 @@
                 low[pl.ds(pl.multiple_of(part * tokens + start, 32), 32)] = value
                 small[layer, bias_row : bias_row + 1] += column_sum(value)
 
-        def put(layer, number, group):
-            start = (2 * head_width + 2 * head_width, 4 * head_width + hidden_width, 0)[group]
+        def columns(group):
+            return pl.ds(pl.multiple_of((2 - group) * group_cols, group_cols), group_cols)
+
+        def part_rows(row_z, row_x):
+            return pl.ds(pl.multiple_of((row_z * 2 + row_x) * shard_rows, shard_rows), shard_rows)
+
+        def put(layer, turn, number, group):
             return pltpu.make_async_copy(
-                stage.at[number],
-                d_out.at[layer, pl.ds(pl.multiple_of(number * tile, tile), tile), pl.ds(start, stage.shape[2])],
-                stage_sem.at[number],
+                stage.at[turn],
+                d_out.at[layer, pl.ds(pl.multiple_of(number * tile, tile), tile), columns(group)],
+                stage_sem.at[turn],
             )
+
+        def route(step):
+            below, above = z, line - 1 - z
+            gap = jnp.maximum(below, above) - jnp.minimum(below, above)
+            rest = jnp.maximum(step - gap, 0)
+            far = step < gap
+            upward = jnp.where(far, jnp.where(above > below, 1, 0), 1 - lax.rem(rest, 2))
+            reach = jnp.where(far, jnp.maximum(below, above) - step, jnp.minimum(below, above) - rest // 2)
+            ends_here = step == line - 1
+            target = jnp.where(ends_here, z, jnp.where(upward == 1, z + reach, z - reach))
+            return target, upward == 1, ends_here
+
+        def to_partner(turn, group, row_z):
+            runner = jnp.where(turn == 0, 1 - section, section)
+            return pltpu.make_async_remote_copy(
+                src_ref=d_out.at[last - turn, part_rows(row_z, 1 - x), columns(group)],
+                dst_ref=x_in.at[turn, group, row_z],
+                send_sem=x_send.at[turn, group, row_z],
+                recv_sem=x_recv.at[turn, group, row_z],
+                device_id={"section": runner, "fsdp": z * 2 + 1 - x},
+                device_id_type=MESH,
+            )
+
+        def to_other(group, row_z):
+            return pltpu.make_async_remote_copy(
+                src_ref=d_out.at[last, part_rows(row_z, x), columns(group)],
+                dst_ref=own_in.at[group, row_z],
+                send_sem=own_send.at[group, row_z],
+                recv_sem=own_recv.at[group, row_z],
+                device_id=other,
+                device_id_type=MESH,
+            )
+
+        def onward(turn, group, row_z, slot, side):
+            return pltpu.make_async_remote_copy(
+                src_ref=run_own.at[slot],
+                dst_ref=z_in.at[turn, group, side, row_z],
+                send_sem=z_send.at[slot],
+                recv_sem=z_recv.at[turn, group, side, row_z],
+                device_id=(to_up, to_down)[side],
+                device_id_type=MESH,
+            )
+
+        def publish(group):
+            return pltpu.make_async_copy(run_out, out.at[0, :, columns(group)], out_sem.at[0])
+
+        def publish_other(group):
+            return pltpu.make_async_remote_copy(
+                src_ref=run_out, dst_ref=out.at[last, :, columns(group)],
+                send_sem=out_sem.at[1], recv_sem=out_sem.at[2 + group],
+                device_id=other, device_id_type=MESH,
+            )
+
+        def add_rows(slot, source):
+            @pl.loop(0, shard_rows, step=16)
+            def _(start):
+                span = pl.ds(pl.multiple_of(start, 16), 16)
+                run_own[slot, span] = run_own[slot, span] + source[span]
+
+        def run_sums(turn):
+            @pl.loop(0, steps)
+            def _(number):
+                group = number // line
+                step = lax.rem(number, line)
+                slot = lax.rem(number, SLOTS)
+                target, upward, ends_here = route(step)
+
+                @pl.when((number >= SLOTS) & (lax.rem(number + line - SLOTS, line) != line - 1))
+                def _():
+                    onward(turn, 0, 0, slot, 0).wait_send()
+
+                if turn == 0:
+                    to_other(group, target).wait_recv()
+                    source = own_in.at[group, target]
+                else:
+                    source = d_out.at[last - turn, part_rows(target, x), columns(group)]
+                own = pltpu.make_async_copy(source, run_own.at[slot], run_sem.at[0])
+                own.start()
+                to_partner(turn, group, target).wait_recv()
+                mate = pltpu.make_async_copy(x_in.at[turn, group, target], run_x, run_sem.at[1])
+                mate.start()
+                feeds = (
+                    jnp.logical_or(upward, ends_here) & (z > 0),
+                    jnp.logical_or(jnp.logical_not(upward), ends_here) & (z < line - 1),
+                )
+                moves = []
+                for side in range(2):
+                    move = pltpu.make_async_copy(z_in.at[turn, group, side, target], run_z.at[side], run_sem.at[2 + side])
+                    moves.append(move)
+
+                    @pl.when(feeds[side])
+                    def _(side=side, move=move):
+                        onward(turn, group, target, slot, side).wait_recv()
+                        move.start()
+
+                own.wait()
+                mate.wait()
+                add_rows(slot, run_x)
+                for side in range(2):
+
+                    @pl.when(feeds[side])
+                    def _(side=side):
+                        moves[side].wait()
+                        add_rows(slot, run_z.at[side])
+
+                @pl.when(jnp.logical_not(ends_here) & upward)
+                def _():
+                    onward(turn, group, target, slot, 0).start()
+
+                @pl.when(jnp.logical_not(ends_here) & jnp.logical_not(upward))
+                def _():
+                    onward(turn, group, target, slot, 1).start()
+
+                @pl.when(ends_here)
+                def _():
+                    @pl.when(group > 0)
+                    def _():
+                        publish(group).wait() if turn else publish_other(group).wait_send()
+
+                    @pl.loop(0, shard_rows, step=16)
+                    def _(start):
+                        span = pl.ds(pl.multiple_of(start, 16), 16)
+                        run_out[span] = run_own[slot, span].astype(jnp.float32)
+
+                    publish(group).start() if turn else publish_other(group).start()
+
+            for number in range(steps - SLOTS, steps):
+                if number % line != line - 1:
+                    onward(turn, 0, 0, number % SLOTS, 0).wait_send()
+            publish(0).wait() if turn else publish_other(0).wait_send()
+
+        @pl.when(section == 0)
+        def _():
+            run_sums(0)
+            hand_over.wait_recv()
+            for part in range(micro):
+                grad[part] = given[pl.ds(part * tokens, tokens)].astype(jnp.float32)
 
         def mlp_stage(layer, part):
             round_grad(layer, part, 5)
@@ -864,29 +819,48 @@
                 value = jnp.dot(low[rows_of(part)], w_down[:, span], preferred_element_type=jnp.float32)
                 value = (value * slope[layer, part, :, span].astype(jnp.float32)).astype(jnp.bfloat16)
                 hidden_grad[rows_of(part), span] = value
-                up_bias[layer, :, span] += column_sum(value)
+                place_in = pl.ds(pl.multiple_of(2 * head_width + start, tile), tile)
+                inner_sum[layer, :, place_in] += column_sum(value)
 
             @pl.when(part == 0)
             def _():
                 fetch(layer, 2).wait()
+
+            @pl.when(layer < last)
+            def _():
+                exchange(0, part).wait_send()
 
             @pl.loop(0, width, step=tile)
             def _(start):
                 span = pl.ds(pl.multiple_of(start, tile), tile)
                 value = contract_last(hidden_grad[rows_of(part)], w_up[span])
-                send[layer, 0, part, :, span] = value.astype(jnp.bfloat16)
-
-            exchange(layer, 0, part).start()
-
-        def weight_tiles(layer, group, free, fill):
-            @pl.loop(0, width // tile)
+                send[0, part, :, span] = value.astype(jnp.bfloat16)
+
+            exchange(0, part).start()
+
+        def weight_tiles(layer, turn, group, fill):
+            def row_of(number):
+                return route(number)[0] if tiles == line else number
+
+            def finish(number):
+                row = row_of(number)
+                put(layer, number, row, group).wait()
+                for extra in range(line // tiles):
+                    row_z = row * (line // tiles) + extra
+                    to_partner(turn, group, row_z).start()
+                    pl.when(turn == 0)(to_other(group, row_z).start)
+
+            @pl.loop(0, tiles)
             def _(number):
-                pl.when(free)(lambda: put(layer, number, group).wait())
-                fill(number, pl.ds(pl.multiple_of(number * tile, tile), tile))
-                put(layer, number, group).start()
+                row = row_of(number)
+                fill(number, pl.ds(pl.multiple_of(row * tile, tile), tile))
+                put(layer, number, row, group).start()
+                pl.when(number > 0)(lambda: finish(jnp.maximum(number - 1, 0)))
+
+            finish(tiles - 1)
 
         def attention_stage(layer, part):
-            exchange(layer, 0, part).wait_recv()
+            exchange(0, part).wait_recv()
             norm_back(layer, 0, part, mid, 1, 4)
             round_grad(layer, part, 3)
 
@@ -924,23 +898,29 @@
                 for piece in range(3):
                     value = jnp.where(lane < HEAD_DIM, halves[0][piece], halves[1][piece]).astype(jnp.bfloat16)
                     qkv_grad[rows_of(part), spans[piece]] = value
-                    qkv_bias[layer, :, spans[piece]] += column_sum(value)
+                    if piece != 1:
+                        place_in = pl.ds((piece // 2) * head_width + pair * LANES, LANES)
+                        inner_sum[layer, :, place_in] += column_sum(value)
 
             @pl.when(part == 0)
             def _():
                 fetch(layer, 0).wait()
+
+            @pl.when(layer < last)
+            def _():
+                exchange(1, part).wait_send()
 
             @pl.loop(0, width, step=tile)
             def _(start):
                 span = pl.ds(pl.multiple_of(start, tile), tile)
                 value = contract_last(qkv_grad[rows_of(part)], w_qkv[span])
-                send[layer, 1, part, :, span] = value.astype(jnp.bfloat16)
-
-            exchange(layer, 1, part).start()
+                send[1, part, :, span] = value.astype(jnp.bfloat16)
+
+            exchange(1, part).start()
 
         @pl.loop(0, layers)
         def _(turn):
-            layer = layers - 1 - turn
+            layer = last - turn
 
             @pl.loop(0, micro)
             def _(part):
@@ -957,7 +937,7 @@
                 both = act[layer].reshape(micro * tokens, hidden_width)
                 stage[number] = contract_rows(low[:, span], both).astype(jnp.bfloat16)
 
-            weight_tiles(layer, 1, turn > 0, fill_down)
+            weight_tiles(layer, turn, 0, fill_down)
             load(4, layer).wait()
 
             @pl.loop(0, micro)
@@ -967,7 +947,7 @@
             def fill_up(number, span):
                 stage[number] = contract_rows(normed[:, span], hidden_grad[...]).astype(jnp.bfloat16)
 
-            weight_tiles(layer, 0, turn >= 0, fill_up)
+            weight_tiles(layer, turn, 1, fill_up)
 
             @pl.loop(0, micro)
             def _(part):
@@ -990,62 +970,105 @@
                 stage[number, :, : 3 * head_width] = contract_rows(normed[:, span], qkv_grad[...]).astype(jnp.bfloat16)
                 stage[number, :, 3 * head_width :] = contract_rows(low[:, span], both).astype(jnp.bfloat16)
 
-            weight_tiles(layer, 2, turn >= 0, fill_attention)
+            weight_tiles(layer, turn, 2, fill_attention)
 
             @pl.loop(0, micro)
             def _(part):
-                exchange(layer, 1, part).wait_recv()
+                exchange(1, part).wait_recv()
                 norm_back(layer, 1, part, hid, 0, 2)
 
         for part in range(micro):
             low[pl.ds(part * tokens, tokens)] = grad[part].astype(jnp.bfloat16)
-        ending = [
-            pltpu.make_async_copy(small, small_out, end_sem.at[0]),
-            pltpu.make_async_copy(qkv_bias, qkv_bias_out, end_sem.at[1]),
-            pltpu.make_async_copy(up_bias, up_bias_out, end_sem.at[2]),
-            pltpu.make_async_copy(grad, g_out, end_sem.at[3]),
-            pltpu.make_async_copy(low, low_out, end_sem.at[4]),
-        ]
-        for copy in ending:
-            copy.start()
-        for number in range(width // tile):
-            put(0, number, 2).wait()
-
-        @pl.loop(0, layers)
-        def _(layer):
-            @pl.loop(0, micro)
-            def _(part):
-                for step in range(2):
-                    exchange(layer, step, part).wait_send()
-
-        for copy in ending:
-            copy.wait()
-
-
-def backward(tick, g0, ids, params, full, saves, previous, head_width, hidden_width):
+        pl.when(section == 1)(hand_over.start)
+        ending = pltpu.make_async_copy(grad, g_out, end_sem.at[0])
+        ending.start()
+
+        def small_copies(peer, turn):
+            if aligned:
+                cut, inner_cut = pl.ds(pl.multiple_of(peer * shard_rows, shard_rows), shard_rows), pl.ds(
+                    pl.multiple_of(peer * 3 * shard_rows, 3 * shard_rows), 3 * shard_rows
+                )
+            else:
+                cut, inner_cut = pl.ds(0, width), pl.ds(0, 3 * width)
+            made = []
+            for source, target, sends, receives in (
+                (small.at[:, :, cut], small_in, small_send, small_recv),
+                (inner_sum.at[:, :, inner_cut], inner_in, inner_send, inner_recv),
+            ):
+                made.append(pltpu.make_async_remote_copy(
+                    src_ref=source, dst_ref=target.at[turn], send_sem=sends.at[turn], recv_sem=receives.at[turn],
+                    device_id={"fsdp": peer}, device_id_type=MESH,
+                ))
+            return made
+
+        for turn in range(1, count):
+            for copy in small_copies(lax.rem(place + turn, count), turn):
+                copy.start()
+
+        run_sums(1)
+        pl.when(section == 1)(lambda: run_sums(0))
+
+        if aligned:
+            mine = pl.ds(pl.multiple_of(place * shard_rows, shard_rows), shard_rows)
+            inner_mine = pl.ds(pl.multiple_of(place * 3 * shard_rows, 3 * shard_rows), 3 * shard_rows)
+        else:
+            mine, inner_mine = pl.ds(0, width), pl.ds(0, 3 * width)
+        small_out[...] = small[:, :, mine]
+        inner_out[...] = inner_sum[:, :, inner_mine]
+        for turn in range(1, count):
+            for copy in small_copies(lax.rem(place + turn, count), turn):
+                copy.wait()
+            small_out[...] += small_in[turn]
+            inner_out[...] += inner_in[turn]
+
+        for step in range(2):
+            for part in range(micro):
+                exchange(step, part).wait_send()
+
+        @pl.loop(0, groups)
+        def _(group):
+            @pl.loop(0, line)
+            def _(row_z):
+                to_partner(0, group, row_z).wait_send()
+                to_partner(1, group, row_z).wait_send()
+                to_other(group, row_z).wait_send()
+
+        for group in range(groups):
+            publish_other(group).wait_recv()
+        pl.when(section == 1)(hand_over.wait_send)
+        ending.wait()
+
+
+def backward(g0, ids, params, full, saves, head_width, hidden_width):
     rows, qkv_bias, up_bias = params
     layers, width, cols = full.shape
     micro, tokens = ids.shape
+    count = lax.axis_size("fsdp")
+    line = count // 2
+    shard_rows = width // count
+    aligned = shard_rows % LANES == 0
+    group_cols = 4 * head_width
+    small_width = shard_rows if aligned else width
     shapes = saved_shapes(layers, micro, tokens, width, head_width, hidden_width)
     vmem = pl.BlockSpec(memory_space=pltpu.VMEM)
     hbm = pl.BlockSpec(memory_space=pl.ANY)
     dma = pltpu.SemaphoreType.DMA
     low, wide = jnp.bfloat16, jnp.float32
     outs = (
-        ((layers, width, cols), low),
-        ((layers, 8, width), wide),
-        ((layers, 1, 3 * head_width), wide),
-        ((layers, 1, hidden_width), wide),
+        ((layers, shard_rows, 3 * group_cols), wide),
+        ((layers, 8, small_width), wide),
+        ((layers, 1, 3 * small_width), wide),
         ((micro, tokens, width), wide),
-        ((micro * tokens, width), low),
+        ((layers, width, 3 * group_cols), low),
+        ((3, line, shard_rows, group_cols), low),
+        ((2, 3, line, shard_rows, group_cols), low),
+        ((2, 3, 2, line, shard_rows, group_cols), low),
     )
-    aliased = () if previous is None else tuple(previous)
     return pl.pallas_call(
-        functools.partial(backward_kernel, tick, previous is not None, head_width, hidden_width),
+        functools.partial(backward_kernel, line, aligned, head_width, hidden_width),
         out_shape=[jax.ShapeDtypeStruct(shape, kind) for shape, kind in outs],
-        in_specs=[vmem] * 4 + [hbm] * (8 + len(aliased)),
-        out_specs=[hbm] * len(outs),
-        input_output_aliases={12 + number: number for number in range(len(aliased))},
+        in_specs=[vmem] * 4 + [hbm] * 8,
+        out_specs=[hbm, vmem, vmem] + [hbm] * 5,
         scratch_shapes=[
             pltpu.VMEM((width, 3 * head_width), low),
             pltpu.VMEM((width, head_width), low),
@@ -1059,48 +1082,53 @@
             pltpu.VMEM((micro * tokens, width), low),
             pltpu.VMEM((tokens, head_width), low),
             pltpu.VMEM((micro, tokens, tokens), wide),
-            pltpu.VMEM((layers, 2, micro, tokens, width), low),
-            pltpu.VMEM((layers, 2, micro, tokens, width), low),
-            pltpu.VMEM((width // 256, 256, 4 * head_width), low),
+            pltpu.VMEM((2, micro, tokens, width), low),
+            pltpu.VMEM((2, micro, tokens, width), low),
+            pltpu.VMEM((width // 256, 256, group_cols), low),
             pltpu.VMEM((layers, 8, width), wide),
-            pltpu.VMEM((layers, 1, 3 * head_width), wide),
-            pltpu.VMEM((layers, 1, hidden_width), wide),
+            pltpu.VMEM((layers, 1, 3 * width), wide),
+            pltpu.VMEM((micro * tokens, width), low),
+            pltpu.VMEM((SLOTS, shard_rows, group_cols), low),
+            pltpu.VMEM((shard_rows, group_cols), low),
+            pltpu.VMEM((2, shard_rows, group_cols), low),
+            pltpu.VMEM((shard_rows, group_cols), wide),
+            pltpu.VMEM((count, layers, 8, small_width), wide),
+            pltpu.VMEM((count, layers, 1, 3 * small_width), wide),
             dma((4,)),
             dma((7, layers)),
-            dma((layers, 2, micro)),
-            dma((layers, 2, micro)),
+            dma((2, micro)),
+            dma((2, micro)),
             dma((width // 256,)),
+            dma((1,)),
+            dma((2,)),
+            dma((3, line)),
+            dma((3, line)),
+            dma((2, 3, line)),
+            dma((2, 3, line)),
+            dma((SLOTS,)),
+            dma((2, 3, 2, line)),
+            dma((4,)),
             dma((5,)),
+            dma((count,)),
+            dma((count,)),
+            dma((count,)),
+            dma((count,)),
         ],
         compiler_params=pltpu.CompilerParams(
-            collective_id=4 + tick, has_side_effects=True, vmem_limit_bytes=62 << 20
+            collective_id=4, has_side_effects=True, vmem_limit_bytes=63 << 20
         ),
         name="backward",
-    )(g0, ids[:, :, None], ids[:, None, :], rows, full, *saves, *aliased)
-
-
-def pack_small(small, qkv_bias, up_bias, head_width, count):
-    layers, _, width = small.shape
-    inner = jnp.concatenate(
-        [qkv_bias[:, 0, :head_width], qkv_bias[:, 0, 2 * head_width :], up_bias[:, 0]], axis=1
-    )
-    inner = jnp.swapaxes(inner.reshape(layers, count, 3, width // count), 1, 2).reshape(layers, 3, width)
-    columns = jnp.swapaxes(jnp.concatenate([small[:, :6], inner], axis=1), 1, 2)
-    return jnp.pad(columns, ((0, 0), (0, 0), (0, SMALL_COLS - columns.shape[2]))).astype(jnp.bfloat16)
+    )(g0, ids[:, :, None], ids[:, None, :], rows, full, *saves)
 
 
 def unpack_grads(full, head_width, hidden_width):
     layers, rows, cols = full.shape
     ends = [3 * head_width, 4 * head_width, 4 * head_width + hidden_width, 4 * head_width + 2 * hidden_width]
-    small = jnp.swapaxes(full[:, :, ends[3] : ends[3] + 9], 1, 2)
     return (
         full[:, :, : ends[0]].reshape(layers, rows, 3, head_width),
         full[:, :, ends[0] : ends[1]],
         full[:, :, ends[1] : ends[2]],
         full[:, :, ends[2] : ends[3]],
-        small[:, :2],
-        small[:, 2:6],
-        small[:, 6:].reshape(layers, 1, -1),
     )
 
 
@@ -1125,15 +1153,22 @@
     saved = forward(0, block_input, image_ids, params, full, None, head_width, hidden_width)
     received = shifted(saved[8], "section", 1)
     saved = forward(1, received, image_ids, params, full, saved, head_width, hidden_width)
-    grads = backward(0, cotangent, image_ids, params, full, saved[:7], None, head_width, hidden_width)
-    received = shifted(grads[5], "section", -1).reshape(cotangent.shape)
-    grads = backward(1, received, image_ids, params, full, saved[:7], grads, head_width, hidden_width)
-    partial, small, qkv_bias, up_bias, input_grad, _ = grads
-    columns = pack_small(small, qkv_bias, up_bias, head_width, count)
-    partial = lax.dynamic_update_slice(partial, columns, (0, 0, partial.shape[2] - SMALL_COLS))
-    summed = unpack_grads(scatter_grads(partial), head_width, hidden_width)
+    summed, small, inner, input_grad = backward(
+        cotangent, image_ids, params, full, saved[:7], head_width, hidden_width
+    )[:4]
+    rows = qkv_weight.shape[1]
+    if small.shape[2] != rows:
+        place = lax.axis_index("fsdp")
+        small = lax.dynamic_slice_in_dim(small, place * rows, rows, 2)
+        inner = lax.dynamic_slice_in_dim(inner, place * 3 * rows, 3 * rows, 2)
     section_ends = jnp.where(section == 0, input_grad, saved[7])[None]
-    return (section_ends, *summed)
+    return (
+        section_ends,
+        *unpack_grads(summed, head_width, hidden_width),
+        small[:, :2],
+        small[:, 2:6],
+        inner,
+    )
 
 
 def solution(mesh):

time: 740 us -> 703 us (0.950)
  waiting for transfers between devices: 160 us -> 2.23 us
  Pallas kernels: 472 us -> 596 us
    ppermute x2 -> x1, waiting for transfers between devices: 160 us -> 2.23 us  [shifted(): lax.ppermute(value, axis, [(source, source + steps) for source in range(i...]
    pallas_call x3 -> x1, Pallas kernels: 265 us -> 389 us  [backward(): pl.pallas_call(functools.partial(backward_kernel, line, aligned, head_wid...]
    ppermute x2 -> x1, starting transfers between devices: 71.6 us -> 70.3 us  [shifted(): lax.ppermute(value, axis, [(source, source + steps) for source in range(i...]
  transfers between devices with their start and end apart: 2 -> 1, of which waited for: 2 -> 1; matrix products, arithmetic and copies ran while one was open for 0% -> 0% of each run, Pallas kernels for 0% -> 0%
where the time goes in v3:
time: 703 us; the launch traced here: 702 us
  Pallas kernels  596 us (85%)
  starting transfers between devices  70.3 us (10%)
  local copies, waits for them, and re-layouts  28.3 us (4%)
    pallas_call x1, Pallas kernels, backward(): pl.pallas_call(functools.partial(backward_kernel, line, aligned, head_wid...  389 us
    pallas_call x1, Pallas kernels, gather_weights(): pl.pallas_call(functools.partial(gather_kernel, line), out_shape=jax.Shap...  140 us
    ppermute x1, starting transfers between devices, shifted(): lax.ppermute(value, axis, [(source, source + steps) for source in range(i...  70.3 us
    pallas_call x2, Pallas kernels, forward(): pl.pallas_call(functools.partial(forward_kernel, tick, previous is not No...  67.7 us
  transfers between devices with their start and end apart: 1, of which 1 were waited for; matrix products, arithmetic and copies ran while one was open for 0% of the time, Pallas kernels for 0%

profile of v3, /device:TPU:0, one launch (start us, length us, event | category | flops | bytes accessed | tf_op | source)
XLA Modules:
  0.0 701.7 jit_solution(762415041765097938)
XLA Ops:
  0.7 1.5 copy.66
  2.2 1.2 copy.70
  3.4 1.2 constant_dynamic-update-slice_fusion.3
  4.6 0.1 copy.69
  4.8 0.8 copy.67
  5.5 0.8 copy.68
  6.3 1.4 constant_dynamic-update-slice_fusion.1
  7.9 0.1 maximum_bitcast_fusion
  8.1 1.6 copy-done.1
  9.7 139.7 %gather_weights.1.full_ref = bf16[2,1024,6272]{2,1,0:T(8,128)(2,1)} custom-call(bf16[2,128,6272]{2,1,0:T(8,128)(2,1)} %copy-done.1), custom_call_target="tpu_custom_call" | custom-call | tf_op jit(solution)/shard_map/gather_weights/pallas_call | solution.py:171
  149.4 1.1 slice.27
  150.5 0.2 copy.84
  150.9 0.6 split.14.up_bias_ref
  151.5 0.6 slice.36.rows_ref
  152.1 0.6 broadcast_in_dim.17.ids_row_ref
  152.7 0.8 copy.79.ids_col_ref
  153.5 0.6 pad_maximum_fusion.qkv_bias_ref
  154.1 65.8 %forward.2 = (f32[2,2,224,1024]{3,2,1,0:T(8,128)}, bf16[2,2,224,1536]{3,2,1,0:T(8,128)(2,1)}, f32[2,2,224,8]{3,2,1,0:T(8,128)}, bf16[2,2,224,512]{3,2,1,0:T(8,12...) custom-call(bf16[2,224,1024]{2,1,0:T(8,128)(2,1)} %h0_ref.1, ...), custom_call_target="tpu_custom_call" | custom-call | tf_op jit(solution)/shard_map/forward/pallas_call | solution.py:485
  219.9 70.3 %collective-permute-start = (bf16[2,224,1024]{2,1,0:T(8,128)(2,1)}, bf16[2,224,1024]{2,1,0:T(8,128)(2,1)S(1)}, u32[]{:S(2)}, u32[]{:S(2)}) collective-permute-start(bf16[2,224,1024]{2,1,0:T(8,128)(2,1)} %get-tuple-element.29.refs_8_), channel_id=1, source_target_pairs={{0,16},{1,17},{2,18},{3,19},{4,20},{5,21},{6,22},{7,23},{8,24},{9,... | collective-permute-start | bytes 2752520 | tf_op jit(solution)/shard_map/ppermute | solution.py:215
  290.3 2.2 collective-permute-done.h0_ref
  292.5 0.9 copy-done.3
  293.4 1.9 forward.3
  295.3 388.8 %backward.1 = (f32[2,128,6144]{2,1,0:T(8,128)}, f32[2,8,128]{2,1,0:T(8,128)}, f32[2,1,384]{2,1,0:T(1,128)}, f32[2,224,1024]{2,1,0:T(8,128)}, bf16[2,1024,6144]{2...) custom-call(bf16[2,224,1024]{2,1,0:T(8,128)(2,1)} %g0_ref.1, ...), custom_call_target="tpu_custom_call" | custom-call | tf_op jit(solution)/shard_map/backward/pallas_call | solution.py:1067
  684.1 1.5 slice.30
  685.6 4.7 fusion
  690.4 1.9 slice.31
  692.2 0.6 slice.35
  692.8 0.6 slice.34
  693.4 1.6 copy.80
  695.0 3.0 copy.81
  698.1 3.1 select_bitcast_fusion
  701.1 0.6 copy.99
  (36 shorter events, 0.4 us)
Async XLA Ops:
  0.6 3.9 copy-start.11
  0.6 4.1 copy-start.12
  0.7 4.9 copy-start.10
  0.7 5.6 copy-start.4
  6.3 1.5 copy-start.2
  6.3 1.6 copy-start.5
  6.3 1.6 copy-start.6
  8.1 1.6 copy-start.1
  9.7 142.4 %copy-start.7 = (s32[2,224]{1,0:T(2,128)S(1)}, s32[2,224]{1,0:T(2,128)}, u32[]{:S(2)}) copy-start(s32[2,224]{1,0:T(2,128)} %param.11) | copy-start | bytes 5380
  219.9 72.6 %collective-permute-start = (bf16[2,224,1024]{2,1,0:T(8,128)(2,1)}, bf16[2,224,1024]{2,1,0:T(8,128)(2,1)S(1)}, u32[]{:S(2)}, u32[]{:S(2)}) collective-permute-start(bf16[2,224,1024]{2,1,0:T(8,128)(2,1)} %get-tuple-element.29.refs_8_), channel_id=1, source_target_pairs={{0,16},{1,17},{2,18},{3,19},{4,20},{5,21},{6,22},{7,23},{8,24},{9,... | collective-permute-start | bytes 2752520 | tf_op jit(solution)/shard_map/ppermute | solution.py:215
  292.5 0.9 copy-start.3
  685.6 6.6 copy-start.8
  692.2 5.8 copy-start
  698.1 3.1 copy-start.9

commit v4 on v3

--- a/solution.py
+++ b/solution.py
@@ -13,188 +13,6 @@
 
 
 MESH = pl.DeviceIdType.MESH
-X_FIRST_COLS = 1024
-
-
-def gather_kernel(line, w_ref, g_ref, local_sem, go_sem, sax, rax, sau, rau, sad, rad, sbx, rbx, sbu, rbu, sbd, rbd):
-    layers, shard_rows, cols = w_ref.shape
-    cols_a = cols - X_FIRST_COLS
-    section = lax.axis_index("section")
-    place = lax.axis_index("fsdp")
-    z = place // 2
-    x = lax.rem(place, 2)
-    has_up = z < line - 1
-    has_down = z > 0
-    to_x = {"fsdp": z * 2 + 1 - x}
-    to_up = {"fsdp": jnp.minimum(z + 1, line - 1) * 2 + x}
-    to_down = {"fsdp": jnp.maximum(z - 1, 0) * 2 + x}
-
-    barrier = pltpu.get_barrier_semaphore()
-    pl.semaphore_signal(barrier, inc=1, device_id=to_x, device_id_type=MESH)
-    pl.semaphore_signal(barrier, inc=1, device_id={"section": 1 - section}, device_id_type=MESH)
-
-    @pl.when(has_up)
-    def _():
-        pl.semaphore_signal(barrier, inc=1, device_id=to_up, device_id_type=MESH)
-
-    @pl.when(has_down)
-    def _():
-        pl.semaphore_signal(barrier, inc=1, device_id=to_down, device_id_type=MESH)
-
-    pl.semaphore_wait(barrier, 2 + jnp.where(has_up, 1, 0) + jnp.where(has_down, 1, 0))
-
-    span_a = pl.ds(0, cols_a)
-    span_b = pl.ds(cols_a, X_FIRST_COLS)
-
-    def spot(layer, row_z, row_x, span):
-        start = pl.multiple_of((row_z * 2 + row_x) * shard_rows, shard_rows)
-        return g_ref.at[layer, pl.ds(start, shard_rows), span]
-
-    def own(layer, span):
-        return w_ref.at[layer, :, span]
-
-    def send(source, layer, row_z, row_x, span, send_sem, recv_sem, target):
-        return pltpu.make_async_remote_copy(
-            src_ref=source,
-            dst_ref=spot(layer, row_z, row_x, span),
-            send_sem=send_sem,
-            recv_sem=recv_sem,
-            device_id=target,
-            device_id_type=MESH,
-        )
-
-    def relay(layer, row_z, row_x, span, send_sem, recv_sem, target):
-        return send(spot(layer, row_z, row_x, span), layer, row_z, row_x, span, send_sem, recv_sem, target)
-
-    @pl.when(section == 1)
-    def _():
-        pl.semaphore_wait(go_sem, 1)
-
-    finish = []
-
-    def launch(copy, condition=None):
-        if condition is None:
-            copy.start()
-            finish.append((copy, None))
-        else:
-            pl.when(condition)(copy.start)
-            finish.append((copy, condition))
-
-    locals_ = []
-    for layer in range(layers):
-        copy = pltpu.make_async_copy(
-            w_ref.at[layer], spot(layer, z, x, pl.ds(0, cols)), local_sem.at[layer]
-        )
-        copy.start()
-        locals_.append(copy)
-        a, b = own(layer, span_a), own(layer, span_b)
-        launch(send(b, layer, z, x, span_b, sbx.at[layer], rbx.at[layer], to_x))
-        launch(send(a, layer, z, x, span_a, sau.at[layer, 0], rau.at[layer, 0], to_up), has_up)
-        launch(send(a, layer, z, x, span_a, sad.at[layer, 0], rad.at[layer, 0], to_down), has_down)
-        launch(send(a, layer, z, x, span_a, sax.at[layer, 0], rax.at[layer, 0], to_x))
-        launch(send(b, layer, z, x, span_b, sbu.at[layer, 0, 0], rbu.at[layer, 0, 0], to_up), has_up)
-        launch(send(b, layer, z, x, span_b, sbd.at[layer, 0, 0], rbd.at[layer, 0, 0], to_down), has_down)
-
-    def arrive(layer, row_z, row_x, span, sem):
-        relay(layer, row_z, row_x, span, sem, sem, to_x).wait_recv()
-
-    for layer in range(layers):
-        arrive(layer, z, 1 - x, span_b, rbx.at[layer])
-        launch(relay(layer, z, 1 - x, span_b, sbu.at[layer, 0, 1], rbu.at[layer, 0, 1], to_up), has_up)
-        launch(relay(layer, z, 1 - x, span_b, sbd.at[layer, 0, 1], rbd.at[layer, 0, 1], to_down), has_down)
-    for hop in range(line - 1):
-        for layer in range(layers):
-            from_below = z - 1 - hop
-            from_above = z + 1 + hop
-            below = from_below >= 0
-            above = from_above < line
-            row_below = jnp.maximum(from_below, 0)
-            row_above = jnp.minimum(from_above, line - 1)
-
-            def pass_on(live, row, rau, sau, rbu, sbu, sem_place, onward, target, hop=hop, layer=layer):
-                pl.when(live)(lambda: arrive(layer, row, x, span_a, rau.at[layer, hop]))
-                launch(relay(layer, row, x, span_a, sax.at[layer, sem_place], rax.at[layer, sem_place], to_x), live)
-                if hop + 1 < line - 1:
-                    launch(
-                        relay(layer, row, x, span_a, sau.at[layer, hop + 1], rau.at[layer, hop + 1], target),
-                        live & onward,
-                    )
-                for side, row_x in ((0, x), (1, 1 - x)):
-                    pl.when(live)(
-                        functools.partial(arrive, layer, row, row_x, span_b, rbu.at[layer, hop, side])
-                    )
-                    if hop + 1 < line - 1:
-                        launch(
-                            relay(
-                                layer, row, row_x, span_b,
-                                sbu.at[layer, hop + 1, side], rbu.at[layer, hop + 1, side], target,
-                            ),
-                            live & onward,
-                        )
-
-            pass_on(below, row_below, rau, sau, rbu, sbu, 1 + hop, has_up, to_up)
-            pass_on(above, row_above, rad, sad, rbd, sbd, line + hop, has_down, to_down)
-    for layer in range(layers):
-        arrive(layer, z, 1 - x, span_a, rax.at[layer, 0])
-        for hop in range(line - 1):
-            from_below = z - 1 - hop
-            from_above = z + 1 + hop
-            pl.when(from_below >= 0)(
-                functools.partial(
-                    arrive, layer, jnp.maximum(from_below, 0), 1 - x, span_a, rax.at[layer, 1 + hop]
-                )
-            )
-            pl.when(from_above < line)(
-                functools.partial(
-                    arrive, layer, jnp.minimum(from_above, line - 1), 1 - x, span_a, rax.at[layer, line + hop]
-                )
-            )
-
-    @pl.when(section == 0)
-    def _():
-        pl.semaphore_signal(go_sem, inc=1, device_id={"section": 1}, device_id_type=MESH)
-
-    for copy in locals_:
-        copy.wait()
-    for copy, condition in finish:
-        if condition is None:
-            copy.wait_send()
-        else:
-            pl.when(condition)(copy.wait_send)
-
-
-def gather_weights(shard):
-    layers, shard_rows, cols = shard.shape
-    count = lax.axis_size("fsdp")
-    line = count // 2
-    dma = pltpu.SemaphoreType.DMA
-    return pl.pallas_call(
-        functools.partial(gather_kernel, line),
-        out_shape=jax.ShapeDtypeStruct((layers, shard_rows * count, cols), shard.dtype),
-        in_specs=[pl.BlockSpec(memory_space=pl.ANY)],
-        out_specs=pl.BlockSpec(memory_space=pl.ANY),
-        scratch_shapes=[
-            dma((layers,)),
-            pltpu.SemaphoreType.REGULAR,
-            dma((layers, 2 * line - 1)),
-            dma((layers, 2 * line - 1)),
-            dma((layers, line - 1)),
-            dma((layers, line - 1)),
-            dma((layers, line - 1)),
-            dma((layers, line - 1)),
-            dma((layers,)),
-            dma((layers,)),
-            dma((layers, line - 1, 2)),
-            dma((layers, line - 1, 2)),
-            dma((layers, line - 1, 2)),
-            dma((layers, line - 1, 2)),
-        ],
-        compiler_params=pltpu.CompilerParams(collective_id=0, has_side_effects=True),
-        name="gather_weights",
-    )(shard)
-
-
-SMALL_COLS = 128
 
 
 def contract_last(left, right):
@@ -209,66 +27,270 @@
     )
 
 
-def shifted(value, axis, steps):
-    count = lax.axis_size(axis)
-    initial, last = (max(0, -steps), min(count, count - steps))
-    return lax.ppermute(value, axis, [(source, source + steps) for source in range(initial, last)])
-
-
-def pack_shard(qkv_w, out_w, up_w, down_w, gains, shifts, inner_part):
-    layers, rows = qkv_w.shape[:2]
-    columns = jnp.concatenate([gains, shifts, inner_part.reshape(layers, -1, rows)], axis=1)
-    columns = jnp.swapaxes(columns, 1, 2)
-    columns = jnp.pad(columns, ((0, 0), (0, 0), (0, SMALL_COLS - columns.shape[2])))
-    return jnp.concatenate([qkv_w.reshape(layers, rows, -1), out_w, up_w, down_w, columns], axis=2)
-
-
-def unpack_params(full, head_width, count):
-    layers, width, cols = full.shape
-    small = jnp.swapaxes(full[:, :, cols - SMALL_COLS : cols - SMALL_COLS + 9], 1, 2).astype(jnp.float32)
-    inner = small[:, 6:].reshape(layers, 3, count, width // count)
-    inner = jnp.swapaxes(inner, 1, 2).reshape(layers, 1, -1)
-    query_bias, value_bias, up_bias = jnp.split(inner, [head_width, 2 * head_width], axis=2)
-    qkv_bias = jnp.concatenate([query_bias, jnp.zeros_like(query_bias), value_bias], axis=2)
-    return small[:, :6], qkv_bias, up_bias
-
-
 LANES = 128
-
-
-def forward_kernel(
-    tick, has_alias, head_width, hidden_width, h0_ref, ids_col_ref, ids_row_ref, rows_ref, qkv_bias_ref, up_bias_ref, full_ref, *refs
-):
-    saved_count = 9
-    if has_alias:
-        refs = refs[saved_count:]
-    outs = refs[:saved_count]
+X_FIRST_COLS = 1024
+
+
+def allowed_bias(ids_row, tokens):
+    spread = jnp.broadcast_to(ids_row, (tokens, tokens))
+    mirror = jnp.transpose(spread)
+    one = lax.broadcasted_iota(jnp.int32, (tokens, tokens), 0)
+    two = lax.broadcasted_iota(jnp.int32, (tokens, tokens), 1)
+    allowed = ((mirror == spread) & (spread >= 0)) | (one == two)
+    return jnp.where(allowed, 0.0, -1e30)
+
+
+def forward_kernel(line, aligned, h0_ref, ids_ref, small_ref, inner_ref, qkv_in, out_in, up_in, down_in, *refs):
+    outs = refs[:8]
     (
-        w_qkv, w_out, w_up, w_down, hid, qkv, lse, mixed, mid, act, slope, final, final_low,
-        normed, mask, send, recv, w_sem, save_sem, send_sem, recv_sem,
-    ) = refs[saved_count:]
+        full_ref, guest_full, guest_shard, rows_out,
+        w_qkv, w_out, w_up, w_down, hid, qkv, lse, mixed, mid, act, slope, final,
+        rows_ref, inner_all, final_low, given, normed, mask, send, recv,
+        w_sem, save_sem, send_sem, recv_sem, local_sem, go_sem, guest_sem, push_sem, push_recv, given_sem, small_sem, inner_sem,
+        sax, rax, sau, rau, sad, rad, sbx, rbx, sbu, rbu, sbd, rbd,
+    ) = refs[8:]
     layers, micro, tokens, width = hid.shape
+    head_width, hidden_width = out_in.shape[2], up_in.shape[2]
     section = lax.axis_index("section")
+    place = lax.axis_index("fsdp")
+    count = 2 * line
+    shard_rows = width // count
+    z = place // 2
+    x = lax.rem(place, 2)
     partner = {"tensor": 1 - lax.axis_index("tensor")}
-
-    @pl.when(section == tick)
+    other = {"section": 1 - section}
+    to_x = {"fsdp": z * 2 + 1 - x}
+    to_x_other = {"section": 1 - section, "fsdp": z * 2 + 1 - x}
+    has_up = z < line - 1
+    has_down = z > 0
+    to_up = {"fsdp": jnp.minimum(z + 1, line - 1) * 2 + x}
+    to_down = {"fsdp": jnp.maximum(z - 1, 0) * 2 + x}
+    ends = (0, 3 * head_width, 4 * head_width, 4 * head_width + hidden_width, 4 * head_width + 2 * hidden_width)
+    cols = ends[4]
+    cols_a = cols - X_FIRST_COLS
+    span_a = pl.ds(0, cols_a)
+    span_b = pl.ds(cols_a, X_FIRST_COLS)
+    last = layers - 1
+
+    barrier = pltpu.get_barrier_semaphore()
+    for peer in (partner, other, to_x_other):
+        pl.semaphore_signal(barrier, inc=1, device_id=peer, device_id_type=MESH)
+    for turn in range(1, count):
+        peer = {"fsdp": lax.rem(place + turn, count)}
+        pl.semaphore_signal(barrier, inc=1, device_id=peer, device_id_type=MESH)
+    pl.semaphore_wait(barrier, count + 2)
+
+    small_copies = []
+    if aligned:
+        mine = pl.ds(pl.multiple_of(place * shard_rows, shard_rows), shard_rows)
+        inner_mine = pl.ds(pl.multiple_of(place * 3 * shard_rows, 3 * shard_rows), 3 * shard_rows)
+        rows_ref[:, :, mine] = small_ref[...]
+        inner_all[:, :, inner_mine] = inner_ref[...]
+        for turn in range(1, count):
+            peer = {"fsdp": lax.rem(place + turn, count)}
+            for source, target, sems in (
+                (small_ref, rows_ref.at[:, :, mine], small_sem), (inner_ref, inner_all.at[:, :, inner_mine], inner_sem),
+            ):
+                copy = pltpu.make_async_remote_copy(
+                    src_ref=source, dst_ref=target, send_sem=sems.at[0, turn], recv_sem=sems.at[1, turn],
+                    device_id=peer, device_id_type=MESH,
+                )
+                copy.start()
+                small_copies.append(copy)
+    else:
+        rows_ref[...] = small_ref[...]
+        inner_all[...] = inner_ref[...]
+
+    def spot(layer, row_z, row_x, span):
+        start = pl.multiple_of((row_z * 2 + row_x) * shard_rows, shard_rows)
+        target = guest_full if layer is None else full_ref.at[layer]
+        return target.at[pl.ds(start, shard_rows), span]
+
+    def pieces(layer, span):
+        if layer is None:
+            return [(guest_shard.at[:, span], span)]
+        if span is span_b:
+            return [(down_in.at[layer, :, pl.ds(hidden_width - X_FIRST_COLS, X_FIRST_COLS)], span)]
+        return [
+            (qkv_in.at[layer], pl.ds(ends[0], 3 * head_width)),
+            (out_in.at[layer], pl.ds(ends[1], head_width)),
+            (up_in.at[layer], pl.ds(ends[2], hidden_width)),
+            (down_in.at[layer, :, pl.ds(0, hidden_width - X_FIRST_COLS)], pl.ds(ends[3], hidden_width - X_FIRST_COLS)),
+        ]
+
+    def remote(source, target, send_sem, recv_sem, device):
+        return pltpu.make_async_remote_copy(
+            src_ref=source, dst_ref=target, send_sem=send_sem, recv_sem=recv_sem, device_id=device, device_id_type=MESH,
+        )
+
+    def always(condition, action):
+        if condition is None:
+            action()
+        else:
+            pl.when(condition)(action)
+
+    def gather(served):
+        finish = []
+
+        def launch(layer, row_z, row_x, span, send_sem, recv_sem, device, condition=None, fresh=False):
+            whole = spot(layer, row_z, row_x, span)
+            if layer is None and device is to_x and span is span_a:
+                device = to_x_other
+
+                def landing(part):
+                    start = pl.multiple_of((row_z * 2 + row_x) * shard_rows, shard_rows)
+                    return full_ref.at[last, pl.ds(start, shard_rows), part]
+            else:
+
+                def landing(part):
+                    return spot(layer, row_z, row_x, part)
+
+            def begin():
+                for source, part in pieces(layer, span) if fresh else [(whole, span)]:
+                    remote(source, landing(part), send_sem, recv_sem, device).start()
+
+            always(condition, begin)
+            finish.append((remote(whole, whole, send_sem, recv_sem, device), condition))
+
+        def arrive(layer, row_z, row_x, span, sem):
+            remote(spot(layer, row_z, row_x, span), spot(layer, row_z, row_x, span), sem, sem, to_x).wait_recv()
+
+        def deliver(layer, row_z, row_x, half, condition=None):
+            if layer is not None:
+                return
+            span = (span_a, span_b)[half]
+            start = pl.multiple_of((row_z * 2 + row_x) * shard_rows, shard_rows)
+            index = row_z * 2 + row_x
+            copy = remote(
+                spot(None, row_z, row_x, span), full_ref.at[last, pl.ds(start, shard_rows), span],
+                push_sem.at[index, half], push_recv.at[index, half], other,
+            )
+            always(condition, copy.start)
+            finish.append((copy, condition))
+
+        for layer in served:
+            s = 2 if layer is None else layer
+            launch(layer, z, x, span_b, sbx.at[s], rbx.at[s], to_x, None, True)
+            launch(layer, z, x, span_a, sau.at[s, 0], rau.at[s, 0], to_up, has_up, True)
+            launch(layer, z, x, span_a, sad.at[s, 0], rad.at[s, 0], to_down, has_down, True)
+            launch(layer, z, x, span_a, sax.at[s, 0], rax.at[s, 0], to_x, None, True)
+            launch(layer, z, x, span_b, sbu.at[s, 0, 0], rbu.at[s, 0, 0], to_up, has_up, True)
+            launch(layer, z, x, span_b, sbd.at[s, 0, 0], rbd.at[s, 0, 0], to_down, has_down, True)
+        for layer in served:
+            s = 2 if layer is None else layer
+            arrive(layer, z, 1 - x, span_b, rbx.at[s])
+            launch(layer, z, 1 - x, span_b, sbu.at[s, 0, 1], rbu.at[s, 0, 1], to_up, has_up)
+            launch(layer, z, 1 - x, span_b, sbd.at[s, 0, 1], rbd.at[s, 0, 1], to_down, has_down)
+            deliver(layer, z, 1 - x, 1)
+        for hop in range(line - 1):
+            for layer in served:
+                s = 2 if layer is None else layer
+                below, above = z - 1 - hop >= 0, z + 1 + hop < line
+                row_below, row_above = jnp.maximum(z - 1 - hop, 0), jnp.minimum(z + 1 + hop, line - 1)
+                for live, row, sa, ra, sb, rb, number, onward, device in (
+                    (below, row_below, sau, rau, sbu, rbu, 1 + hop, has_up, to_up),
+                    (above, row_above, sad, rad, sbd, rbd, line + hop, has_down, to_down),
+                ):
+                    pl.when(live)(functools.partial(arrive, layer, row, x, span_a, ra.at[s, hop]))
+                    launch(layer, row, x, span_a, sax.at[s, number], rax.at[s, number], to_x, live)
+                    if hop + 1 < line - 1:
+                        launch(layer, row, x, span_a, sa.at[s, hop + 1], ra.at[s, hop + 1], device, live & onward)
+                    deliver(layer, row, x, 0, live)
+                    for side, row_x in ((0, x), (1, 1 - x)):
+                        pl.when(live)(functools.partial(arrive, layer, row, row_x, span_b, rb.at[s, hop, side]))
+                        if hop + 1 < line - 1:
+                            launch(
+                                layer, row, row_x, span_b, sb.at[s, hop + 1, side], rb.at[s, hop + 1, side], device,
+                                live & onward,
+                            )
+                        deliver(layer, row, row_x, 1, live)
+        for layer in served:
+            if layer is not None:
+                await_x(layer, layer)
+        return finish
+
+    def await_x(layer, s):
+        for hop in range(line):
+            for row, number, live in (
+                (z - hop, hop, z - hop >= 0), (z + hop, line - 1 + hop, z + hop < line),
+            )[: 2 if hop else 1]:
+                row = jnp.clip(row, 0, line - 1)
+                whole = spot(layer, row, 1 - x, span_a)
+                pl.when(live)(remote(whole, whole, rax.at[s, number], rax.at[s, number], to_x).wait_recv)
+
+    def close(finish):
+        for copy, condition in finish:
+            always(condition, copy.wait_send)
+
+    own_copies = []
+    for layer in range(layers):
+        for span in (span_a, span_b):
+            for source, part in pieces(layer, span):
+                copy = pltpu.make_async_copy(source, spot(layer, z, x, part), local_sem.at[layer, len(own_copies) % 5])
+                copy.start()
+                own_copies.append(copy)
+    guest_copies = []
+    for number, (source, part) in enumerate(pieces(last, span_a) + pieces(last, span_b)):
+        guest_copies.append(remote(source, guest_shard.at[:, part], guest_sem.at[0, number], guest_sem.at[1, number], other))
+
+    def fetch(layer, index):
+        buffer = (w_qkv, w_out, w_up, w_down)[index]
+        return pltpu.make_async_copy(
+            full_ref.at[layer, :, pl.ds(ends[index], ends[index + 1] - ends[index])],
+            buffer.at[layer],
+            w_sem.at[layer, index],
+        )
+
+    @pl.when(section == 1)
     def _():
-        ends = (0, 3 * head_width, 4 * head_width, 4 * head_width + hidden_width, 4 * head_width + 2 * hidden_width)
-
-        def fetch(layer, index):
-            buffer = (w_qkv, w_out, w_up, w_down)[index]
-            return pltpu.make_async_copy(
-                full_ref.at[layer, :, pl.ds(ends[index], ends[index + 1] - ends[index])],
-                buffer.at[layer],
-                w_sem.at[layer, index],
-            )
-
+        for copy in guest_copies:
+            copy.start()
+
+    @pl.when(section == 0)
+    def _():
+        finish = gather(list(range(layers)))
+        pl.semaphore_signal(go_sem, inc=1, device_id=other, device_id_type=MESH)
+        for copy in own_copies:
+            copy.wait()
         for layer in range(layers):
             for index in range(4):
                 fetch(layer, index).start()
-        barrier = pltpu.get_barrier_semaphore()
-        pl.semaphore_signal(barrier, inc=1, device_id=partner, device_id_type=MESH)
-        pl.semaphore_wait(barrier, 1)
+        close(finish)
+
+    @pl.when(section == 1)
+    def _():
+        pl.semaphore_wait(go_sem, 1)
+        finish = gather(list(range(last)))
+        pl.semaphore_signal(go_sem, inc=1, device_id=other, device_id_type=MESH)
+        for copy in own_copies:
+            copy.wait()
+        for layer in range(last):
+            for index in range(4):
+                fetch(layer, index).start()
+        close(finish)
+
+    for copy in small_copies:
+        copy.wait()
+
+    if True:
+        for part in range(micro):
+            mask[part] = allowed_bias(ids_ref[part], tokens)
+
+        hand_over = pltpu.make_async_remote_copy(
+            src_ref=final_low, dst_ref=given, send_sem=given_sem.at[0], recv_sem=given_sem.at[1],
+            device_id=other, device_id_type=MESH,
+        )
+
+        @pl.when(section == 0)
+        def _():
+            for part in range(micro):
+                hid[0, part] = h0_ref[part].astype(jnp.float32)
+
+        @pl.when(section == 1)
+        def _():
+            hand_over.wait_recv()
+            for part in range(micro):
+                hid[0, part] = given[part].astype(jnp.float32)
 
         def save(index, source, layer, part):
             return pltpu.make_async_copy(source.at[layer, part], outs[index].at[layer, part], save_sem.at[index, layer, part])
@@ -285,14 +307,6 @@
                 device_id_type=MESH,
             )
 
-        for part in range(micro):
-            col = ids_col_ref[part]
-            row = ids_row_ref[part]
-            one = lax.broadcasted_iota(jnp.int32, (tokens, tokens), 0)
-            two = lax.broadcasted_iota(jnp.int32, (tokens, tokens), 1)
-            allowed = ((col == row) & (col >= 0)) | (one == two)
-            mask[part] = jnp.where(allowed, 0.0, -1e30)
-
         def norm_rows(value, gain, shift):
             average = jnp.mean(value, axis=-1, keepdims=True)
             centred = value - average
@@ -314,13 +328,6 @@
                         joined(layer - 1, 1, part, span) + rows_ref[layer - 1, 5:6]
                     )
 
-            @pl.when(layer == 0)
-            def _():
-                @pl.loop(0, tokens, step=32)
-                def _(start):
-                    span = pl.ds(pl.multiple_of(start, 32), 32)
-                    hid[layer, part, span] = h0_ref[part, span].astype(jnp.float32)
-
             @pl.loop(0, tokens, step=32)
             def _(start):
                 span = pl.ds(pl.multiple_of(start, 32), 32)
@@ -335,7 +342,9 @@
                 def _(start, piece=piece):
                     span = pl.ds(pl.multiple_of(piece * head_width + start, 256), 256)
                     value = jnp.dot(normed[...], w_qkv[layer, :, span], preferred_element_type=jnp.float32)
-                    value = (value + qkv_bias_ref[layer, :, span]).astype(jnp.bfloat16)
+                    if piece != 1:
+                        value = value + inner_all[layer, :, pl.ds(pl.multiple_of(piece // 2 * head_width + start, 256), 256)]
+                    value = value.astype(jnp.bfloat16)
                     if piece == 0:
                         value = value * jnp.asarray(1.0 / math.sqrt(HEAD_DIM), jnp.bfloat16)
                     qkv[layer, part, :, span] = value
@@ -393,7 +402,7 @@
             def _(start):
                 span = pl.ds(pl.multiple_of(start, 256), 256)
                 upward = jnp.dot(normed[...], w_up[layer, :, span], preferred_element_type=jnp.float32)
-                upward = upward + up_bias_ref[layer, :, span]
+                upward = upward + inner_all[layer, :, pl.ds(pl.multiple_of(2 * head_width + start, 256), 256)]
                 phi = 0.5 + 0.5 * lax.erf(upward * math.sqrt(0.5))
                 density = jnp.exp(-0.5 * upward * upward) * (1.0 / math.sqrt(2.0 * math.pi))
                 act[layer, part, :, span] = (upward * phi).astype(jnp.bfloat16)
@@ -415,6 +424,21 @@
 
         @pl.loop(0, layers)
         def _(layer):
+            @pl.when((section == 1) & (layer == last))
+            def _():
+                await_x(last, 2)
+                for row_z in range(line):
+                    for row_x in range(2):
+                        for half in range(2):
+                            live = (row_x == x) & (row_z != z) if half == 0 else (row_z * 2 + row_x != place)
+                            index = row_z * 2 + row_x
+                            whole = spot(last, row_z, row_x, (span_a, span_b)[half])
+                            pl.when(live)(
+                                remote(whole, whole, push_recv.at[index, half], push_recv.at[index, half], other).wait_recv
+                            )
+                for index in range(4):
+                    fetch(last, index).start()
+
             @pl.loop(0, micro)
             def _(part):
                 attention_stage(layer, part)
@@ -422,8 +446,6 @@
             @pl.loop(0, micro)
             def _(part):
                 mlp_stage(layer, part)
-
-        last = layers - 1
 
         @pl.loop(0, micro)
         def _(part):
@@ -436,12 +458,23 @@
                 final[part, span] = value
                 final_low[part, span] = value.astype(jnp.bfloat16)
 
-        ending = [
-            pltpu.make_async_copy(final, outs[7], save_sem.at[7, 0, 0]),
-            pltpu.make_async_copy(final_low, outs[8], save_sem.at[8, 0, 0]),
-        ]
-        for copy in ending:
-            copy.start()
+        rows_out[...] = rows_ref[...]
+        ending = pltpu.make_async_copy(final, outs[7], save_sem.at[7, 0, 0])
+        ending.start()
+
+        @pl.when(section == 0)
+        def _():
+            hand_over.start()
+            for copy in guest_copies:
+                copy.wait_recv()
+            pl.semaphore_wait(go_sem, 1)
+            close(gather([None]))
+            hand_over.wait_send()
+
+        @pl.when(section == 1)
+        def _():
+            for copy in guest_copies:
+                copy.wait_send()
 
         @pl.loop(0, layers)
         def _(layer):
@@ -452,8 +485,7 @@
                 for index, source in saves:
                     save(index, source, layer, part).wait()
 
-        for copy in ending:
-            copy.wait()
+        ending.wait()
 
 
 def saved_shapes(layers, micro, tokens, width, head_width, hidden_width):
@@ -468,53 +500,89 @@
         ((layers, micro, tokens, hidden_width), low),
         ((layers, micro, tokens, hidden_width), low),
         ((micro, tokens, width), full),
-        ((micro, tokens, width), low),
     )
 
 
-def forward(tick, h0, ids, params, full, previous, head_width, hidden_width):
-    rows, qkv_bias, up_bias = params
-    layers, width = full.shape[:2]
+def forward(h0, ids, small, inner, qkv_in, out_in, up_in, down_in):
+    layers, shard_rows = qkv_in.shape[:2]
+    head_width, hidden_width = out_in.shape[2], up_in.shape[2]
+    count = lax.axis_size("fsdp")
+    line = count // 2
+    width = shard_rows * count
     micro, tokens = ids.shape
     shapes = saved_shapes(layers, micro, tokens, width, head_width, hidden_width)
+    cols = 4 * head_width + 2 * hidden_width
+    low, wide = jnp.bfloat16, jnp.float32
+    outs = shapes + (
+        ((layers, width, cols), low),
+        ((width, cols), low),
+        ((shard_rows, cols), low),
+        ((layers, 8, width), wide),
+    )
     vmem = pl.BlockSpec(memory_space=pltpu.VMEM)
     hbm = pl.BlockSpec(memory_space=pl.ANY)
     dma = pltpu.SemaphoreType.DMA
-    low = jnp.bfloat16
-    aliased = () if previous is None else tuple(previous)
+    aligned = shard_rows % LANES == 0
+    if not aligned:
+        small = lax.all_gather(small, "fsdp", axis=2, tiled=True)
+        inner = lax.all_gather(inner, "fsdp", axis=2, tiled=True)
+    sets = layers + 1
     return pl.pallas_call(
-        functools.partial(forward_kernel, tick, previous is not None, head_width, hidden_width),
-        out_shape=[jax.ShapeDtypeStruct(shape, kind) for shape, kind in shapes],
-        in_specs=[vmem] * 6 + [hbm] * (1 + len(aliased)),
-        out_specs=[hbm] * len(shapes),
-        input_output_aliases={7 + number: number for number in range(len(aliased))},
+        functools.partial(forward_kernel, line, aligned),
+        out_shape=[jax.ShapeDtypeStruct(shape, kind) for shape, kind in outs],
+        in_specs=[vmem] * 4 + [hbm] * 4,
+        out_specs=[hbm] * (len(outs) - 1) + [vmem],
         scratch_shapes=[
             pltpu.VMEM((layers, width, 3 * head_width), low),
             pltpu.VMEM((layers, width, head_width), low),
             pltpu.VMEM((layers, width, hidden_width), low),
             pltpu.VMEM((layers, width, hidden_width), low),
             *(pltpu.VMEM(shape, kind) for shape, kind in shapes),
+            pltpu.VMEM((layers, 8, width), wide),
+            pltpu.VMEM((layers, 1, 3 * width), wide),
+            pltpu.VMEM((micro, tokens, width), low),
+            pltpu.VMEM((micro, tokens, width), low),
             pltpu.VMEM((tokens, width), low),
-            pltpu.VMEM((micro, tokens, tokens), jnp.float32),
+            pltpu.VMEM((micro, tokens, tokens), wide),
             pltpu.VMEM((layers, 2, micro, tokens, width), low),
             pltpu.VMEM((layers, 2, micro, tokens, width), low),
             dma((layers, 4)),
             dma((len(shapes), layers, micro)),
             dma((layers, 2, micro)),
             dma((layers, 2, micro)),
+            dma((layers, 5)),
+            pltpu.SemaphoreType.REGULAR,
+            dma((2, 5)),
+            dma((count, 2)),
+            dma((count, 2)),
+            dma((2,)),
+            dma((2, count)),
+            dma((2, count)),
+            dma((sets, 2 * line - 1)),
+            dma((sets, 2 * line - 1)),
+            dma((sets, line - 1)),
+            dma((sets, line - 1)),
+            dma((sets, line - 1)),
+            dma((sets, line - 1)),
+            dma((sets,)),
+            dma((sets,)),
+            dma((sets, line - 1, 2)),
+            dma((sets, line - 1, 2)),
+            dma((sets, line - 1, 2)),
+            dma((sets, line - 1, 2)),
         ],
         compiler_params=pltpu.CompilerParams(
-            collective_id=2 + tick, has_side_effects=True, vmem_limit_bytes=62 << 20
+            collective_id=2, has_side_effects=True, vmem_limit_bytes=63 << 20
         ),
         name="forward",
-    )(h0, ids[:, :, None], ids[:, None, :], rows, qkv_bias, up_bias, full, *aliased)
+    )(h0, ids[:, None, :], small, inner, qkv_in, out_in, up_in, down_in)
 
 
 SLOTS = 2
 
 
 def backward_kernel(
-    line, aligned, head_width, hidden_width, g0_ref, ids_col_ref, ids_row_ref, rows_ref, full_ref, *refs
+    line, aligned, head_width, hidden_width, g0_ref, ids_ref, rows_ref, full_ref, *refs
 ):
     saves = refs[:7]
     (
@@ -588,12 +656,7 @@
         small[...] = jnp.zeros_like(small)
         inner_sum[...] = jnp.zeros_like(inner_sum)
         for part in range(micro):
-            col = ids_col_ref[part]
-            row = ids_row_ref[part]
-            one = lax.broadcasted_iota(jnp.int32, (tokens, tokens), 0)
-            two = lax.broadcasted_iota(jnp.int32, (tokens, tokens), 1)
-            allowed = ((col == row) & (col >= 0)) | (one == two)
-            mask[part] = jnp.where(allowed, 0.0, -1e30)
+            mask[part] = allowed_bias(ids_ref[part], tokens)
 
         @pl.when(section == 1)
         def _():
@@ -1039,8 +1102,7 @@
         ending.wait()
 
 
-def backward(g0, ids, params, full, saves, head_width, hidden_width):
-    rows, qkv_bias, up_bias = params
+def backward(g0, ids, rows, full, saves, head_width, hidden_width):
     layers, width, cols = full.shape
     micro, tokens = ids.shape
     count = lax.axis_size("fsdp")
@@ -1067,7 +1129,7 @@
     return pl.pallas_call(
         functools.partial(backward_kernel, line, aligned, head_width, hidden_width),
         out_shape=[jax.ShapeDtypeStruct(shape, kind) for shape, kind in outs],
-        in_specs=[vmem] * 4 + [hbm] * 8,
+        in_specs=[vmem] * 3 + [hbm] * 8,
         out_specs=[hbm, vmem, vmem] + [hbm] * 5,
         scratch_shapes=[
             pltpu.VMEM((width, 3 * head_width), low),
@@ -1118,7 +1180,7 @@
             collective_id=4, has_side_effects=True, vmem_limit_bytes=63 << 20
         ),
         name="backward",
-    )(g0, ids[:, :, None], ids[:, None, :], rows, full, *saves)
+    )(g0, ids[:, None, :], rows, full, *saves)
 
 
 def unpack_grads(full, head_width, hidden_width):
@@ -1147,16 +1209,15 @@
     section = lax.axis_index("section")
     count = lax.axis_size("fsdp")
     head_width, hidden_width = out_weight.shape[2], up_weight.shape[2]
-    shard = pack_shard(qkv_weight, out_weight, up_weight, down_weight, norm_gains, biases, inner_bias)
-    full = gather_weights(shard)
-    params = unpack_params(full, head_width, count)
-    saved = forward(0, block_input, image_ids, params, full, None, head_width, hidden_width)
-    received = shifted(saved[8], "section", 1)
-    saved = forward(1, received, image_ids, params, full, saved, head_width, hidden_width)
+    layers, rows = qkv_weight.shape[:2]
+    small = jnp.concatenate([norm_gains, biases, jnp.zeros_like(norm_gains)], axis=1).astype(jnp.float32)
+    *saved, full, _, _, row_values = forward(
+        block_input, image_ids, small, inner_bias.astype(jnp.float32),
+        qkv_weight.reshape(layers, rows, -1), out_weight, up_weight, down_weight,
+    )
     summed, small, inner, input_grad = backward(
-        cotangent, image_ids, params, full, saved[:7], head_width, hidden_width
+        cotangent, image_ids, row_values, full, saved[:7], head_width, hidden_width
     )[:4]
-    rows = qkv_weight.shape[1]
     if small.shape[2] != rows:
         place = lax.axis_index("fsdp")
         small = lax.dynamic_slice_in_dim(small, place * rows, rows, 2)

time: 703 us -> 677 us (0.963)
  starting transfers between devices: 70.3 us -> 0 us
  Pallas kernels: 596 us -> 655 us
  local copies, waits for them, and re-layouts: 28.3 us -> 16.7 us
    pallas_call x3 -> x1, Pallas kernels: 207 us -> 292 us  [forward(): pl.pallas_call(functools.partial(forward_kernel, line, aligned), out_shap...]
    ppermute x1 -> x0, starting transfers between devices: 70.3 us -> none  [shifted(): lax.ppermute(value, axis, [(source, source + steps) for source in range(i...]
    pallas_call x1, Pallas kernels: 389 us -> 362 us  [backward(): pl.pallas_call(functools.partial(backward_kernel, line, aligned, head_wid...]
    unnamed x36 -> x15, local copies, waits for them, and re-layouts: 12.2 us -> 3.72 us
  transfers between devices with their start and end apart: 1 -> 0, of which waited for: 1 -> 0; matrix products, arithmetic and copies ran while one was open for 0% -> 0% of each run, Pallas kernels for 0% -> 0%
where the time goes in v4:
time: 677 us; the launch traced here: 676 us
  Pallas kernels  655 us (97%)
  local copies, waits for them, and re-layouts  16.7 us (2%)
    pallas_call x1, Pallas kernels, backward(): pl.pallas_call(functools.partial(backward_kernel, line, aligned, head_wid...  362 us
    pallas_call x1, Pallas kernels, forward(): pl.pallas_call(functools.partial(forward_kernel, line, aligned), out_shap...  292 us

profile of v4, /device:TPU:0, one launch (start us, length us, event | category | flops | bytes accessed | tf_op | source)
XLA Modules:
  0.0 675.7 jit_solution(8557195330382757802)
XLA Ops:
  0.6 0.0 copy-start.5
  0.6 0.0 copy-start.3
  0.7 0.0 copy-start.4
  0.7 1.3 broadcast_in_dim.10.ids_ref
  1.9 1.5 copy.26
  3.5 1.2 copy.28.qkv_in
  4.6 0.1 pad.2.clone
  4.7 0.0 copy-done.5
  4.7 0.0 copy-done.3
  4.7 0.7 maximum_convert_fusion.small_ref
  5.4 0.0 copy-done.4
  5.4 0.6 copy.27.inner_ref
  6.0 292.3 %forward.1 = (f32[2,2,224,1024]{3,2,1,0:T(8,128)}, bf16[2,2,224,1536]{3,2,1,0:T(8,128)(2,1)}, f32[2,2,224,8]{3,2,1,0:T(8,128)}, bf16[2,2,224,512]{3,2,1,0:T(8,12...) custom-call(bf16[2,224,1024]{2,1,0:T(8,128)(2,1)} %h0_ref.1, ...), custom_call_target="tpu_custom_call" | custom-call | tf_op jit(solution)/shard_map/forward/pallas_call | solution.py:530
  298.3 362.2 %backward.1 = (f32[2,128,6144]{2,1,0:T(8,128)}, f32[2,8,128]{2,1,0:T(8,128)}, f32[2,1,384]{2,1,0:T(1,128)}, f32[2,224,1024]{2,1,0:T(8,128)}, bf16[2,1024,6144]{2...) custom-call(bf16[2,224,1024]{2,1,0:T(8,128)(2,1)} %g0_ref.1, ...), custom_call_target="tpu_custom_call" | custom-call | tf_op jit(solution)/shard_map/backward/pallas_call | solution.py:1129
  660.5 1.5 slice.18
  662.0 0.5 copy.29
  662.5 1.6 copy.30
  664.1 0.0 copy-start
  664.1 4.9 fusion
  669.0 0.0 copy-done
  669.0 0.0 copy-start.1
  669.0 0.0 copy-start.2
  669.0 3.1 select_bitcast_fusion
  672.1 1.9 slice.19
  673.9 0.0 copy-done.1
  673.9 0.6 slice.23
  674.5 0.6 slice.22
  675.1 0.0 copy-done.2
  675.1 0.6 copy.32
  (1 shorter events, 0.0 us)
Async XLA Ops:
  0.6 4.1 copy-start.5
  0.6 4.1 copy-start.3
  0.7 4.7 copy-start.4
  664.1 4.9 copy-start
  669.0 4.9 copy-start.1
  669.0 6.1 copy-start.2

commit v5 on v4

v5 whole, which is shorter than its diff:
```python
import functools
import math

import jax
import jax.numpy as jnp
from jax import lax
from jax.experimental import pallas as pl
from jax.experimental.pallas import tpu as pltpu
from jax.sharding import PartitionSpec as P

HEAD_DIM = 64
EPSILON = 1e-06


MESH = pl.DeviceIdType.MESH


def contract_last(left, right):
    return lax.dot_general(
        left, right, (((1,), (1,)), ((), ())), preferred_element_type=jnp.float32
    )


def contract_rows(left, right):
    return lax.dot_general(
        left, right, (((0,), (0,)), ((), ())), preferred_element_type=jnp.float32
    )


LANES = 128
X_FIRST_COLS = 1024
GUEST_X_FIRST_COLS = 256


def allowed_bias(ids_row, tokens):
    spread = jnp.broadcast_to(ids_row, (tokens, tokens))
    mirror = jnp.transpose(spread)
    one = lax.broadcasted_iota(jnp.int32, (tokens, tokens), 0)
    two = lax.broadcasted_iota(jnp.int32, (tokens, tokens), 1)
    allowed = ((mirror == spread) & (spread >= 0)) | (one == two)
    return jnp.where(allowed, 0.0, -1e30)


def forward_part(line, aligned, h0_ref, ids_ref, gains_in, shifts_in, inner_in, qkv_in, out_in, up_in, down_in, refs):
    (
        full_ref, guest_full, guest_shard,
        w_qkv, w_out, w_up, w_down, hid, qkv, lse, mixed, mid, act, slope,
        small_ref, inner_ref, own_shard, rows_ref, inner_all, final_low, given, normed, mask, send, recv,
        w_sem, h0_sem, send_sem, recv_sem, local_sem, go_sem, guest_sem, push_sem, push_recv, given_sem, small_sem, inner_sem,
        sax, rax, sau, rau, sad, rad, sbx, rbx, sbu, rbu, sbd, rbd,
    ) = refs
    layers, micro, tokens, width = hid.shape
    head_width, hidden_width = out_in.shape[2], up_in.shape[2]
    section = lax.axis_index("section")
    place = lax.axis_index("fsdp")
    count = 2 * line
    shard_rows = width // count
    z = place // 2
    x = lax.rem(place, 2)
    partner = {"tensor": 1 - lax.axis_index("tensor")}
    other = {"section": 1 - section}
    to_x = {"fsdp": z * 2 + 1 - x}
    to_x_other = {"section": 1 - section, "fsdp": z * 2 + 1 - x}
    has_up = z < line - 1
    has_down = z > 0
    to_up = {"fsdp": jnp.minimum(z + 1, line - 1) * 2 + x}
    to_down = {"fsdp": jnp.maximum(z - 1, 0) * 2 + x}
    ends = (0, 3 * head_width, 4 * head_width, 4 * head_width + hidden_width, 4 * head_width + 2 * hidden_width)
    cols = ends[4]
    guest_cols = cols // 3
    last = layers - 1

    first_copy = pltpu.make_async_copy(h0_ref, given, h0_sem.at[0])
    pl.when(section == 0)(first_copy.start)
    takes = []
    for layer in range(layers):
        for number, (source, start, wide) in enumerate((
            *((qkv_in.at[layer, piece], piece * head_width, head_width) for piece in range(3)),
            (out_in.at[layer], ends[1], head_width), (up_in.at[layer], ends[2], hidden_width),
            (down_in.at[layer], ends[3], hidden_width),
        )):
            take = pltpu.make_async_copy(source, own_shard.at[layer, :, pl.ds(start, wide)], local_sem.at[layer, number])
            take.start()
            takes.append(take)
    barrier = pltpu.get_barrier_semaphore()
    for peer in (partner, other, to_x_other):
        pl.semaphore_signal(barrier, inc=1, device_id=peer, device_id_type=MESH)
    for turn in range(1, count):
        peer = {"fsdp": lax.rem(place + turn, count)}
        pl.semaphore_signal(barrier, inc=1, device_id=peer, device_id_type=MESH)
    pl.semaphore_wait(barrier, count + 2)

    small_ref[:, 0:2] = gains_in[...].astype(jnp.float32)
    small_ref[:, 2:6] = shifts_in[...].astype(jnp.float32)
    small_ref[:, 6:8] = jnp.zeros_like(small_ref[:, 6:8])
    inner_ref[...] = inner_in[...].astype(jnp.float32)
    small_copies = []
    if aligned:
        mine = pl.ds(pl.multiple_of(place * shard_rows, shard_rows), shard_rows)
        inner_mine = pl.ds(pl.multiple_of(place * 3 * shard_rows, 3 * shard_rows), 3 * shard_rows)
        rows_ref[:, :, mine] = small_ref[...]
        inner_all[:, :, inner_mine] = inner_ref[...]
        for turn in range(1, count):
            peer = {"fsdp": lax.rem(place + turn, count)}
            for source, target, sems in (
                (small_ref, rows_ref.at[:, :, mine], small_sem), (inner_ref, inner_all.at[:, :, inner_mine], inner_sem),
            ):
                copy = pltpu.make_async_remote_copy(
                    src_ref=source, dst_ref=target, send_sem=sems.at[0, turn], recv_sem=sems.at[1, turn],
                    device_id=peer, device_id_type=MESH,
                )
                copy.start()
                small_copies.append(copy)
    else:
        rows_ref[...] = small_ref[...]
        inner_all[...] = inner_ref[...]

    def halves(unit):
        if unit < layers:
            return pl.ds(0, cols - X_FIRST_COLS), pl.ds(cols - X_FIRST_COLS, X_FIRST_COLS)
        base, middle = (unit - layers) * guest_cols, guest_cols - GUEST_X_FIRST_COLS
        return pl.ds(base, middle), pl.ds(base + middle, GUEST_X_FIRST_COLS)

    def spot(unit, row_z, row_x, span):
        start = pl.multiple_of((row_z * 2 + row_x) * shard_rows, shard_rows)
        target = full_ref.at[unit] if unit < layers else guest_full
        return target.at[pl.ds(start, shard_rows), span]

    def pieces(unit, half):
        span = halves(unit)[half]
        return [((own_shard.at[unit] if unit < layers else guest_shard).at[:, span], span)]

    def remote(source, target, send_sem, recv_sem, device):
        return pltpu.make_async_remote_copy(
            src_ref=source, dst_ref=target, send_sem=send_sem, recv_sem=recv_sem, device_id=device, device_id_type=MESH,
        )

    def always(condition, action):
        if condition is None:
            action()
        else:
            pl.when(condition)(action)

    def gather(waves, nearly):
        finish = []

        def launch(unit, row_z, row_x, half, send_sem, recv_sem, device, condition=None, fresh=False):
            span = halves(unit)[half]
            whole = spot(unit, row_z, row_x, span)
            direct = unit >= layers and device is to_x and half == 0
            start = pl.multiple_of((row_z * 2 + row_x) * shard_rows, shard_rows)

            def landing(part):
                return full_ref.at[last, pl.ds(start, shard_rows), part] if direct else spot(unit, row_z, row_x, part)

            target = to_x_other if direct else device

            def begin():
                for source, part in pieces(unit, half) if fresh else [(whole, span)]:
                    remote(source, landing(part), send_sem, recv_sem, target).start()

            always(condition, begin)
            finish.append((remote(whole, whole, send_sem, recv_sem, target), condition))

        def arrive(unit, row_z, row_x, half, sem):
            whole = spot(unit, row_z, row_x, halves(unit)[half])
            remote(whole, whole, sem, sem, to_x).wait_recv()

        def deliver(unit, row_z, row_x, half, condition=None):
            if unit < layers:
                return
            span = halves(unit)[half]
            start = pl.multiple_of((row_z * 2 + row_x) * shard_rows, shard_rows)
            index = row_z * 2 + row_x
            copy = remote(
                spot(unit, row_z, row_x, span), full_ref.at[last, pl.ds(start, shard_rows), span],
                push_sem.at[unit - layers, index, half], push_recv.at[unit - layers, index, half], other,
            )
            always(condition, copy.start)
            finish.append((copy, condition))

        def first_sends(wave):
            for u in wave:
                launch(u, z, x, 1, sbx.at[u], rbx.at[u], to_x, None, True)
                launch(u, z, x, 0, sau.at[u, 0], rau.at[u, 0], to_up, has_up, True)
                launch(u, z, x, 0, sad.at[u, 0], rad.at[u, 0], to_down, has_down, True)
                launch(u, z, x, 1, sbu.at[u, 0, 0], rbu.at[u, 0, 0], to_up, has_up, True)
                launch(u, z, x, 1, sbd.at[u, 0, 0], rbd.at[u, 0, 0], to_down, has_down, True)

        def first_across(wave):
            for u in wave:
                launch(u, z, x, 0, sax.at[u, 0], rax.at[u, 0], to_x, None, True)

        first_sends(waves[0])
        first_across(waves[0])
        for number, wave in enumerate(waves):
            for u in wave:
                arrive(u, z, 1 - x, 1, rbx.at[u])
                launch(u, z, 1 - x, 1, sbu.at[u, 0, 1], rbu.at[u, 0, 1], to_up, has_up)
                launch(u, z, 1 - x, 1, sbd.at[u, 0, 1], rbd.at[u, 0, 1], to_down, has_down)
                deliver(u, z, 1 - x, 1)
            for hop in range(line - 1):
                if hop == line - 2 and number + 1 < len(waves):
                    first_sends(waves[number + 1])
                if hop == line - 2 and number + 1 == len(waves):
                    nearly()
                for u in wave:
                    below, above = z - 1 - hop >= 0, z + 1 + hop < line
                    row_below, row_above = jnp.maximum(z - 1 - hop, 0), jnp.minimum(z + 1 + hop, line - 1)
                    for live, row, sa, ra, sb, rb, place_in, onward, device in (
                        (below, row_below, sau, rau, sbu, rbu, 1 + hop, has_up, to_up),
                        (above, row_above, sad, rad, sbd, rbd, line + hop, has_down, to_down),
                    ):
                        pl.when(live)(functools.partial(arrive, u, row, x, 0, ra.at[u, hop]))
                        launch(u, row, x, 0, sax.at[u, place_in], rax.at[u, place_in], to_x, live)
                        if hop + 1 < line - 1:
                            launch(u, row, x, 0, sa.at[u, hop + 1], ra.at[u, hop + 1], device, live & onward)
                        deliver(u, row, x, 0, live)
                        for side, row_x in ((0, x), (1, 1 - x)):
                            pl.when(live)(functools.partial(arrive, u, row, row_x, 1, rb.at[u, hop, side]))
                            if hop + 1 < line - 1:
                                launch(
                                    u, row, row_x, 1, sb.at[u, hop + 1, side], rb.at[u, hop + 1, side], device, live & onward
                                )
                            deliver(u, row, row_x, 1, live)
            if number + 1 < len(waves):
                first_across(waves[number + 1])
        for wave in waves:
            for u in wave:
                if u < layers:
                    await_x(u)
        return finish

    def await_x(unit):
        for hop in range(line):
            for row, number, live in (
                (z - hop, hop, z - hop >= 0), (z + hop, line - 1 + hop, z + hop < line),
            )[: 2 if hop else 1]:
                whole = spot(unit, jnp.clip(row, 0, line - 1), 1 - x, halves(unit)[0])
                pl.when(live)(remote(whole, whole, rax.at[unit, number], rax.at[unit, number], to_x).wait_recv)

    def await_guest(third):
        unit = layers + third
        await_x(unit)
        for row_z in range(line):
            for row_x in range(2):
                for half in range(2):
                    live = (row_x == x) & (row_z != z) if half == 0 else (row_z * 2 + row_x != place)
                    index = row_z * 2 + row_x
                    whole = spot(unit, row_z, row_x, halves(unit)[half])
                    sem = push_recv.at[third, index, half]
                    pl.when(live)(remote(whole, whole, sem, sem, other).wait_recv)

    def close(finish):
        for copy, condition in finish:
            always(condition, copy.wait_send)

    for take in takes:
        take.wait()
    guest_copies = [remote(own_shard.at[last], guest_shard, guest_sem.at[0], guest_sem.at[1], other)]
    own_copies = [
        pltpu.make_async_copy(own_shard.at[layer], spot(layer, z, x, pl.ds(0, cols)), local_sem.at[layer, 6])
        for layer in range(layers)
    ]
    for copy in own_copies:
        copy.start()

    def fetch(layer, index):
        buffer = (w_qkv, w_out, w_up, w_down)[index]
        return pltpu.make_async_copy(
            full_ref.at[layer, :, pl.ds(ends[index], ends[index + 1] - ends[index])],
            buffer,
            w_sem.at[layer, index],
        )

    def give_way():
        pl.semaphore_signal(go_sem, inc=1, device_id=other, device_id_type=MESH)

    for copy in guest_copies:
        copy.start()
    thirds = [[layers + third] for third in range(3)]

    @pl.when(section == 0)
    def _():
        finish = gather([list(range(last))], give_way)
        for copy in own_copies:
            copy.wait()
        for layer in range(last):
            for index in range(4):
                fetch(layer, index).start()
        close(finish)

    @pl.when(section == 1)
    def _():
        for copy in guest_copies:
            copy.wait_recv()
        pl.semaphore_wait(go_sem, 1)
        finish = gather([sum(thirds, []), list(range(last))], give_way)
        for copy in own_copies:
            copy.wait()
        for layer in range(last):
            for index in range(4):
                fetch(layer, index).start()
        close(finish)

    for copy in small_copies:
        copy.wait()

    if True:
        for part in range(micro):
            mask[part] = allowed_bias(ids_ref[part : part + 1], tokens)

        hand_over = pltpu.make_async_remote_copy(
            src_ref=final_low, dst_ref=given, send_sem=given_sem.at[0], recv_sem=given_sem.at[1],
            device_id=other, device_id_type=MESH,
        )

        pl.when(section == 0)(first_copy.wait)
        pl.when(section == 1)(hand_over.wait_recv)
        for part in range(micro):
            hid[0, part] = given[pl.ds(part * tokens, tokens)].astype(jnp.float32)

        def exchange(stage, part):
            return pltpu.make_async_remote_copy(
                src_ref=send.at[stage, part],
                dst_ref=recv.at[stage, part],
                send_sem=send_sem.at[stage, part],
                recv_sem=recv_sem.at[stage, part],
                device_id=partner,
                device_id_type=MESH,
            )

        def norm_rows(value, gain, shift):
            average = jnp.mean(value, axis=-1, keepdims=True)
            centred = value - average
            spread = jnp.mean(centred * centred, axis=-1, keepdims=True)
            return centred * lax.rsqrt(spread + EPSILON) * gain + shift

        def joined(stage, part, span):
            return send[stage, part, span].astype(jnp.float32) + recv[stage, part, span].astype(jnp.float32)

        def attention_stage(layer, part):
            @pl.when(layer > 0)
            def _():
                exchange(1, part).wait_recv()

                @pl.loop(0, tokens, step=112)
                def _(start):
                    span = pl.ds(pl.multiple_of(start, 112), 112)
                    hid[layer, part, span] = mid[layer - 1, part, span] + (
                        joined(1, part, span) + rows_ref[layer - 1, 5:6]
                    )

            @pl.loop(0, tokens, step=112)
            def _(start):
                span = pl.ds(pl.multiple_of(start, 112), 112)
                normed[span] = norm_rows(hid[layer, part, span], rows_ref[layer, 0:1], rows_ref[layer, 2:3]).astype(jnp.bfloat16)

            @pl.when(part == 0)
            def _():
                fetch(layer, 0).wait()

            for piece in range(3):
                @pl.loop(0, head_width, step=512)
                def _(start, piece=piece):
                    span = pl.ds(pl.multiple_of(piece * head_width + start, 512), 512)
                    value = jnp.dot(normed[...], w_qkv[:, span], preferred_element_type=jnp.float32)
                    if piece != 1:
                        value = value + inner_all[layer, :, pl.ds(pl.multiple_of(piece // 2 * head_width + start, 512), 512)]
                    value = value.astype(jnp.bfloat16)
                    if piece == 0:
                        value = value * jnp.asarray(1.0 / math.sqrt(HEAD_DIM), jnp.bfloat16)
                    qkv[layer, part, :, span] = value

            lane = lax.broadcasted_iota(jnp.int32, (tokens, LANES), 1)
            tops = []
            for pair in range(head_width // LANES):
                q2 = qkv[layer, part, :, pair * LANES : (pair + 1) * LANES]
                k2 = qkv[layer, part, :, head_width + pair * LANES : head_width + (pair + 1) * LANES]
                v2 = qkv[layer, part, :, 2 * head_width + pair * LANES : 2 * head_width + (pair + 1) * LANES]
                halves = []
                for side in range(2):
                    live = (lane < HEAD_DIM) if side == 0 else (lane >= HEAD_DIM)
                    scores = contract_last(jnp.where(live, q2, jnp.zeros_like(q2)), k2) + mask[part]
                    top = jnp.max(scores, axis=-1, keepdims=True)
                    exponent = jnp.exp(scores - top)
                    total = jnp.sum(exponent, axis=-1, keepdims=True)
                    probs = (exponent * (1.0 / total)).astype(jnp.bfloat16)
                    halves.append(jnp.dot(probs, v2, preferred_element_type=jnp.float32))
                    head = 2 * pair + side
                    lse[layer, part, :, head : head + 1] = top + jnp.log(total)
                mixed[layer, part, :, pair * LANES : (pair + 1) * LANES] = jnp.where(
                    lane < HEAD_DIM, halves[0], halves[1]
                ).astype(jnp.bfloat16)

            @pl.when(part == 0)
            def _():
                fetch(layer, 1).wait()

            pl.when(layer > 0)(exchange(0, part).wait_send)

            @pl.loop(0, width, step=1024)
            def _(start):
                span = pl.ds(pl.multiple_of(start, 1024), 1024)
                value = contract_last(mixed[layer, part], w_out[span])
                send[0, part, :, span] = value.astype(jnp.bfloat16)

            exchange(0, part).start()

        def mlp_stage(layer, part):
            exchange(0, part).wait_recv()

            @pl.loop(0, tokens, step=112)
            def _(start):
                span = pl.ds(pl.multiple_of(start, 112), 112)
                middle = hid[layer, part, span] + (joined(0, part, span) + rows_ref[layer, 3:4])
                mid[layer, part, span] = middle
                normed[span] = norm_rows(middle, rows_ref[layer, 1:2], rows_ref[layer, 4:5]).astype(jnp.bfloat16)

            @pl.when(part == 0)
            def _():
                fetch(layer, 2).wait()

            @pl.loop(0, hidden_width, step=1024)
            def _(start):
                span = pl.ds(pl.multiple_of(start, 1024), 1024)
                upward = jnp.dot(normed[...], w_up[:, span], preferred_element_type=jnp.float32)
                upward = upward + inner_all[layer, :, pl.ds(pl.multiple_of(2 * head_width + start, 1024), 1024)]
                phi = 0.5 + 0.5 * lax.erf(upward * math.sqrt(0.5))
                density = jnp.exp(-0.5 * upward * upward) * (1.0 / math.sqrt(2.0 * math.pi))
                act[layer, part, :, span] = (upward * phi).astype(jnp.bfloat16)
                slope[layer, part, :, span] = (phi + upward * density).astype(jnp.bfloat16)

            @pl.when((section == 0) | (layer < last))
            def _():
                @pl.when(part == 0)
                def _():
                    fetch(layer, 3).wait()

                pl.when(layer > 0)(exchange(1, part).wait_send)

                @pl.loop(0, width, step=1024)
                def _(start):
                    span = pl.ds(pl.multiple_of(start, 1024), 1024)
                    value = contract_last(act[layer, part], w_down[span])
                    send[1, part, :, span] = value.astype(jnp.bfloat16)

                exchange(1, part).start()


        @pl.loop(0, layers)
        def _(layer):
            @pl.when(layer == last)
            def _():
                await_guest(0)
                fetch(last, 0).start()
                fetch(last, 1).start()

            @pl.loop(0, micro)
            def _(part):
                attention_stage(layer, part)

            @pl.when(layer == last)
            def _():
                await_guest(1)
                fetch(last, 2).start()

            @pl.when((section == 0) & (layer == last))
            def _():
                await_guest(2)
                fetch(last, 3).start()

            @pl.loop(0, micro)
            def _(part):
                mlp_stage(layer, part)

        @pl.when(section == 0)
        def _():
            @pl.loop(0, micro)
            def _(part):
                exchange(1, part).wait_recv()

                @pl.loop(0, tokens, step=112)
                def _(start):
                    span = pl.ds(pl.multiple_of(start, 112), 112)
                    value = mid[last, part, span] + (joined(1, part, span) + rows_ref[last, 5:6])
                    final_low[pl.ds(pl.multiple_of(part * tokens + start, 112), 112)] = value.astype(jnp.bfloat16)

        @pl.when(section == 0)
        def _():
            hand_over.start()
            for copy in guest_copies:
                copy.wait_recv()
            pl.semaphore_wait(go_sem, 1)
            close(gather(thirds, lambda: None))
            hand_over.wait_send()

        for copy in guest_copies:
            copy.wait_send()
        for stage in range(2):
            for part in range(micro):
                exchange(stage, part).wait_send()

    return await_guest


def saved_shapes(layers, micro, tokens, width, head_width, hidden_width):
    low, full = jnp.bfloat16, jnp.float32
    heads = head_width // HEAD_DIM
    return (
        ((layers, micro, tokens, width), full),
        ((layers, micro, tokens, 3 * head_width), low),
        ((layers, micro, tokens, heads), full),
        ((layers, micro, tokens, head_width), low),
        ((layers, micro, tokens, width), full),
        ((layers, micro, tokens, hidden_width), low),
        ((layers, micro, tokens, hidden_width), low),
    )


SLOTS = 4
LENT = (4, 4)
LINE_FIRST_COLS = 256


def backward_part(line, aligned, head_width, hidden_width, g0_ref, rows_ref, full_ref, await_guest, refs):
    (
        out, small_out, inner_out, ends_out, d_out, own_in, x_in, z_in,
        w_qkv, w_out, w_up, w_down, hid, qkv, lse, mixed, mid, act, slope, grad, low, hidden_grad, qkv_grad, normed,
        mixed_grad, mask, send, recv, stage, small, inner_sum, given, run_own, run_x, run_z, run_out, late_in, small_in, inner_in,
        w_sem, g0_sem, send_sem, recv_sem, stage_sem, end_sem, given_sem, own_send, own_recv, x_send, x_recv, z_send, z_recv, run_sem,
        late_send, late_recv, out_sem, small_send, small_recv, inner_send, inner_recv,
    ) = refs
    layers, micro, tokens, width = hid.shape
    section = lax.axis_index("section")
    partner = {"tensor": 1 - lax.axis_index("tensor")}
    other = {"section": 1 - section}
    place = lax.axis_index("fsdp")
    count = 2 * line
    z = place // 2
    x = lax.rem(place, 2)
    to_x = {"fsdp": z * 2 + 1 - x}
    to_up = {"fsdp": jnp.minimum(z + 1, line - 1) * 2 + x}
    to_down = {"fsdp": jnp.maximum(z - 1, 0) * 2 + x}
    tile = 256
    wide_tile = 512
    tiles = width // tile
    shard_rows = width // count
    group_cols = stage.shape[2]
    x_cols = group_cols - LINE_FIRST_COLS
    groups = 3
    scale = 1.0 / math.sqrt(HEAD_DIM)

    if True:
        ends = (0, 3 * head_width, 4 * head_width, 4 * head_width + hidden_width, 4 * head_width + 2 * hidden_width)

        def fetch(layer, index):
            buffer = (w_qkv, w_out, w_up, w_down)[index]
            return pltpu.make_async_copy(
                full_ref.at[layer, :, pl.ds(ends[index], ends[index + 1] - ends[index])], buffer, w_sem.at[layer, index]
            )

        last = layers - 1
        first_copy = pltpu.make_async_copy(g0_ref, given, g0_sem.at[0])
        pl.when(section == 1)(first_copy.start)
        hand_over = pltpu.make_async_remote_copy(
            src_ref=low, dst_ref=given, send_sem=given_sem.at[0], recv_sem=given_sem.at[1],
            device_id=other, device_id_type=MESH,
        )

        small[...] = jnp.zeros_like(small)
        inner_sum[...] = jnp.zeros_like(inner_sum)

        @pl.when(section == 1)
        def _():
            first_copy.wait()
            for part in range(micro):
                grad[part] = given[pl.ds(part * tokens, tokens)].astype(jnp.float32)


        def exchange(step, part):
            return pltpu.make_async_remote_copy(
                src_ref=send.at[1 - step, part],
                dst_ref=recv.at[1 - step, part],
                send_sem=send_sem.at[1 - step, part],
                recv_sem=recv_sem.at[1 - step, part],
                device_id=partner,
                device_id_type=MESH,
            )

        def rows_of(part):
            return pl.ds(pl.multiple_of(part * tokens, tokens), tokens)

        def column_sum(value):
            return jnp.sum(value.astype(jnp.float32), axis=0, keepdims=True)

        def norm_parts(value):
            average = jnp.mean(value, axis=-1, keepdims=True)
            centred = value - average
            spread = jnp.mean(centred * centred, axis=-1, keepdims=True)
            inverse = lax.rsqrt(spread + EPSILON)
            return centred * inverse, inverse

        def norm_back(layer, step, part, source, gain_row, shift_row):
            gain = rows_ref[layer, gain_row : gain_row + 1]

            @pl.loop(0, tokens, step=112)
            def _(start):
                span = pl.ds(pl.multiple_of(start, 112), 112)
                outer = send[1 - step, part, span].astype(jnp.float32) + recv[1 - step, part, span].astype(jnp.float32)
                unit, inverse = norm_parts(source[layer, part, span])
                inner = outer * gain
                first = jnp.mean(inner, axis=-1, keepdims=True)
                second = jnp.mean(inner * unit, axis=-1, keepdims=True)
                small[layer, gain_row : gain_row + 1] += column_sum(outer * unit)
                small[layer, shift_row : shift_row + 1] += column_sum(outer)
                grad[part, span] = grad[part, span] + inverse * (inner - first - unit * second)

        def renorm(layer, part, source, gain_row, shift_row):
            @pl.loop(0, tokens, step=112)
            def _(start):
                span = pl.ds(pl.multiple_of(start, 112), 112)
                unit, _ = norm_parts(source[layer, part, span])
                value = unit * rows_ref[layer, gain_row : gain_row + 1] + rows_ref[layer, shift_row : shift_row + 1]
                normed[pl.ds(pl.multiple_of(part * tokens + start, 112), 112)] = value.astype(jnp.bfloat16)

        def round_grad(layer, part, bias_row):
            @pl.loop(0, tokens, step=112)
            def _(start):
                span = pl.ds(pl.multiple_of(start, 112), 112)
                value = grad[part, span].astype(jnp.bfloat16)
                low[pl.ds(pl.multiple_of(part * tokens + start, 112), 112)] = value
                small[layer, bias_row : bias_row + 1] += column_sum(value)

        def columns(group):
            return pl.ds(pl.multiple_of((2 - group) * group_cols, group_cols), group_cols)

        def x_columns(group):
            return pl.ds(pl.multiple_of((2 - group) * group_cols, LANES), x_cols)

        def line_columns(group):
            return pl.ds(pl.multiple_of((2 - group) * group_cols + x_cols, LANES), LINE_FIRST_COLS)

        def part_rows(row_z, row_x):
            return pl.ds(pl.multiple_of((row_z * 2 + row_x) * shard_rows, shard_rows), shard_rows)

        def put(layer, turn, number, group):
            return pltpu.make_async_copy(
                stage.at[turn],
                d_out.at[layer, pl.ds(pl.multiple_of(number * tile, tile), tile), columns(group)],
                stage_sem.at[turn],
            )

        def route(step):
            below, above = z, line - 1 - z
            gap = jnp.maximum(below, above) - jnp.minimum(below, above)
            rest = jnp.maximum(step - gap, 0)
            far = step < gap
            upward = jnp.where(far, jnp.where(above > below, 1, 0), 1 - lax.rem(rest, 2))
            reach = jnp.where(far, jnp.maximum(below, above) - step, jnp.minimum(below, above) - rest // 2)
            ends_here = step == line - 1
            target = jnp.where(ends_here, z, jnp.where(upward == 1, z + reach, z - reach))
            return target, upward == 1, ends_here

        lent = jnp.where(section == 0, LENT[0], LENT[1])
        borrowed = jnp.where(section == 0, LENT[1], LENT[0])

        def split(number):
            return last - number // groups, lax.rem(number, groups)

        def bay(number, mine):
            return number if mine else 3 * layers + number

        def to_partner(number, row_z):
            layer, group = split(number)
            away = number < lent
            return pltpu.make_async_remote_copy(
                src_ref=d_out.at[layer, part_rows(row_z, 1 - x), x_columns(group)],
                dst_ref=x_in.at[jnp.where(away, 3 * layers + number, number), row_z],
                send_sem=x_send.at[number, row_z],
                recv_sem=x_recv.at[jnp.where(away, 3 * layers + number, number), row_z],
                device_id={"section": jnp.where(away, 1 - section, section), "fsdp": z * 2 + 1 - x},
                device_id_type=MESH,
            )

        def held_rows(number, row_z):
            layer, group = split(number)
            return (
                (d_out.at[layer, part_rows(row_z, x), x_columns(group)], pl.ds(0, x_cols)),
                (d_out.at[layer, part_rows(row_z, 0), line_columns(group)], pl.ds(x_cols, LINE_FIRST_COLS)),
                (d_out.at[layer, part_rows(row_z, 1), line_columns(group)], pl.ds(x_cols + LINE_FIRST_COLS, LINE_FIRST_COLS)),
            )

        def to_other(number, row_z, source, span):
            return pltpu.make_async_remote_copy(
                src_ref=source,
                dst_ref=own_in.at[number, row_z, :, span],
                send_sem=own_send.at[number, row_z],
                recv_sem=own_recv.at[number, row_z],
                device_id=other,
                device_id_type=MESH,
            )

        def to_other_whole(number, row_z):
            return to_other(number, row_z, own_in.at[number, row_z], pl.ds(0, x_cols + 2 * LINE_FIRST_COLS))

        def from_partner(place_in, row_z):
            return pltpu.make_async_remote_copy(
                src_ref=x_in.at[place_in, row_z], dst_ref=x_in.at[place_in, row_z],
                send_sem=x_recv.at[place_in, row_z], recv_sem=x_recv.at[place_in, row_z],
                device_id=to_x, device_id_type=MESH,
            )

        def late(place_in, slot, side):
            return pltpu.make_async_remote_copy(
                src_ref=run_own.at[slot, :, pl.ds(x_cols + side * LINE_FIRST_COLS, LINE_FIRST_COLS)],
                dst_ref=late_in.at[place_in],
                send_sem=late_send.at[0],
                recv_sem=late_recv.at[place_in],
                device_id=to_x,
                device_id_type=MESH,
            )

        def onward(place_in, row_z, slot, side):
            return pltpu.make_async_remote_copy(
                src_ref=run_own.at[slot],
                dst_ref=z_in.at[place_in, side, row_z],
                send_sem=z_send.at[slot],
                recv_sem=z_recv.at[place_in, side, row_z],
                device_id=(to_up, to_down)[side],
                device_id_type=MESH,
            )

        def publish(number):
            layer, group = split(number)
            return pltpu.make_async_copy(run_out, out.at[layer, :, columns(group)], out_sem.at[0])

        def publish_other(number):
            layer, group = split(number)
            return pltpu.make_async_remote_copy(
                src_ref=run_out, dst_ref=out.at[layer, :, columns(group)],
                send_sem=out_sem.at[1], recv_sem=out_sem.at[2 + number],
                device_id=other, device_id_type=MESH,
            )

        def add_rows(slot, source, cols):
            @pl.loop(0, shard_rows, step=16)
            def _(start):
                span = pl.ds(pl.multiple_of(start, 16), 16)
                run_own[slot, span, :cols] = run_own[slot, span, :cols] + source[span]

        def collect(number, mine, target, slot, feeds):
            place_in = bay(number, mine)
            own = pltpu.make_async_copy(own_in.at[0 if mine else number, target], run_own.at[slot], run_sem.at[0])
            if mine:
                for source, span in held_rows(number, target):
                    pltpu.make_async_copy(source, run_own.at[slot, :, span], run_sem.at[0]).start()
            else:
                to_other_whole(number, target).wait_recv()
                own.start()
            from_partner(place_in, target).wait_recv()
            mate = pltpu.make_async_copy(x_in.at[place_in, target], run_x, run_sem.at[1])
            mate.start()
            own.wait()
            mate.wait()
            add_rows(slot, run_x, x_cols)
            moves = []
            for side in range(2):
                move = pltpu.make_async_copy(z_in.at[place_in, side, target], run_z.at[side], run_sem.at[2 + side])
                moves.append(move)

                @pl.when(feeds[side])
                def _(side=side, move=move):
                    onward(place_in, target, 0, side).wait_recv()
                    move.start()

            for side in range(2):

                @pl.when(feeds[side])
                def _(side=side):
                    moves[side].wait()
                    add_rows(slot, run_z.at[side], x_cols + 2 * LINE_FIRST_COLS)

        def pass_on(number, mine, turn, step):
            slot = lax.rem(turn, SLOTS)
            target, upward, _ = route(step)
            place_in = bay(number, mine)

            @pl.when(turn >= SLOTS)
            def _():
                onward(0, 0, slot, 0).wait_send()

            collect(number, mine, target, slot, (upward & (z > 0), jnp.logical_not(upward) & (z < line - 1)))

            @pl.when(upward)
            def _():
                onward(place_in, target, slot, 0).start()

            @pl.when(jnp.logical_not(upward))
            def _():
                onward(place_in, target, slot, 1).start()

        def keep(number, mine, first):
            slot = SLOTS
            place_in = bay(number, mine)
            collect(number, mine, z, slot, (z > 0, z < line - 1))
            for side in range(2):
                pl.when(x == 1 - side)(late(place_in, slot, side).start)

            @pl.when(number > first)
            def _():
                publish(0).wait() if mine else publish_other(0).wait_send()

            @pl.loop(0, shard_rows, step=16)
            def _(start):
                span = pl.ds(pl.multiple_of(start, 16), 16)
                run_out[span, :x_cols] = run_own[slot, span, :x_cols].astype(jnp.float32)

            late(place_in, slot, 0).wait_recv()

            @pl.loop(0, shard_rows, step=16)
            def _(start):
                span = pl.ds(pl.multiple_of(start, 16), 16)
                own_half = jnp.where(
                    x == 0,
                    run_own[slot, span, x_cols : x_cols + LINE_FIRST_COLS].astype(jnp.float32),
                    run_own[slot, span, x_cols + LINE_FIRST_COLS :].astype(jnp.float32),
                )
                run_out[span, x_cols:] = own_half + late_in[place_in, span].astype(jnp.float32)

            late(place_in, slot, 0).wait_send()
            publish(number).start() if mine else publish_other(number).start()

        def run_sums(first, end, mine):
            first, end = jnp.asarray(first, jnp.int32), jnp.asarray(end, jnp.int32)

            @pl.loop(first, end + 1)
            def _(number):
                @pl.when(number < end)
                def _():
                    @pl.loop(0, line - 1)
                    def _(step):
                        pass_on(number, mine, (number - first) * (line - 1) + step, step)

                pl.when(number > first)(lambda: keep(number - 1, mine, first))

            for slot in range(SLOTS):
                pl.when(slot < (end - first) * (line - 1))(onward(0, 0, slot, 0).wait_send)
            pl.when(end > first)(publish(0).wait if mine else publish_other(0).wait_send)

        @pl.when(section == 0)
        def _():
            run_sums(0, LENT[1], False)
            hand_over.wait_recv()
            for part in range(micro):
                grad[part] = given[pl.ds(part * tokens, tokens)].astype(jnp.float32)

        def mlp_stage(layer, part):
            @pl.when((part == 0) & ((layer < last) | (section == 1)))
            def _():
                fetch(layer, 3).wait()

            @pl.loop(0, hidden_width, step=wide_tile)
            def _(start):
                span = pl.ds(pl.multiple_of(start, wide_tile), wide_tile)
                value = jnp.dot(low[rows_of(part)], w_down[:, span], preferred_element_type=jnp.float32)
                value = (value * slope[layer, part, :, span].astype(jnp.float32)).astype(jnp.bfloat16)
                hidden_grad[rows_of(part), span] = value
                place_in = pl.ds(pl.multiple_of(2 * head_width + start, wide_tile), wide_tile)
                inner_sum[layer, :, place_in] += column_sum(value)

            @pl.when((part == 0) & (layer < last))
            def _():
                fetch(layer, 2).wait()

            @pl.when(layer < last)
            def _():
                exchange(0, part).wait_send()

            @pl.loop(0, width, step=wide_tile)
            def _(start):
                span = pl.ds(pl.multiple_of(start, wide_tile), wide_tile)
                value = contract_last(hidden_grad[rows_of(part)], w_up[span])
                send[1, part, :, span] = value.astype(jnp.bfloat16)

            exchange(0, part).start()

        def weight_tiles(layer, turn, group, fill):
            def row_of(number):
                return route(number)[0] if tiles == line else number

            def finish(number):
                row = row_of(number)
                put(layer, number, row, group).wait()
                for extra in range(line // tiles):
                    row_z = row * (line // tiles) + extra
                    made = 3 * turn + group
                    to_partner(made, row_z).start()

                    @pl.when(made < lent)
                    def _(row_z=row_z, made=made):
                        for source, span in held_rows(made, row_z):
                            to_other(made, row_z, source, span).start()

            @pl.loop(0, tiles)
            def _(number):
                row = row_of(number)
                fill(number, pl.ds(pl.multiple_of(row * tile, tile), tile))
                put(layer, number, row, group).start()
                pl.when(number > 0)(lambda: finish(jnp.maximum(number - 1, 0)))

            finish(tiles - 1)

        def attention_stage(layer, part):
            exchange(0, part).wait_recv()
            norm_back(layer, 0, part, mid, 1, 4)
            round_grad(layer, part, 3)

            @pl.when((part == 0) & (layer < last))
            def _():
                fetch(layer, 1).wait()

            @pl.loop(0, head_width, step=wide_tile)
            def _(start):
                span = pl.ds(pl.multiple_of(start, wide_tile), wide_tile)
                value = jnp.dot(low[rows_of(part)], w_out[:, span], preferred_element_type=jnp.float32)
                mixed_grad[:, span] = value.astype(jnp.bfloat16)

            lane = lax.broadcasted_iota(jnp.int32, (tokens, LANES), 1)
            for pair in range(head_width // LANES):
                spans = [pl.ds(piece * head_width + pair * LANES, LANES) for piece in range(3)]
                q2, k2, v2 = (qkv[layer, part, :, span] for span in spans)
                go2 = mixed_grad[:, pair * LANES : (pair + 1) * LANES]
                halves = []
                for side in range(2):
                    live = (lane < HEAD_DIM) if side == 0 else (lane >= HEAD_DIM)
                    head = 2 * pair + side
                    scores = contract_last(jnp.where(live, q2, jnp.zeros_like(q2)), k2) + mask[part]
                    probs = jnp.exp(scores - lse[layer, part, :, head : head + 1])
                    outer = contract_last(jnp.where(live, go2, jnp.zeros_like(go2)), v2)
                    centre = jnp.sum(probs * outer, axis=-1, keepdims=True)
                    inner = (probs * (outer - centre)).astype(jnp.bfloat16)
                    halves.append((
                        jnp.dot(inner, k2, preferred_element_type=jnp.float32) * scale,
                        contract_rows(inner, q2),
                        contract_rows(probs.astype(jnp.bfloat16), go2),
                    ))
                for piece in range(3):
                    value = jnp.where(lane < HEAD_DIM, halves[0][piece], halves[1][piece]).astype(jnp.bfloat16)
                    qkv_grad[rows_of(part), spans[piece]] = value
                    if piece != 1:
                        place_in = pl.ds((piece // 2) * head_width + pair * LANES, LANES)
                        inner_sum[layer, :, place_in] += column_sum(value)

            @pl.when((part == 0) & (layer < last))
            def _():
                fetch(layer, 0).wait()

            @pl.when(layer < last)
            def _():
                exchange(1, part).wait_send()

            @pl.loop(0, width, step=wide_tile)
            def _(start):
                span = pl.ds(pl.multiple_of(start, wide_tile), wide_tile)
                value = contract_last(qkv_grad[rows_of(part)], w_qkv[span])
                send[0, part, :, span] = value.astype(jnp.bfloat16)

            exchange(1, part).start()

        @pl.loop(0, layers)
        def _(turn):
            layer = last - turn

            @pl.loop(0, micro)
            def _(part):
                round_grad(layer, part, 5)


            def fill_down(number, span):
                both = act[layer].reshape(micro * tokens, hidden_width)
                stage[number] = contract_rows(low[:, span], both).astype(jnp.bfloat16)

            weight_tiles(layer, turn, 0, fill_down)

            @pl.when((section == 1) & (layer == last))
            def _():
                await_guest(2)
                fetch(last, 3).start()

            @pl.loop(0, micro)
            def _(part):
                mlp_stage(layer, part)

            @pl.when(layer > 0)
            def _():
                fetch(layer - 1, 3).start()
                fetch(layer - 1, 2).start()


            @pl.loop(0, micro)
            def _(part):
                renorm(layer, part, mid, 1, 4)

            def fill_up(number, span):
                stage[number] = contract_rows(normed[:, span], hidden_grad[...]).astype(jnp.bfloat16)

            weight_tiles(layer, turn, 1, fill_up)

            @pl.loop(0, micro)
            def _(part):
                attention_stage(layer, part)

            @pl.when(layer > 0)
            def _():
                fetch(layer - 1, 1).start()
                fetch(layer - 1, 0).start()


            @pl.loop(0, micro)
            def _(part):
                renorm(layer, part, hid, 0, 2)

            def fill_attention(number, span):
                both = mixed[layer].reshape(micro * tokens, head_width)
                stage[number, :, : 3 * head_width] = contract_rows(normed[:, span], qkv_grad[...]).astype(jnp.bfloat16)
                stage[number, :, 3 * head_width :] = contract_rows(low[:, span], both).astype(jnp.bfloat16)

            weight_tiles(layer, turn, 2, fill_attention)

            @pl.loop(0, micro)
            def _(part):
                exchange(1, part).wait_recv()
                norm_back(layer, 1, part, hid, 0, 2)

        for part in range(micro):
            low[pl.ds(part * tokens, tokens)] = grad[part].astype(jnp.bfloat16)
        pl.when(section == 1)(hand_over.start)
        ending = pltpu.make_async_copy(grad, ends_out, end_sem.at[0])
        pl.when(section == 0)(ending.start)
        pl.when(section == 1)(fetch(last, 3).start)

        def small_copies(peer, turn):
            if aligned:
                cut, inner_cut = pl.ds(pl.multiple_of(peer * shard_rows, shard_rows), shard_rows), pl.ds(
                    pl.multiple_of(peer * 3 * shard_rows, 3 * shard_rows), 3 * shard_rows
                )
            else:
                cut, inner_cut = pl.ds(0, width), pl.ds(0, 3 * width)
            made = []
            for source, target, sends, receives in (
                (small.at[:, :, cut], small_in, small_send, small_recv),
                (inner_sum.at[:, :, inner_cut], inner_in, inner_send, inner_recv),
            ):
                made.append(pltpu.make_async_remote_copy(
                    src_ref=source, dst_ref=target.at[turn], send_sem=sends.at[turn], recv_sem=receives.at[turn],
                    device_id={"fsdp": peer}, device_id_type=MESH,
                ))
            return made

        for turn in range(1, count):
            for copy in small_copies(lax.rem(place + turn, count), turn):
                copy.start()

        run_sums(lent, 3 * layers, True)
        pl.when(section == 1)(lambda: run_sums(0, LENT[0], False))

        @pl.when(section == 1)
        def _():
            fetch(last, 3).wait()
            for part in range(micro):
                exchange(0, part).wait_send()

                @pl.loop(0, width, step=wide_tile)
                def _(start, part=part):
                    span = pl.ds(pl.multiple_of(start, wide_tile), wide_tile)
                    value = contract_last(act[last, part], w_down[span])
                    send[1, part, :, span] = value.astype(jnp.bfloat16)

                exchange(0, part).start()
            for part in range(micro):
                exchange(0, part).wait_recv()

                @pl.loop(0, tokens, step=112)
                def _(start, part=part):
                    span = pl.ds(pl.multiple_of(start, 112), 112)
                    down = send[1, part, span].astype(jnp.float32) + recv[1, part, span].astype(jnp.float32)
                    grad[part, span] = mid[last, part, span] + (down + rows_ref[last, 5:6])

            ending.start()


        if aligned:
            mine = pl.ds(pl.multiple_of(place * shard_rows, shard_rows), shard_rows)
            inner_mine = pl.ds(pl.multiple_of(place * 3 * shard_rows, 3 * shard_rows), 3 * shard_rows)
        else:
            mine, inner_mine = pl.ds(0, width), pl.ds(0, 3 * width)
        small_out[...] = small[:, :, mine]
        inner_out[...] = inner_sum[:, :, inner_mine]
        for turn in range(1, count):
            for copy in small_copies(lax.rem(place + turn, count), turn):
                copy.wait()
            small_out[...] += small_in[turn]
            inner_out[...] += inner_in[turn]

        for step in range(2):
            for part in range(micro):
                exchange(step, part).wait_send()

        @pl.loop(0, 3 * layers)
        def _(number):
            @pl.loop(0, line)
            def _(row_z):
                to_partner(number, row_z).wait_send()
                pl.when(number < lent)(lambda: to_other_whole(number, row_z).wait_send())

            pl.when(number < lent)(lambda: publish_other(number).wait_recv())

        pl.when(section == 1)(hand_over.wait_send)
        ending.wait()


def both_kernel(line, aligned, *refs):
    h0, g0, ids, gains, shifts, inner, qkv_in, out_in, up_in, down_in = refs[:10]
    sums, scratch = refs[10:21], refs[21:]
    results, full_ref, guests = sums[:8], sums[8], sums[9:]
    weights, saves, scratch = scratch[:4], scratch[4:11], scratch[11:]
    small_own, inner_own, own_shard, rows, inner_all, low, given_h, given_g, normed_part, mask, send, recv = scratch[:12]
    scratch = scratch[12:]
    back_buffers, scratch = scratch[:15], scratch[15:]
    w_sem, send_sem, recv_sem = scratch[:3]
    fore_sems, back_sems = scratch[3:24], scratch[24:]
    head_width, hidden_width = out_in.shape[2], up_in.shape[2]
    h0_sem, local_sems = fore_sems[0], fore_sems[1:]
    await_guest = forward_part(
        line, aligned, h0, ids, gains, shifts, inner, qkv_in, out_in, up_in, down_in,
        (
            full_ref, *guests, *weights, *saves, small_own, inner_own, own_shard, rows, inner_all, low, given_h,
            normed_part, mask, send, recv, w_sem, h0_sem, send_sem, recv_sem, *local_sems,
        ),
    )
    grad, hidden_grad, qkv_grad, normed, mixed_grad, stage, small, inner_sum = back_buffers[:8]
    backward_part(
        line, aligned, head_width, hidden_width, g0, rows, full_ref, await_guest,
        (
            *results, *weights, *saves, grad, low, hidden_grad, qkv_grad, normed, mixed_grad, mask, send, recv, stage,
            small, inner_sum, given_g, *back_buffers[8:], w_sem, back_sems[0], send_sem, recv_sem, *back_sems[1:],
        ),
    )


def forward_backward(h0, g0, ids, gains, shifts, inner, qkv_in, out_in, up_in, down_in):
    layers, shard_rows = out_in.shape[:2]
    head_width, hidden_width = out_in.shape[2], up_in.shape[2]
    count = lax.axis_size("fsdp")
    line = count // 2
    width = shard_rows * count
    micro, tokens = ids.shape
    cols = 4 * head_width + 2 * hidden_width
    group_cols = 4 * head_width
    x_cols = group_cols - LINE_FIRST_COLS
    line_cols = x_cols + 2 * LINE_FIRST_COLS
    low, wide = jnp.bfloat16, jnp.float32
    aligned = shard_rows % LANES == 0
    if not aligned:
        gains = lax.all_gather(gains, "fsdp", axis=2, tiled=True)
        shifts = lax.all_gather(shifts, "fsdp", axis=2, tiled=True)
        inner = lax.all_gather(inner, "fsdp", axis=2, tiled=True)
    small_width = shard_rows if aligned else width
    bays = 3 * layers + max(LENT)
    outs = (
        ((layers, shard_rows, cols), wide),
        ((layers, 8, small_width), wide),
        ((layers, 1, 3 * small_width), wide),
        ((micro, tokens, width), wide),
        ((layers, width, cols), low),
        ((max(LENT), line, shard_rows, line_cols), low),
        ((bays, line, shard_rows, x_cols), low),
        ((bays, 2, line, shard_rows, line_cols), low),
        ((layers, width, cols), low),
        ((width, cols), low),
        ((shard_rows, cols), low),
    )
    vmem = pl.BlockSpec(memory_space=pltpu.VMEM)
    hbm = pl.BlockSpec(memory_space=pl.ANY)
    dma = pltpu.SemaphoreType.DMA
    sets = layers + 3
    buffers = (
        ((width, 3 * head_width), low),
        ((width, head_width), low),
        ((width, hidden_width), low),
        ((width, hidden_width), low),
        *saved_shapes(layers, micro, tokens, width, head_width, hidden_width),
        ((layers, 8, gains.shape[2]), wide),
        (inner.shape, wide),
        ((layers, shard_rows, cols), low),
        ((layers, 8, width), wide),
        ((layers, 1, 3 * width), wide),
        ((micro * tokens, width), low),
        ((micro * tokens, width), low),
        ((micro * tokens, width), low),
        ((tokens, width), low),
        ((micro, tokens, tokens), wide),
        ((2, micro, tokens, width), low),
        ((2, micro, tokens, width), low),
        ((micro, tokens, width), wide),
        ((micro * tokens, hidden_width), low),
        ((micro * tokens, 3 * head_width), low),
        ((micro * tokens, width), low),
        ((tokens, head_width), low),
        ((width // 256, 256, group_cols), low),
        ((layers, 8, width), wide),
        ((layers, 1, 3 * width), wide),
        ((SLOTS + 1, shard_rows, line_cols), low),
        ((shard_rows, x_cols), low),
        ((2, shard_rows, line_cols), low),
        ((shard_rows, group_cols), wide),
        ((bays, shard_rows, LINE_FIRST_COLS), low),
        ((count, layers, 8, small_width), wide),
        ((count, layers, 1, 3 * small_width), wide),
    )
    h0 = h0.reshape(micro * tokens, width)
    g0 = g0.reshape(micro * tokens, width)
    return pl.pallas_call(
        functools.partial(both_kernel, line, aligned),
        out_shape=[jax.ShapeDtypeStruct(shape, kind) for shape, kind in outs],
        in_specs=[hbm] * 2 + [vmem] * 4 + [hbm] * 4,
        out_specs=[hbm, vmem, vmem] + [hbm] * 8,
        scratch_shapes=[
            *(pltpu.VMEM(shape, kind) for shape, kind in buffers),
            dma((layers, 4)),
            dma((2, micro)),
            dma((2, micro)),
            dma((1,)),
            dma((layers, 7)),
            pltpu.SemaphoreType.REGULAR,
            dma((2,)),
            dma((3, count, 2)),
            dma((3, count, 2)),
            dma((2,)),
            dma((2, count)),
            dma((2, count)),
            dma((sets, 2 * line - 1)),
            dma((sets, 2 * line - 1)),
            dma((sets, line - 1)),
            dma((sets, line - 1)),
            dma((sets, line - 1)),
            dma((sets, line - 1)),
            dma((sets,)),
            dma((sets,)),
            dma((sets, line - 1, 2)),
            dma((sets, line - 1, 2)),
            dma((sets, line - 1, 2)),
            dma((sets, line - 1, 2)),
            dma((1,)),
            dma((width // 256,)),
            dma((1,)),
            dma((2,)),
            dma((max(LENT), line)),
            dma((max(LENT), line)),
            dma((3 * layers, line)),
            dma((bays, line)),
            dma((SLOTS,)),
            dma((bays, 2, line)),
            dma((4,)),
            dma((1,)),
            dma((bays,)),
            dma((2 + 3 * layers,)),
            dma((count,)),
            dma((count,)),
            dma((count,)),
            dma((count,)),
        ],
        compiler_params=pltpu.CompilerParams(
            collective_id=2, has_side_effects=True, vmem_limit_bytes=63 << 20
        ),
        name="forward_backward",
    )(h0, g0, ids, gains, shifts, inner, qkv_in, out_in, up_in, down_in)


def finish_kernel(
    summed, small_in, inner_in, ends, qkv_out, out_out, up_out, down_out, gains_out, shifts_out, inner_out, ends_out,
    small, inner, parts, halves, sems, out_sems,
):
    layers, _, rows, head_width = qkv_out.shape
    bounds = (0, head_width, 2 * head_width, 3 * head_width, 4 * head_width, 4 * head_width + up_out.shape[2], summed.shape[2])
    loads = [
        pltpu.make_async_copy(small_in, small, sems.at[7, 0]),
        pltpu.make_async_copy(inner_in, inner, sems.at[7, 1]),
    ]
    copies = []
    for layer in range(layers):
        targets = [qkv_out.at[layer, piece] for piece in range(3)] + [out_out.at[layer], up_out.at[layer], down_out.at[layer]]
        for number, target in enumerate(targets):
            source = summed.at[layer, :, pl.ds(bounds[number], bounds[number + 1] - bounds[number])]
            held = parts.at[layer, :, pl.ds(bounds[number], bounds[number + 1] - bounds[number])]
            copies.append((
                pltpu.make_async_copy(source, held, sems.at[number, layer]),
                pltpu.make_async_copy(held, target, out_sems.at[number, layer]),
            ))
    for part in range(ends.shape[0]):
        copies.append((
            pltpu.make_async_copy(ends.at[part], halves.at[part], sems.at[6, part]),
            pltpu.make_async_copy(halves.at[part], ends_out.at[0, part], out_sems.at[6, part]),
        ))
    for copy in loads + [bring for bring, _ in copies]:
        copy.start()
    for bring, store in copies:
        bring.wait()
        store.start()
    for copy in loads:
        copy.wait()
    gains_out[...] = small[:, 0:2]
    shifts_out[...] = small[:, 2:6]
    inner_out[...] = inner[...]
    for _, store in copies:
        store.wait()


def finish(summed, small, inner, ends, head_width, hidden_width):
    layers, rows, cols = summed.shape
    wide = jnp.float32
    shapes = (
        (layers, 3, rows, head_width), (layers, rows, head_width), (layers, rows, hidden_width), (layers, rows, hidden_width),
        (layers, 2, rows), (layers, 4, rows), (layers, 1, 3 * rows), (1, *ends.shape),
    )
    vmem = pl.BlockSpec(memory_space=pltpu.VMEM)
    hbm = pl.BlockSpec(memory_space=pltpu.HBM)
    return pl.pallas_call(
        finish_kernel,
        out_shape=[jax.ShapeDtypeStruct(shape, wide) for shape in shapes],
        in_specs=[hbm] * 4,
        out_specs=[hbm, hbm, hbm, hbm, vmem, vmem, vmem, hbm],
        scratch_shapes=[
            pltpu.VMEM(small.shape, wide),
            pltpu.VMEM(inner.shape, wide),
            pltpu.VMEM(summed.shape, wide),
            pltpu.VMEM(ends.shape, wide),
            pltpu.SemaphoreType.DMA((8, max(layers, ends.shape[0], 2))),
            pltpu.SemaphoreType.DMA((7, max(layers, ends.shape[0]))),
        ],
        compiler_params=pltpu.CompilerParams(vmem_limit_bytes=62 << 20),
        name="finish",
    )(summed, small, inner, ends)


def body(
    block_input,
    image_ids,
    qkv_weight,
    out_weight,
    up_weight,
    down_weight,
    norm_gains,
    biases,
    inner_bias,
    cotangent,
):
    head_width, hidden_width = out_weight.shape[2], up_weight.shape[2]
    layers, rows = qkv_weight.shape[:2]
    summed, small, inner, ends = forward_backward(
        block_input, cotangent, image_ids, norm_gains, biases, inner_bias,
        jnp.swapaxes(qkv_weight, 1, 2), out_weight, up_weight, down_weight,
    )[:4]
    if small.shape[2] != rows:
        place = lax.axis_index("fsdp")
        small = lax.dynamic_slice_in_dim(small, place * rows, rows, 2)
        inner = lax.dynamic_slice_in_dim(inner, place * 3 * rows, 3 * rows, 2)
    qkv_grad, *grads, section_ends = finish(summed, small, inner, ends, head_width, hidden_width)
    return (section_ends, jnp.swapaxes(qkv_grad, 1, 2), *grads)


def solution(mesh):
    placed = (
        P(None, "fsdp", None),
        P(None, "fsdp"),
        P("section", "fsdp", None, "tensor"),
        P("section", "fsdp", "tensor"),
        P("section", "fsdp", "tensor"),
        P("section", "fsdp", "tensor"),
        P("section", None, "fsdp"),
        P("section", None, "fsdp"),
        P("section", "tensor", "fsdp"),
        P(None, "fsdp", None),
    )
    return jax.shard_map(
        body,
        mesh=mesh,
        in_specs=placed,
        out_specs=(
            P("section", None, "fsdp", None),
            P("section", "fsdp", None, "tensor"),
            P("section", "fsdp", "tensor"),
            P("section", "fsdp", "tensor"),
            P("section", "fsdp", "tensor"),
            P("section", None, "fsdp"),
            P("section", None, "fsdp"),
            P("section", "tensor", "fsdp"),
        ),
        check_vma=False,
    )
```

time: 677 us -> 553 us (0.82)
  Pallas kernels: 655 us -> 548 us
  local copies, waits for them, and re-layouts: 16.7 us -> 1.26 us
    pallas_call x2, Pallas kernels: 655 us -> 548 us  [the longest x1 541 us: forward_backward(): pl.pallas_call(functools.partial(both_kernel, line, aligned), out_shape=[...]
    slice x6 -> x0, local copies, waits for them, and re-layouts: 9.87 us -> none  [the longest x1 4.86 us: unpack_grads(): full[:, :, ends[2]:ends[3]]]
where the time goes in v5:
time: 553 us; the launch traced here: 550 us
  Pallas kernels  548 us (99%)
    pallas_call x1, Pallas kernels, forward_backward(): pl.pallas_call(functools.partial(both_kernel, line, aligned), out_shape=[...  541 us

profile of v5, /device:TPU:0, one launch (start us, length us, event | category | flops | bytes accessed | tf_op | source)
XLA Modules:
  0.0 549.9 jit_solution(6797597780805284606)
XLA Ops:
  0.6 1.3 copy.18.refs_5_
  1.9 541.0 %forward_backward.1 = (f32[2,128,6144]{2,1,0:T(8,128)}, f32[2,8,128]{2,1,0:T(8,128)}, f32[2,1,384]{2,1,0:T(1,128)}, f32[2,224,1024]{2,1,0:T(8,128)}, bf16[2,1024...) custom-call(bf16[448,1024]{1,0:T(8,128)(2,1)} %bitcast.4, ...), custom_call_target="tpu_custom_call" | custom-call | tf_op jit(solution)/shard_map/forward_backward/pallas_call | solution.py:1224
  542.9 6.8 %finish.1 = (f32[2,3,128,512]{3,2,1,0:T(8,128)}, f32[2,128,512]{2,1,0:T(8,128)}, f32[2,128,2048]{2,1,0:T(8,128)}, f32[2,128,2048]{2,1,0:T(8,128)}, f32[2,2,128]{...) custom-call(f32[2,128,6144]{2,1,0:T(8,128)} %get-tuple-element.20.summed, ...), custom_call_target="tpu_custom_call" | custom-call | tf_op jit(solution)/shard_map/finish/pallas_call | solution.py:1329
